TPU v7x, 32 devices: a whole 2x2x4 slice. The times are simulated.
32 devices in a mesh: groups: 2 (over y), outer: 4 (over z), inner: 4 (over x, core).
Axes of the slice: x: 2, y: 2, z: 4, core: 2. Of those that a mesh axis runs over, the one named last changes fastest.
Arguments:
- decoder: bfloat16 [4096, 16384], P('inner', ('groups', 'outer')), parts along dimension 1, may hold values from -0.09375 to 0.09375
- stretch_blocks: int32 [64, 2], P('groups'), parts along dimension 0, may hold values from 0 to 63, as said below
- stretch_weight: float32 [64], P('groups'), parts along dimension 0, may hold values from 24 to 192
Outputs:
- tangent_grad: bfloat16 [4096, 16384], P('inner', ('groups', 'outer')), parts along dimension 1
There are 2 independent parts, one for each index of `groups`. A program takes and returns all parts, laid end to end along the dimension named above; each array names one. Nothing has to cross between parts.
Inputs may be any that keep to these rules, and one draw needn't show every extreme that they name: `stretch_blocks`: each block id appears once. Block b is stored at outer index b // 16. Stretches c with equal c // 8 form one group of 16 blocks; at each outer index either exactly 4 or none of a group's blocks are stored. The second block of every stretch is stored 2 outer indices below its first block, counted around the axis, so every outer index stores the first blocks of 8 stretches.
All inputs are finite; a program needn't handle non-finite values.
Results may differ from a plain program's by a relative error of at most 0.0085.
Values may be sent and summed in bfloat16 or wider, within the bound.
No kernel may reach another device: no remote copies, remote signals or barrier semaphores. Data moves between devices by JAX's collectives and lax.ppermute only.
A program may use at most 64 MiB of HBM per device.

v0:
```python
import jax
import jax.numpy as jnp
from jax import lax
from jax.sharding import PartitionSpec as P

BLOCK = 128
STRETCH = 256


def shards(decoder, stretch_blocks, stretch_weight):
    width_dev = decoder.shape[0]
    per_dev = decoder.shape[1] // BLOCK
    stretches_dev = per_dev // 2
    owners = lax.axis_size("outer")
    my_index = lax.axis_index("outer")
    capacity = (per_dev + owners - 1) // owners
    slots = owners * capacity
    blocks = decoder.reshape(width_dev, per_dev, BLOCK)
    flat_ids = stretch_blocks.reshape(-1)
    position = jnp.arange(flat_ids.shape[0], dtype=jnp.int32)
    local_ids = jnp.arange(per_dev, dtype=jnp.int32)
    slot_range = jnp.arange(slots, dtype=jnp.int32)
    own_ids = my_index * per_dev + local_ids
    found = own_ids[:, None] == flat_ids[None, :]
    place_of = jnp.sum(jnp.where(found, position[None, :], 0), axis=1)
    diagonal = jnp.eye(STRETCH, dtype=bool)
    target = place_of // per_dev
    earlier = (target[None, :] == target[:, None]) & (local_ids[None, :] < local_ids[:, None])
    send_slot = target * capacity + jnp.sum(earlier, axis=1)
    send_hit = send_slot[None, :] == slot_range[:, None]
    send_index = jnp.sum(jnp.where(send_hit, local_ids[None, :], 0), axis=1)
    outgoing = jnp.take(blocks, send_index, axis=1)
    incoming = lax.all_to_all(outgoing, "outer", split_axis=1, concat_axis=1, tiled=True)
    my_group = lax.dynamic_slice_in_dim(flat_ids, my_index * per_dev, per_dev)
    source = my_group // per_dev
    before = (source[None, :] == source[:, None]) & (my_group[None, :] < my_group[:, None])
    recv_slot = source * capacity + jnp.sum(before, axis=1)
    columns = jnp.take(incoming, recv_slot, axis=1).reshape(width_dev, stretches_dev, STRETCH)
    my_weights = lax.dynamic_slice_in_dim(stretch_weight, my_index * stretches_dev, stretches_dev)
    widened = lax.all_to_all(columns, "inner", split_axis=1, concat_axis=0, tiled=True)
    share_count = widened.shape[1]
    weight = lax.dynamic_slice_in_dim(
        my_weights, lax.axis_index("inner") * share_count, share_count
    )
    gram_part = jnp.einsum("dck,dcl->ckl", widened, widened, preferred_element_type=jnp.float32)
    scaled = jnp.where(diagonal[None], 0.0, gram_part) * (4.0 * weight)[:, None, None]
    local_grad = jnp.einsum(
        "dck,ckl->dcl", widened, scaled.astype(jnp.bfloat16), preferred_element_type=jnp.float32
    ).astype(jnp.bfloat16)
    grad_cols = lax.all_to_all(local_grad, "inner", split_axis=0, concat_axis=1, tiled=True)
    back_hit = recv_slot[None, :] == slot_range[:, None]
    back_index = jnp.sum(jnp.where(back_hit, local_ids[None, :], 0), axis=1)
    returning = jnp.take(grad_cols.reshape(width_dev, per_dev, BLOCK), back_index, axis=1)
    returned = lax.all_to_all(returning, "outer", split_axis=1, concat_axis=1, tiled=True)
    grads = jnp.take(returned, send_slot, axis=1).reshape(width_dev, per_dev * BLOCK)
    grads_wide = grads.astype(jnp.float32)
    decoder_wide = decoder.astype(jnp.float32)
    along_dir = lax.psum(jnp.sum(decoder_wide * grads_wide, axis=0), "inner")
    return (grads_wide - along_dir[None, :] * decoder_wide).astype(jnp.bfloat16)


def solution(mesh):
    placed = (P("inner", ("groups", "outer")), P("groups", None), P("groups"))
    return jax.shard_map(
        shards,
        mesh=mesh,
        in_specs=placed,
        out_specs=P("inner", ("groups", "outer")),
        check_vma=False,
    )
```

profile of v0, /device:TPU:0, one launch (start us, length us, event | category | flops | bytes accessed | tf_op | source)
XLA Modules:
  0.0 444.4 jit_solution(9055524706503776655)
XLA Ops:
  0.0 0.8 copy.50
  1.4 6.4 %copy.51 = bf16[1024,2048]{0,1:T(8,128)(2,1)} copy(bf16[1024,2048]{1,0:T(8,128)(2,1)} %param.5) | data formatting | bytes 8388608 | tf_op args[0]
  7.8 6.4 %copy.52 = bf16[1024,16,128]{2,0,1:T(8,128)(2,1)} copy(bf16[1024,16,128]{0,2,1:T(8,128)(2,1)} %bitcast.27) | data formatting | bytes 8388608 | tf_op jit(solution)/shard_map/reshape | solution.py:18
  14.2 5.2 %gather_fusion = bf16[16,1024,128]{2,1,0:T(8,128)(2,1)} fusion(bf16[1024,16,128]{2,0,1:T(8,128)(2,1)} %copy.52, s32[1024]{0:T(1024)S(1)} %pad_clamp_fusion.3), kind=kCustom, calls=%fused_computation.clone | custom fusion | bytes 8388672 | tf_op jit(solution)/shard_map/jit(_take)/gather | solution.py:32
  19.5 4.6 %select_bitcast_fusion.2 = bf16[1024,16,128]{2,0,1:T(8,128)(2,1)} fusion(bf16[16,1024,128]{2,1,0:T(8,128)(2,1)} %gather_fusion, pred[16]{0:T(512)(128)(4,1)S(1)} %compare_and_fusion.3), kind=kLoop, calls=%fused_computation.14 | loop fusion | flops 2097152 | bytes 8388624 | tf_op jit(solution)/shard_map/jit(_take)/select_n | solution.py:32
  24.1 6.3 %all-to-all-start = ((bf16[1024,16,128]{2,0,1:T(8,128)(2,1)}), bf16[1024,16,128]{2,0,1:T(8,128)(2,1)}, u32[]{:S(2)}, u32[]{:S(2)}) async-start(bf16[1024,16,128]{2,0,1:T(8,128)(2,1)} %select_bitcast_fusion.2), calls=%async_computation | async-start | bytes 8388608 | tf_op jit(solution)/shard_map/all_to_all | solution.py:33
  30.5 0.2 convert_reduce_fusion
  30.7 93.1 %all-to-all-done = bf16[1024,16,128]{2,0,1:T(8,128)(2,1)} async-done(((bf16[1024,16,128]{2,0,1:T(8,128)(2,1)}), bf16[1024,16,128]{2,0,1:T(8,128)(2,1)}, u32[]{:S(2)}, u32[]{:S(2)}) %all-to-all-start) | async-done | bytes 4194336 | tf_op jit(solution)/shard_map/all_to_all | solution.py:33
  123.8 5.2 %gather_fusion.1 = bf16[16,1024,128]{2,1,0:T(8,128)(2,1)} fusion(bf16[1024,16,128]{2,0,1:T(8,128)(2,1)} %all-to-all-done, s32[1024]{0:T(1024)S(1)} %pad_clamp_fusion.2), kind=kCustom, calls=%fused_computation.1.clone | custom fusion | bytes 8388672 | tf_op jit(solution)/shard_map/jit(_take)/gather | solution.py:38
  129.1 4.6 %select_bitcast_fusion.1 = bf16[1024,16,128]{2,0,1:T(8,128)(2,1)} fusion(bf16[16,1024,128]{2,1,0:T(8,128)(2,1)} %gather_fusion.1, pred[16]{0:T(512)(128)(4,1)S(1)} %get-tuple-element.8), kind=kLoop, calls=%fused_computation.13 | loop fusion | flops 2097152 | bytes 8388624 | tf_op jit(solution)/shard_map/jit(_take)/select_n | solution.py:38
  133.7 6.4 %copy.53 = bf16[1024,16,128]{0,2,1:T(8,128)(2,1)} copy(bf16[1024,16,128]{2,0,1:T(8,128)(2,1)} %select_bitcast_fusion.1) | data formatting | bytes 8388608 | tf_op jit(solution)/shard_map/jit(_take)/select_n | solution.py:38
  140.1 5.0 %all-to-all-start.1 = ((bf16[1024,8,256]{0,2,1:T(8,128)(2,1)}), bf16[1024,8,256]{0,2,1:T(8,128)(2,1)}, u32[]{:S(2)}, u32[]{:S(2)}) async-start(bf16[1024,8,256]{0,2,1:T(8,128)(2,1)} %bitcast.28), calls=%async_computation.1 | async-start | bytes 8388608 | tf_op jit(solution)/shard_map/all_to_all | solution.py:40
  145.2 48.1 %all-to-all-done.1 = bf16[1024,8,256]{0,2,1:T(8,128)(2,1)} async-done(((bf16[1024,8,256]{0,2,1:T(8,128)(2,1)}), bf16[1024,8,256]{0,2,1:T(8,128)(2,1)}, u32[]{:S(2)}, u32[]{:S(2)}) %all-to-all-start.1) | async-done | bytes 4194336 | tf_op jit(solution)/shard_map/all_to_all | solution.py:40
  193.3 6.3 %copy.55 = bf16[4,1024,2,256]{3,1,0,2:T(8,128)(2,1)} copy(bf16[4,1024,2,256]{1,3,2,0:T(8,128)(2,1)} %bitcast.6) | data formatting | bytes 8388608 | tf_op jit(solution)/shard_map/all_to_all | solution.py:40
  199.6 9.5 %fusion.3 = bf16[4096,2,256]{0,2,1:T(8,128)(2,1)} fusion(bf16[4096,2,256]{2,0,1:T(8,128)(2,1)} %bitcast.26, f32[2]{0:T(128)S(1)} %dynamic-slice_multiply_fusion, pred[256,256]{1,0:T(8,128)(4,1)S(1)} %iota_compare_fusion), kind=kOutput, calls=%fused_computation.10 | convolution fusion | flops 2149974016 | bytes 8454152 | tf_op jit(solution)/shard_map/dck,ckl->dcl/dot_general | solution.py:47
  209.1 11.1 %copy.58 = bf16[4096,2,256]{2,1,0:T(2,128)(2,1)} copy(bf16[4096,2,256]{0,2,1:T(8,128)(2,1)} %fusion.3) | data formatting | bytes 8388608 | tf_op jit(solution)/shard_map/convert_element_type | solution.py:49
  220.2 4.9 %all-to-all-start.2 = ((bf16[4096,2,256]{2,1,0:T(2,128)(2,1)}), bf16[4096,2,256]{2,1,0:T(2,128)(2,1)}, u32[]{:S(2)}, u32[]{:S(2)}) async-start(bf16[4096,2,256]{2,1,0:T(2,128)(2,1)} %copy.58), calls=%async_computation.2 | async-start | bytes 8388608 | tf_op jit(solution)/shard_map/all_to_all | solution.py:50
  225.2 48.1 %all-to-all-done.2 = bf16[4096,2,256]{2,1,0:T(2,128)(2,1)} async-done(((bf16[4096,2,256]{2,1,0:T(2,128)(2,1)}), bf16[4096,2,256]{2,1,0:T(2,128)(2,1)}, u32[]{:S(2)}, u32[]{:S(2)}) %all-to-all-start.2) | async-done | bytes 4194336 | tf_op jit(solution)/shard_map/all_to_all | solution.py:50
  273.3 4.7 %copy.59 = bf16[4096,2,256]{2,0,1:T(8,128)(2,1)} copy(bf16[4096,2,256]{2,1,0:T(2,128)(2,1)} %all-to-all-done.2) | data formatting | bytes 8388608 | tf_op jit(solution)/shard_map/all_to_all | solution.py:50
  278.0 6.3 %copy.60 = bf16[1024,4,2,256]{0,3,2,1:T(8,128)(2,1)} copy(bf16[1024,4,2,256]{3,0,1,2:T(8,128)(2,1)} %bitcast.29) | data formatting | bytes 8388608 | tf_op jit(solution)/shard_map/all_to_all | solution.py:50
  284.3 6.4 %copy.61 = bf16[1024,16,128]{2,0,1:T(8,128)(2,1)} copy(bf16[1024,16,128]{0,2,1:T(8,128)(2,1)} %bitcast.30) | data formatting | bytes 8388608 | tf_op jit(solution)/shard_map/reshape | solution.py:53
  290.7 5.2 %gather_fusion.2 = bf16[16,1024,128]{2,1,0:T(8,128)(2,1)} fusion(bf16[1024,16,128]{2,0,1:T(8,128)(2,1)} %copy.61, s32[1024]{0:T(1024)S(1)} %pad_clamp_fusion.1), kind=kCustom, calls=%fused_computation.2.clone | custom fusion | bytes 8388672 | tf_op jit(solution)/shard_map/jit(_take)/gather | solution.py:53
  295.9 4.6 %select_bitcast_fusion = bf16[1024,16,128]{2,0,1:T(8,128)(2,1)} fusion(bf16[16,1024,128]{2,1,0:T(8,128)(2,1)} %gather_fusion.2, pred[16]{0:T(512)(128)(4,1)S(1)} %compare_and_fusion.1), kind=kLoop, calls=%fused_computation.12 | loop fusion | flops 2097152 | bytes 8388624 | tf_op jit(solution)/shard_map/jit(_take)/select_n | solution.py:53
  300.6 5.0 %all-to-all-start.3 = ((bf16[1024,16,128]{2,0,1:T(8,128)(2,1)}), bf16[1024,16,128]{2,0,1:T(8,128)(2,1)}, u32[]{:S(2)}, u32[]{:S(2)}) async-start(bf16[1024,16,128]{2,0,1:T(8,128)(2,1)} %select_bitcast_fusion), calls=%async_computation.3 | async-start | bytes 8388608 | tf_op jit(solution)/shard_map/all_to_all | solution.py:54
  305.6 93.1 %all-to-all-done.3 = bf16[1024,16,128]{2,0,1:T(8,128)(2,1)} async-done(((bf16[1024,16,128]{2,0,1:T(8,128)(2,1)}), bf16[1024,16,128]{2,0,1:T(8,128)(2,1)}, u32[]{:S(2)}, u32[]{:S(2)}) %all-to-all-start.3) | async-done | bytes 4194336 | tf_op jit(solution)/shard_map/all_to_all | solution.py:54
  398.7 5.2 %gather_fusion.3 = bf16[16,1024,128]{2,1,0:T(8,128)(2,1)} fusion(bf16[1024,16,128]{2,0,1:T(8,128)(2,1)} %all-to-all-done.3, s32[1024]{0:T(1024)S(1)} %pad_clamp_fusion), kind=kCustom, calls=%fused_computation.3.clone | custom fusion | bytes 8388672 | tf_op jit(solution)/shard_map/jit(_take)/gather | solution.py:55
  403.9 6.0 %bitcast_convert_fusion = f32[1024,16,128]{2,0,1:T(8,128)} fusion(bf16[16,1024,128]{2,1,0:T(8,128)(2,1)} %gather_fusion.3, pred[16]{0:T(512)(128)(4,1)S(1)} %get-tuple-element.6), kind=kLoop, calls=%fused_computation.11 | loop fusion | flops 4194304 | bytes 12582928 | tf_op jit(solution)/shard_map/convert_element_type | solution.py:56
  410.0 9.3 %copy.62 = f32[1024,16,128]{0,2,1:T(8,128)} copy(f32[1024,16,128]{2,0,1:T(8,128)} %bitcast_convert_fusion) | data formatting | bytes 16777216 | tf_op jit(solution)/shard_map/convert_element_type | solution.py:56
  419.2 5.5 %fusion = f32[2048]{0:T(1024)S(1)} fusion(bf16[1024,2048]{0,1:T(8,128)(2,1)} %copy.51, f32[1024,16,128]{0,2,1:T(8,128)} %copy.62), kind=kLoop, calls=%fused_computation.6 | loop fusion | flops 6289408 | bytes 12591104 | tf_op jit(solution)/shard_map/reduce_sum | solution.py:58
  424.8 6.1 %psum.7 = f32[2048]{0:T(1024)S(1)} all-reduce(f32[2048]{0:T(1024)S(1)} %fusion), channel_id=1, replica_groups=mesh['groups'=2,'outer'=4,'inner'=4] {'inner'}, use_global_device_ids=true, to_apply=%region_6.8 | all-reduce | flops 2048 | bytes 16384 | tf_op jit(solution)/shard_map/psum | solution.py:58
  430.9 7.1 %fusion.2 = bf16[1024,2048]{0,1:T(8,128)(2,1)} fusion(bf16[1024,2048]{0,1:T(8,128)(2,1)} %copy.51, f32[1024,16,128]{0,2,1:T(8,128)} %copy.62, f32[2048]{0:T(1024)S(1)} %psum.7), kind=kLoop, calls=%fused_computation.8 | loop fusion | flops 8388608 | bytes 16785408 | tf_op jit(solution)/shard_map/convert_element_type | solution.py:59
  438.0 6.4 %copy.64 = bf16[1024,2048]{1,0:T(8,128)(2,1)} copy(bf16[1024,2048]{0,1:T(8,128)(2,1)} %fusion.2) | data formatting | bytes 8388608 | tf_op jit(solution)/shard_map/convert_element_type | solution.py:59
  (24 shorter events, 1.0 us)
Async XLA Ops:
  24.1 99.7 %all-to-all-start = ((bf16[1024,16,128]{2,0,1:T(8,128)(2,1)}), bf16[1024,16,128]{2,0,1:T(8,128)(2,1)}, u32[]{:S(2)}, u32[]{:S(2)}) async-start(bf16[1024,16,128]{2,0,1:T(8,128)(2,1)} %select_bitcast_fusion.2), calls=%async_computation | async-start | bytes 8388608 | tf_op jit(solution)/shard_map/all_to_all | solution.py:33
  140.1 5.0 %copy-start = (f32[32]{0:T(128)S(1)}, f32[32]{0:T(128)}, u32[]{:S(2)}) copy-start(f32[32]{0:T(128)} %param.7) | copy-start | bytes 388
  140.1 53.2 %all-to-all-start.1 = ((bf16[1024,8,256]{0,2,1:T(8,128)(2,1)}), bf16[1024,8,256]{0,2,1:T(8,128)(2,1)}, u32[]{:S(2)}, u32[]{:S(2)}) async-start(bf16[1024,8,256]{0,2,1:T(8,128)(2,1)} %bitcast.28), calls=%async_computation.1 | async-start | bytes 8388608 | tf_op jit(solution)/shard_map/all_to_all | solution.py:40
  220.2 53.1 %all-to-all-start.2 = ((bf16[4096,2,256]{2,1,0:T(2,128)(2,1)}), bf16[4096,2,256]{2,1,0:T(2,128)(2,1)}, u32[]{:S(2)}, u32[]{:S(2)}) async-start(bf16[4096,2,256]{2,1,0:T(2,128)(2,1)} %copy.58), calls=%async_computation.2 | async-start | bytes 8388608 | tf_op jit(solution)/shard_map/all_to_all | solution.py:50
  300.6 98.1 %all-to-all-start.3 = ((bf16[1024,16,128]{2,0,1:T(8,128)(2,1)}), bf16[1024,16,128]{2,0,1:T(8,128)(2,1)}, u32[]{:S(2)}, u32[]{:S(2)}) async-start(bf16[1024,16,128]{2,0,1:T(8,128)(2,1)} %select_bitcast_fusion), calls=%async_computation.3 | async-start | bytes 8388608 | tf_op jit(solution)/shard_map/all_to_all | solution.py:54
where the time goes:
time: 446 us; the launch traced here: 444 us
  waiting for transfers between devices  282 us (63%)
  local copies, waits for them, and re-layouts  91.5 us (21%)
  other arithmetic  33.6 us (8%)
  starting transfers between devices  21.2 us (5%)
  matrix products  9.5 us (2%)
  blocking collectives  6.11 us (1%)
    all_to_all x1, waiting for transfers between devices, shards(): lax.all_to_all(outgoing, 'outer', split_axis=1, concat_axis=1, tiled=True)  93.1 us
    all_to_all x1, waiting for transfers between devices, shards(): lax.all_to_all(returning, 'outer', split_axis=1, concat_axis=1, tiled=True)  93.1 us
    all_to_all x1, waiting for transfers between devices, shards(): lax.all_to_all(columns, 'inner', split_axis=1, concat_axis=0, tiled=True)  48.1 us
    all_to_all x1, waiting for transfers between devices, shards(): lax.all_to_all(local_grad, 'inner', split_axis=0, concat_axis=1, tiled=True)  48.1 us
    convert_element_type x1, local copies, waits for them, and re-layouts, shards(): local_grad = jnp.einsum('dck,ckl->dcl', widened, scaled.astype(jnp.bfloat...  11.1 us
    all_to_all x2, local copies, waits for them, and re-layouts, shards(): lax.all_to_all(local_grad, 'inner', split_axis=0, concat_axis=1, tiled=True)  11 us
    dot_general x1, matrix products, shards(): jnp.einsum('dck,ckl->dcl', widened, scaled.astype(jnp.bfloat16), preferre...  9.5 us
    convert_element_type x1, local copies, waits for them, and re-layouts, shards(): grads_wide = grads.astype(jnp.float32)  9.26 us
  transfers between devices with their start and end apart: 4, of which 4 were waited for; matrix products, arithmetic and copies ran while one was open for 0% of the time, Pallas kernels for 0%

commit v1 on v0

v1 whole, which is shorter than its diff:
```python
import functools

import jax
import jax.numpy as jnp
from jax import lax
from jax.experimental import pallas as pl
from jax.experimental.pallas import tpu as pltpu
from jax.sharding import PartitionSpec as P

BLOCK = 128
STRETCH = 256
CHUNKS = (2, 2, 2, 1, 1)
LAG = 2

ANY = pl.BlockSpec(memory_space=pl.ANY)
VMEM = pl.BlockSpec(memory_space=pltpu.VMEM)
SMEM = pl.BlockSpec(memory_space=pltpu.SMEM)


def column(ref, block):
    start = block * BLOCK
    if not isinstance(block, int):
        start = pl.multiple_of(start, BLOCK)
    return ref.at[:, pl.ds(start, BLOCK)]


def plan(per_dev, blocks_ref, weight_ref, place_ref, scale_ref):
    me = lax.axis_index("outer")

    def one(c, counts):
        first, second = blocks_ref[c, 0], blocks_ref[c, 1]
        firsts, seconds = counts
        place_ref[0, firsts] = lax.rem(first, per_dev)
        scale_ref[0, firsts] = 4.0 * weight_ref[c]
        place_ref[1, seconds] = lax.rem(second, per_dev)
        firsts += (lax.div(first, per_dev) == me).astype(jnp.int32)
        seconds += (lax.div(second, per_dev) == me).astype(jnp.int32)
        return firsts, seconds

    lax.fori_loop(0, blocks_ref.shape[0], one, (jnp.int32(0), jnp.int32(0)))


def opening_kernel(per_dev, starts, sizes, blocks_ref, weight_ref, decoder_ref, place_ref, scale_ref, *rest):
    outs, sem = rest[:-1], rest[-1]
    plan(per_dev, blocks_ref, weight_ref, place_ref, scale_ref)
    copies = []
    for start, size, out in zip(starts, sizes, outs):
        for j in range(size):
            copies.append(
                pltpu.make_async_copy(
                    column(decoder_ref, place_ref[1, start + j]), column(out, j), sem.at[len(copies)]
                )
            )
            copies[-1].start()
    for copy in copies:
        copy.wait()


def gram_parts(x):
    gram = lax.dot_general(x, x, (((0,), (0,)), ((), ())), preferred_element_type=jnp.float32)
    row = lax.broadcasted_iota(jnp.int32, (BLOCK, BLOCK), 0)
    col = lax.broadcasted_iota(jnp.int32, (BLOCK, BLOCK), 1)
    own = jnp.where(row < col, gram[:BLOCK, :BLOCK], gram[BLOCK:, BLOCK:])
    return own, gram[:BLOCK, BLOCK:]


def tangents(x, own, cross, scale):
    row = lax.broadcasted_iota(jnp.int32, (BLOCK, BLOCK), 0)
    col = lax.broadcasted_iota(jnp.int32, (BLOCK, BLOCK), 1)
    upper = jnp.where(row < col, own, 0.0)
    lower = jnp.where(row > col, own, 0.0)
    gram = jnp.concatenate(
        [
            jnp.concatenate([upper + upper.T, cross], axis=1),
            jnp.concatenate([cross.T, lower + lower.T], axis=1),
        ],
        axis=0,
    )
    coef = (gram * scale).astype(jnp.bfloat16)
    along = jnp.sum(gram * coef.astype(jnp.float32), axis=0, keepdims=True)
    grad = jnp.dot(x, coef, preferred_element_type=jnp.float32).astype(jnp.bfloat16)
    return (grad.astype(jnp.float32) - along * x.astype(jnp.float32)).astype(jnp.bfloat16)


def step_kernel(spec, *refs):
    refs = list(refs)
    take = lambda: refs.pop(0)
    place_ref, scale_ref, decoder_ref = take(), take(), take()
    gram_in = take() if spec["gram"] else None
    final_in = take() if spec["final"] else None
    parts = [take() for _ in range(spec["ranks"])] if spec["final"] else None
    back_in = take() if spec["back"] else None
    if spec["aliased"]:
        take()
    gram_out = take() if spec["gram"] else None
    send_out = take() if spec["final"] or spec["pack"] else None
    out_ref = take() if spec["final"] or spec["back"] else None
    gram_x, final_x, final_t, load_sem, move_sem, store_sem = refs

    loads = {}

    def load(kind, scratch, source, start, size):
        for j in range(size):
            pair = (
                pltpu.make_async_copy(
                    column(decoder_ref, place_ref[0, start + j]),
                    scratch.at[j, :, pl.ds(0, BLOCK)],
                    load_sem.at[len(loads), 0],
                ),
                pltpu.make_async_copy(
                    column(source, j), scratch.at[j, :, pl.ds(BLOCK, BLOCK)], load_sem.at[len(loads), 1]
                ),
            )
            for copy in pair:
                copy.start()
            loads[kind, j] = pair

    moves = []

    def move(source, target):
        moves.append(pltpu.make_async_copy(source, target, move_sem.at[len(moves)]))
        moves[-1].start()

    if spec["pack"]:
        start, size = spec["pack"]
        for j in range(size):
            move(column(decoder_ref, place_ref[1, start + j]), column(send_out, j))
    if spec["gram"]:
        load("gram", gram_x, gram_in, *spec["gram"])
    if spec["final"]:
        load("final", final_x, final_in, *spec["final"])
    if spec["back"]:
        start, size = spec["back"]
        for j in range(size):
            move(column(back_in, j), column(out_ref, place_ref[1, start + j]))

    if spec["gram"]:
        for j in range(spec["gram"][1]):
            for copy in loads["gram", j]:
                copy.wait()
            gram_out[j, 0], gram_out[j, 1] = gram_parts(gram_x[j])

    stores = []
    if spec["final"]:
        start, size = spec["final"]
        for j in range(size):
            for copy in loads["final", j]:
                copy.wait()
            a, b, c, d = (part[j] for part in parts)
            total = (a + b) + (c + d)
            final_t[j] = tangents(final_x[j], total[0], total[1], scale_ref[0, start + j])
            for target, half in ((column(out_ref, place_ref[0, start + j]), 0), (column(send_out, j), 1)):
                stores.append(
                    pltpu.make_async_copy(
                        final_t.at[j, :, pl.ds(half * BLOCK, BLOCK)], target, store_sem.at[len(stores)]
                    )
                )
                stores[-1].start()
    for copy in moves + stores:
        copy.wait()


def shards(decoder, stretch_blocks, stretch_weight):
    width, columns = decoder.shape
    per_dev = columns // BLOCK
    half = per_dev // 2
    owners, ranks = lax.axis_size("outer"), lax.axis_size("inner")
    stride = min(owners, per_dev) // 2
    sizes = CHUNKS
    count = len(sizes)
    starts = [sum(sizes[:k]) for k in range(count)]
    chunk = lambda k: (starts[k], sizes[k])
    array = lambda k: jax.ShapeDtypeStruct((width, sizes[k] * BLOCK), decoder.dtype)
    out_shape = jax.ShapeDtypeStruct(decoder.shape, decoder.dtype)
    to_first = [(o, (o + stride) % owners) for o in range(owners)]
    to_second = [(o, (o - stride) % owners) for o in range(owners)]

    place, scale, *raw = pl.pallas_call(
        functools.partial(opening_kernel, per_dev, starts[:LAG], sizes[:LAG]),
        out_shape=[
            jax.ShapeDtypeStruct((2, half + 1), jnp.int32),
            jax.ShapeDtypeStruct((1, half + 1), jnp.float32),
        ]
        + [array(k) for k in range(LAG)],
        in_specs=[SMEM, SMEM, ANY],
        out_specs=[SMEM, SMEM] + [ANY] * LAG,
        scratch_shapes=[pltpu.SemaphoreType.DMA((per_dev,))],
        name="opening",
    )(stretch_blocks, stretch_weight, decoder)

    sends = [lax.ppermute(part, "outer", to_first) for part in raw]
    parts = {}
    out = None
    for step in range(2 * count):
        arrived = sends[step]
        gram = chunk(step) if step < count else None
        pack = chunk(step + LAG) if step + LAG < count else None
        turn = step + LAG - count
        final = chunk(turn) if 0 <= turn < count else None
        back = chunk(step - count) if step >= count else None
        spec = {"gram": gram, "pack": pack, "final": final, "back": back, "ranks": ranks, "aliased": out is not None}
        args, specs = [place, scale, decoder], [SMEM, SMEM, ANY]
        shapes, out_specs, aliases = [], [], {}
        if gram:
            args, specs = args + [arrived], specs + [ANY]
            shapes.append(jax.ShapeDtypeStruct((gram[1], 2, BLOCK, BLOCK), jnp.float32))
            out_specs.append(VMEM)
        if final:
            args, specs = args + [sends[turn]] + parts.pop(turn), specs + [ANY] + [VMEM] * ranks
        if back:
            args, specs = args + [arrived], specs + [ANY]
        if final or pack:
            shapes.append(array(turn if final else step + LAG))
            out_specs.append(ANY)
        if final or back:
            if out is not None:
                aliases = {len(args): len(shapes)}
                args, specs = args + [out], specs + [ANY]
            shapes.append(out_shape)
            out_specs.append(ANY)
        slot = max(sizes)
        results = list(
            pl.pallas_call(
                functools.partial(step_kernel, spec),
                out_shape=shapes,
                in_specs=specs,
                out_specs=out_specs,
                input_output_aliases=aliases,
                scratch_shapes=[
                    pltpu.VMEM((slot, width, STRETCH), decoder.dtype),
                    pltpu.VMEM((slot, width, STRETCH), decoder.dtype),
                    pltpu.VMEM((slot, width, STRETCH), decoder.dtype),
                    pltpu.SemaphoreType.DMA((2 * slot, 2)),
                    pltpu.SemaphoreType.DMA((2 * slot,)),
                    pltpu.SemaphoreType.DMA((2 * slot,)),
                ],
                compiler_params=pltpu.CompilerParams(vmem_limit_bytes=32 * 2**20),
                name="step",
            )(*args)
        )
        if gram:
            mine = results.pop(0)
            parts[step] = [mine] + [
                lax.ppermute(mine, "inner", [(i, i ^ hop) for i in range(ranks)]) for hop in range(1, ranks)
            ]
        if final or pack:
            sends.append(lax.ppermute(results.pop(0), "outer", to_second if final else to_first))
        if final or back:
            out = results.pop(0)
    return out


def solution(mesh):
    placed = (P("inner", ("groups", "outer")), P("groups", None), P("groups"))
    return jax.shard_map(
        shards,
        mesh=mesh,
        in_specs=placed,
        out_specs=P("inner", ("groups", "outer")),
        check_vma=False,
    )
```

time: 446 us -> 236 us (0.53)
  waiting for transfers between devices: 282 us -> 142 us
  local copies, waits for them, and re-layouts: 91.5 us -> 4.82 us
  Pallas kernels: 0 us -> 57.2 us
  other arithmetic: 33.6 us -> 0 us
  starting transfers between devices: 21.2 us -> 31.3 us
  matrix products: 9.5 us -> 0 us
  blocking collectives: 6.11 us -> 0 us
    all_to_all x4 -> x0, waiting for transfers between devices: 282 us -> none  [the longest x1 93.1 us: shards(): lax.all_to_all(outgoing, 'outer', split_axis=1, concat_axis=1, tiled=True)]
    ppermute x0 -> x25, waiting for transfers between devices: none -> 142 us  [the longest x8 95.3 us: shards(): lax.ppermute(results.pop(0), 'outer', to_second if final else to_first)]
    pallas_call x0 -> x11, Pallas kernels: none -> 57.2 us  [the longest x1 35 us: shards(): pl.pallas_call(functools.partial(opening_kernel, per_dev, starts[:LAG], s...]
    ppermute x0 -> x25, starting transfers between devices: none -> 31.3 us  [the longest x15 21 us: shards(): lax.ppermute(mine, 'inner', [(i, i ^ hop) for i in range(ranks)])]
    convert_element_type x3 -> x0, local copies, waits for them, and re-layouts: 26.8 us -> none  [the longest x1 11.1 us: shards(): local_grad = jnp.einsum('dck,ckl->dcl', widened, scaled.astype(jnp.bfloat...]
    all_to_all x4 -> x0, starting transfers between devices: 21.2 us -> none  [the longest x1 6.32 us: shards(): lax.all_to_all(outgoing, 'outer', split_axis=1, concat_axis=1, tiled=True)]
    gather x4 -> x0, local copies, waits for them, and re-layouts: 21 us -> none  [the longest x1 5.25 us: shards(): jnp.take(incoming, recv_slot, axis=1)]
    all_to_all x3 -> x0, local copies, waits for them, and re-layouts: 17.3 us -> none  [the longest x2 11 us: shards(): lax.all_to_all(local_grad, 'inner', split_axis=0, concat_axis=1, tiled=True)]
  transfers between devices with their start and end apart: 4 -> 25, of which waited for: 4 -> 12; matrix products, arithmetic and copies ran while one was open for 0% -> 0% of each run, Pallas kernels for 0% -> 9%
where the time goes in v1:
time: 236 us; the launch traced here: 235 us
  waiting for transfers between devices  142 us (60%)
  Pallas kernels  57.2 us (24%)
  starting transfers between devices  31.3 us (13%)
  local copies, waits for them, and re-layouts  4.82 us (2%)
    ppermute x8, waiting for transfers between devices, shards(): lax.ppermute(results.pop(0), 'outer', to_second if final else to_first)  95.3 us
    ppermute x2, waiting for transfers between devices, shards(): sends = [lax.ppermute(part, 'outer', to_first) for part in raw]  38.1 us
    pallas_call x1, Pallas kernels, shards(): pl.pallas_call(functools.partial(opening_kernel, per_dev, starts[:LAG], s...  35 us
    pallas_call x10, Pallas kernels, shards(): pl.pallas_call(functools.partial(step_kernel, spec), out_shape=shapes, in...  22.2 us
    ppermute x15, starting transfers between devices, shards(): lax.ppermute(mine, 'inner', [(i, i ^ hop) for i in range(ranks)])  21 us
    ppermute x15, waiting for transfers between devices, shards(): lax.ppermute(mine, 'inner', [(i, i ^ hop) for i in range(ranks)])  8.39 us
    ppermute x8, starting transfers between devices, shards(): lax.ppermute(results.pop(0), 'outer', to_second if final else to_first)  6.11 us
    unnamed x7, local copies, waits for them, and re-layouts  4.82 us
  transfers between devices with their start and end apart: 25, of which 12 were waited for; matrix products, arithmetic and copies ran while one was open for 0% of the time, Pallas kernels for 9%

profile of v1, /device:TPU:0, one launch (start us, length us, event | category | flops | bytes accessed | tf_op | source)
XLA Modules:
  0.0 235.3 jit_solution(9322797960158827852)
XLA Ops:
  0.0 1.4 copy.10.blocks_ref
  1.4 35.0 %opening.1 = (s32[2,9]{1,0:T(2,128)}, f32[1,9]{1,0:T(1,128)}, bf16[1024,256]{1,0:T(8,128)(2,1)}, bf16[1024,256]{1,0:T(8,128)(2,1)}) custom-call(s32[32,2]{1,0:T(8,128)} %copy.10.blocks_ref, f32[32]{0:T(128)} %weight_ref.1, bf16[1024,2048]{1,0:T(8,128)(2,1)} %refs_2_.19), custom_call_target="tpu_custom_call" | custom-call | tf_op jit(solution)/shard_map/opening/pallas_call | solution.py:178
  36.3 4.1 %collective-permute-start = (bf16[1024,256]{1,0:T(8,128)(2,1)}, bf16[1024,256]{1,0:T(8,128)(2,1)S(1)}, u32[]{:S(2)}, u32[]{:S(2)}) collective-permute-start(bf16[1024,256]{1,0:T(8,128)(2,1)} %get-tuple-element.29), channel_id=1, source_target_pairs={{0,8},{4,12},{8,0},{12,4},{1,9},{5,13},{9,1},{13,5},{2,10},{6,14},... | collective-permute-start | bytes 1572872 | tf_op jit(solution)/shard_map/ppermute | solution.py:191
  40.5 35.4 %collective-permute-done.refs_3_.refs_4_ = bf16[1024,256]{1,0:T(8,128)(2,1)S(1)} collective-permute-done((bf16[1024,256]{1,0:T(8,128)(2,1)}, bf16[1024,256]{1,0:T(8,128)(2,1)S(1)}, u32[]{:S(2)}, u32[]{:S(2)}) %collective-permute-start) | collective-permute-done | bytes 524320 | tf_op jit(solution)/shard_map/ppermute | solution.py:191
  75.9 2.2 copy-done
  79.3 2.0 step.10
  81.4 1.9 collective-permute-start.8
  83.5 2.7 %collective-permute-done.3.refs_3_.refs_4_ = bf16[1024,256]{1,0:T(8,128)(2,1)S(1)} collective-permute-done((bf16[1024,256]{1,0:T(8,128)(2,1)}, bf16[1024,256]{1,0:T(8,128)(2,1)S(1)}, u32[]{:S(2)}, u32[]{:S(2)}) %collective-permute-start.3) | collective-permute-done | bytes 524320 | tf_op jit(solution)/shard_map/ppermute | solution.py:191
  86.3 1.9 step.12
  88.4 1.3 collective-permute-done.10.refs_8_
  90.4 11.2 %collective-permute-start.5 = (f32[2,2,128,128]{3,2,1,0:T(8,128)S(1)}, f32[2,2,128,128]{3,2,1,0:T(8,128)S(1)}, u32[]{:S(2)}, u32[]{:S(2)}) collective-permute-start(f32[2,2,128,128]{3,2,1,0:T(8,128)S(1)} %get-tuple-element.33.refs_5_), channel_id=1, source_target_pairs={{0,2},{1,3},{2,0},{3,1},{4,6},{5,7},{6,4},{7,5},{8,10},{9,11},{10,... | collective-permute-start | bytes 786440 | tf_op jit(solution)/shard_map/ppermute | solution.py:244
  101.7 18.7 %collective-permute-done.7.refs_3_ = bf16[1024,128]{1,0:T(8,128)(2,1)S(1)} collective-permute-done((bf16[1024,128]{1,0:T(8,128)(2,1)S(1)}, bf16[1024,128]{1,0:T(8,128)(2,1)S(1)}, u32[]{:S(2)}, u32[]{:S(2)}) %collective-permute-start.7) | collective-permute-done | bytes 262176 | tf_op jit(solution)/shard_map/ppermute | solution.py:247
  120.4 3.3 %step.13 = (f32[1,2,128,128]{3,2,1,0:T(8,128)S(1)}, bf16[1024,256]{1,0:T(8,128)(2,1)S(1)}, bf16[1024,2048]{1,0:T(8,128)(2,1)}) custom-call(s32[2,9]{1,0:T(2,128)S(1)} %copy-done.1, f32[1,9]{1,0:T(1,128)S(1)} %copy-done.2, bf16[1024,2048]{1,0:T(8,128)(2,1)S(1)} %copy-done, bf16[1024,128]{1,0:T(8,128)(2,1)S(1)} %collective-permute-done.7.refs_3_, ...), custom_call_target="tpu_custom_call" | custom-call | tf_op jit(solution)/shard_map/step/pallas_call | solution.py:223
  124.3 1.9 step.11
  126.2 2.6 %collective-permute-start.2 = (bf16[1024,128]{1,0:T(8,128)(2,1)S(1)}, bf16[1024,128]{1,0:T(8,128)(2,1)S(1)}, u32[]{:S(2)}, u32[]{:S(2)}) collective-permute-start(bf16[1024,128]{1,0:T(8,128)(2,1)S(1)} %get-tuple-element.31), channel_id=1, source_target_pairs={{0,8},{4,12},{8,0},{12,4},{1,9},{5,13},{9,1},{13,5},{2,10},{6,14},... | collective-permute-start | bytes 786440 | tf_op jit(solution)/shard_map/ppermute | solution.py:247
  130.5 1.7 collective-permute-done.6.refs_8_
  133.0 28.0 %collective-permute-done.2.refs_3_ = bf16[1024,128]{1,0:T(8,128)(2,1)S(1)} collective-permute-done((bf16[1024,128]{1,0:T(8,128)(2,1)S(1)}, bf16[1024,128]{1,0:T(8,128)(2,1)S(1)}, u32[]{:S(2)}, u32[]{:S(2)}) %collective-permute-start.2) | collective-permute-done | bytes 262176 | tf_op jit(solution)/shard_map/ppermute | solution.py:247
  161.0 3.3 %step.14 = (f32[1,2,128,128]{3,2,1,0:T(8,128)S(1)}, bf16[1024,256]{1,0:T(8,128)(2,1)S(1)}, bf16[1024,2048]{1,0:T(8,128)(2,1)}) custom-call(s32[2,9]{1,0:T(2,128)S(1)} %copy-done.1, f32[1,9]{1,0:T(1,128)S(1)} %copy-done.2, bf16[1024,2048]{1,0:T(8,128)(2,1)S(1)} %copy-done, ...), custom_call_target="tpu_custom_call", output_to_operand_aliasing={{2}: (9, {})} | custom-call | tf_op jit(solution)/shard_map/step/pallas_call | solution.py:223
  164.5 2.9 %step.15 = (bf16[1024,256]{1,0:T(8,128)(2,1)S(1)}, bf16[1024,2048]{1,0:T(8,128)(2,1)}) custom-call(s32[2,9]{1,0:T(2,128)S(1)} %copy-done.1, f32[1,9]{1,0:T(1,128)S(1)} %copy-done.2, bf16[1024,2048]{1,0:T(8,128)(2,1)S(1)} %copy-done, bf16[1024,256]{1,0:T(8,128)(2,1)S(1)} %collective-permute-done.1.refs_3_, ...), custom_call_target="tpu_custom_call", output_to_operand_aliasing={{1}: (9, {})} | custom-call | tf_op jit(solution)/shard_map/step/pallas_call | solution.py:223
  167.4 3.0 %collective-permute-start.18 = (bf16[1024,256]{1,0:T(8,128)(2,1)S(1)}, bf16[1024,256]{1,0:T(8,128)(2,1)S(1)}, u32[]{:S(2)}, u32[]{:S(2)}) collective-permute-start(bf16[1024,256]{1,0:T(8,128)(2,1)S(1)} %get-tuple-element.41), channel_id=1, source_target_pairs={{0,8},{4,12},{8,0},{12,4},{1,9},{5,13},{9,1},{13,5},{2,10},{6,14},... | collective-permute-start | bytes 1572872 | tf_op jit(solution)/shard_map/ppermute | solution.py:247
  171.1 1.1 collective-permute-start.21
  172.5 4.1 %collective-permute-done.20.refs_6_ = f32[1,2,128,128]{3,2,1,0:T(8,128)S(1)} collective-permute-done((f32[1,2,128,128]{3,2,1,0:T(8,128)S(1)}, f32[1,2,128,128]{3,2,1,0:T(8,128)S(1)}, u32[]{:S(2)}, u32[]{:S(2)}) %collective-permute-start.20) | collective-permute-done | bytes 131104 | tf_op jit(solution)/shard_map/ppermute | solution.py:244
  177.4 1.2 collective-permute-done.21.refs_7_
  178.7 1.0 collective-permute-start.13
  179.7 20.6 %collective-permute-done.22.refs_8_ = bf16[1024,256]{1,0:T(8,128)(2,1)S(1)} collective-permute-done((bf16[1024,256]{1,0:T(8,128)(2,1)S(1)}, bf16[1024,256]{1,0:T(8,128)(2,1)S(1)}, u32[]{:S(2)}, u32[]{:S(2)}) %collective-permute-start.22) | collective-permute-done | bytes 524320 | tf_op jit(solution)/shard_map/ppermute | solution.py:247
  200.3 2.0 step.16
  202.4 14.7 %collective-permute-done.18.refs_8_ = bf16[1024,256]{1,0:T(8,128)(2,1)S(1)} collective-permute-done((bf16[1024,256]{1,0:T(8,128)(2,1)S(1)}, bf16[1024,256]{1,0:T(8,128)(2,1)S(1)}, u32[]{:S(2)}, u32[]{:S(2)}) %collective-permute-start.18) | collective-permute-done | bytes 524320 | tf_op jit(solution)/shard_map/ppermute | solution.py:247
  217.1 2.0 step.17
  219.2 9.1 %collective-permute-done.24.refs_3_ = bf16[1024,128]{1,0:T(8,128)(2,1)S(1)} collective-permute-done((bf16[1024,128]{1,0:T(8,128)(2,1)S(1)}, bf16[1024,128]{1,0:T(8,128)(2,1)S(1)}, u32[]{:S(2)}, u32[]{:S(2)}) %collective-permute-start.24) | collective-permute-done | bytes 262176 | tf_op jit(solution)/shard_map/ppermute | solution.py:247
  228.4 1.4 step.18.refs_4_
  229.8 4.1 %collective-permute-done.23.refs_3_ = bf16[1024,128]{1,0:T(8,128)(2,1)S(1)} collective-permute-done((bf16[1024,128]{1,0:T(8,128)(2,1)S(1)}, bf16[1024,128]{1,0:T(8,128)(2,1)S(1)}, u32[]{:S(2)}, u32[]{:S(2)}) %collective-permute-start.23) | collective-permute-done | bytes 262176 | tf_op jit(solution)/shard_map/ppermute | solution.py:247
  233.9 1.4 step.19
  (36 shorter events, 7.7 us)
Async XLA Ops:
  36.3 39.5 %collective-permute-start = (bf16[1024,256]{1,0:T(8,128)(2,1)}, bf16[1024,256]{1,0:T(8,128)(2,1)S(1)}, u32[]{:S(2)}, u32[]{:S(2)}) collective-permute-start(bf16[1024,256]{1,0:T(8,128)(2,1)} %get-tuple-element.29), channel_id=1, source_target_pairs={{0,8},{4,12},{8,0},{12,4},{1,9},{5,13},{9,1},{13,5},{2,10},{6,14},... | collective-permute-start | bytes 1572872 | tf_op jit(solution)/shard_map/ppermute | solution.py:191
  40.4 45.8 %collective-permute-start.3 = (bf16[1024,256]{1,0:T(8,128)(2,1)}, bf16[1024,256]{1,0:T(8,128)(2,1)S(1)}, u32[]{:S(2)}, u32[]{:S(2)}) collective-permute-start(bf16[1024,256]{1,0:T(8,128)(2,1)} %get-tuple-element.32), channel_id=1, source_target_pairs={{0,8},{4,12},{8,0},{12,4},{1,9},{5,13},{9,1},{13,5},{2,10},{6,14},... | collective-permute-start | bytes 1572872 | tf_op jit(solution)/shard_map/ppermute | solution.py:191
  75.9 2.2 copy-start
  78.1 0.7 copy-start.1
  78.7 0.6 copy-start.2
  81.3 8.4 %collective-permute-start.10 = (f32[2,2,128,128]{3,2,1,0:T(8,128)S(1)}, f32[2,2,128,128]{3,2,1,0:T(8,128)S(1)}, u32[]{:S(2)}, u32[]{:S(2)}) collective-permute-start(f32[2,2,128,128]{3,2,1,0:T(8,128)S(1)} %get-tuple-element.35.refs_5_), channel_id=1, source_target_pairs={{0,3},{1,2},{2,1},{3,0},{4,7},{5,6},{6,5},{7,4},{8,11},{9,10},{10,... | collective-permute-start | bytes 786440 | tf_op jit(solution)/shard_map/ppermute | solution.py:244
  81.4 9.0 %collective-permute-start.8 = (f32[2,2,128,128]{3,2,1,0:T(8,128)S(1)}, f32[2,2,128,128]{3,2,1,0:T(8,128)S(1)}, u32[]{:S(2)}, u32[]{:S(2)}) collective-permute-start(f32[2,2,128,128]{3,2,1,0:T(8,128)S(1)} %get-tuple-element.35.refs_5_), channel_id=1, source_target_pairs={{0,1},{1,0},{2,3},{3,2},{4,5},{5,4},{6,7},{7,6},{8,9},{9,8},{10,11... | collective-permute-start | bytes 786440 | tf_op jit(solution)/shard_map/ppermute | solution.py:244
  83.3 40.9 %collective-permute-start.1 = (bf16[1024,256]{1,0:T(8,128)(2,1)S(1)}, bf16[1024,256]{1,0:T(8,128)(2,1)S(1)}, u32[]{:S(2)}, u32[]{:S(2)}) collective-permute-start(bf16[1024,256]{1,0:T(8,128)(2,1)S(1)} %get-tuple-element.30), channel_id=1, source_target_pairs={{0,8},{4,12},{8,0},{12,4},{1,9},{5,13},{9,1},{13,5},{2,10},{6,14},... | collective-permute-start | bytes 1572872 | tf_op jit(solution)/shard_map/ppermute | solution.py:247
  83.3 18.3 %collective-permute-start.9 = (f32[2,2,128,128]{3,2,1,0:T(8,128)S(1)}, f32[2,2,128,128]{3,2,1,0:T(8,128)S(1)}, u32[]{:S(2)}, u32[]{:S(2)}) collective-permute-start(f32[2,2,128,128]{3,2,1,0:T(8,128)S(1)} %get-tuple-element.35.refs_5_), channel_id=1, source_target_pairs={{0,2},{1,3},{2,0},{3,1},{4,6},{5,7},{6,4},{7,5},{8,10},{9,11},{10,... | collective-permute-start | bytes 786440 | tf_op jit(solution)/shard_map/ppermute | solution.py:244
  88.2 32.2 %collective-permute-start.7 = (bf16[1024,128]{1,0:T(8,128)(2,1)S(1)}, bf16[1024,128]{1,0:T(8,128)(2,1)S(1)}, u32[]{:S(2)}, u32[]{:S(2)}) collective-permute-start(bf16[1024,128]{1,0:T(8,128)(2,1)S(1)} %get-tuple-element.34), channel_id=1, source_target_pairs={{0,8},{4,12},{8,0},{12,4},{1,9},{5,13},{9,1},{13,5},{2,10},{6,14},... | collective-permute-start | bytes 786440 | tf_op jit(solution)/shard_map/ppermute | solution.py:247
  89.7 39.1 %collective-permute-start.4 = (f32[2,2,128,128]{3,2,1,0:T(8,128)S(1)}, f32[2,2,128,128]{3,2,1,0:T(8,128)S(1)}, u32[]{:S(2)}, u32[]{:S(2)}) collective-permute-start(f32[2,2,128,128]{3,2,1,0:T(8,128)S(1)} %get-tuple-element.33.refs_5_), channel_id=1, source_target_pairs={{0,1},{1,0},{2,3},{3,2},{4,5},{5,4},{6,7},{7,6},{8,9},{9,8},{10,11... | collective-permute-start | bytes 786440 | tf_op jit(solution)/shard_map/ppermute | solution.py:244
  90.4 39.3 %collective-permute-start.5 = (f32[2,2,128,128]{3,2,1,0:T(8,128)S(1)}, f32[2,2,128,128]{3,2,1,0:T(8,128)S(1)}, u32[]{:S(2)}, u32[]{:S(2)}) collective-permute-start(f32[2,2,128,128]{3,2,1,0:T(8,128)S(1)} %get-tuple-element.33.refs_5_), channel_id=1, source_target_pairs={{0,2},{1,3},{2,0},{3,1},{4,6},{5,7},{6,4},{7,5},{8,10},{9,11},{10,... | collective-permute-start | bytes 786440 | tf_op jit(solution)/shard_map/ppermute | solution.py:244
  123.7 40.7 %collective-permute-start.17 = (bf16[1024,256]{1,0:T(8,128)(2,1)S(1)}, bf16[1024,256]{1,0:T(8,128)(2,1)S(1)}, u32[]{:S(2)}, u32[]{:S(2)}) collective-permute-start(bf16[1024,256]{1,0:T(8,128)(2,1)S(1)} %get-tuple-element.39), channel_id=1, source_target_pairs={{0,8},{4,12},{8,0},{12,4},{1,9},{5,13},{9,1},{13,5},{2,10},{6,14},... | collective-permute-start | bytes 1572872 | tf_op jit(solution)/shard_map/ppermute | solution.py:247
  123.8 8.5 %collective-permute-start.6 = (f32[2,2,128,128]{3,2,1,0:T(8,128)S(1)}, f32[2,2,128,128]{3,2,1,0:T(8,128)S(1)}, u32[]{:S(2)}, u32[]{:S(2)}) collective-permute-start(f32[2,2,128,128]{3,2,1,0:T(8,128)S(1)} %get-tuple-element.33.refs_5_), channel_id=1, source_target_pairs={{0,3},{1,2},{2,1},{3,0},{4,7},{5,6},{6,5},{7,4},{8,11},{9,10},{10,... | collective-permute-start | bytes 786440 | tf_op jit(solution)/shard_map/ppermute | solution.py:244
  126.2 34.8 %collective-permute-start.2 = (bf16[1024,128]{1,0:T(8,128)(2,1)S(1)}, bf16[1024,128]{1,0:T(8,128)(2,1)S(1)}, u32[]{:S(2)}, u32[]{:S(2)}) collective-permute-start(bf16[1024,128]{1,0:T(8,128)(2,1)S(1)} %get-tuple-element.31), channel_id=1, source_target_pairs={{0,8},{4,12},{8,0},{12,4},{1,9},{5,13},{9,1},{13,5},{2,10},{6,14},... | collective-permute-start | bytes 786440 | tf_op jit(solution)/shard_map/ppermute | solution.py:247
  128.8 35.6 %collective-permute-start.14 = (f32[2,2,128,128]{3,2,1,0:T(8,128)S(1)}, f32[2,2,128,128]{3,2,1,0:T(8,128)S(1)}, u32[]{:S(2)}, u32[]{:S(2)}) collective-permute-start(f32[2,2,128,128]{3,2,1,0:T(8,128)S(1)} %get-tuple-element.38.refs_4_), channel_id=1, source_target_pairs={{0,1},{1,0},{2,3},{3,2},{4,5},{5,4},{6,7},{7,6},{8,9},{9,8},{10,11... | collective-permute-start | bytes 786440 | tf_op jit(solution)/shard_map/ppermute | solution.py:244
  129.7 34.8 %collective-permute-start.15 = (f32[2,2,128,128]{3,2,1,0:T(8,128)S(1)}, f32[2,2,128,128]{3,2,1,0:T(8,128)S(1)}, u32[]{:S(2)}, u32[]{:S(2)}) collective-permute-start(f32[2,2,128,128]{3,2,1,0:T(8,128)S(1)} %get-tuple-element.38.refs_4_), channel_id=1, source_target_pairs={{0,2},{1,3},{2,0},{3,1},{4,6},{5,7},{6,4},{7,5},{8,10},{9,11},{10,... | collective-permute-start | bytes 786440 | tf_op jit(solution)/shard_map/ppermute | solution.py:244
  132.3 32.2 %collective-permute-start.16 = (f32[2,2,128,128]{3,2,1,0:T(8,128)S(1)}, f32[2,2,128,128]{3,2,1,0:T(8,128)S(1)}, u32[]{:S(2)}, u32[]{:S(2)}) collective-permute-start(f32[2,2,128,128]{3,2,1,0:T(8,128)S(1)} %get-tuple-element.38.refs_4_), channel_id=1, source_target_pairs={{0,3},{1,2},{2,1},{3,0},{4,7},{5,6},{6,5},{7,4},{8,11},{9,10},{10,... | collective-permute-start | bytes 786440 | tf_op jit(solution)/shard_map/ppermute | solution.py:244
  164.3 35.9 %collective-permute-start.22 = (bf16[1024,256]{1,0:T(8,128)(2,1)S(1)}, bf16[1024,256]{1,0:T(8,128)(2,1)S(1)}, u32[]{:S(2)}, u32[]{:S(2)}) collective-permute-start(bf16[1024,256]{1,0:T(8,128)(2,1)S(1)} %get-tuple-element.43), channel_id=1, source_target_pairs={{0,8},{4,12},{8,0},{12,4},{1,9},{5,13},{9,1},{13,5},{2,10},{6,14},... | collective-permute-start | bytes 1572872 | tf_op jit(solution)/shard_map/ppermute | solution.py:247
  167.4 49.7 %collective-permute-start.18 = (bf16[1024,256]{1,0:T(8,128)(2,1)S(1)}, bf16[1024,256]{1,0:T(8,128)(2,1)S(1)}, u32[]{:S(2)}, u32[]{:S(2)}) collective-permute-start(bf16[1024,256]{1,0:T(8,128)(2,1)S(1)} %get-tuple-element.41), channel_id=1, source_target_pairs={{0,8},{4,12},{8,0},{12,4},{1,9},{5,13},{9,1},{13,5},{2,10},{6,14},... | collective-permute-start | bytes 1572872 | tf_op jit(solution)/shard_map/ppermute | solution.py:247
  170.3 1.9 collective-permute-start.19
  170.3 6.3 %collective-permute-start.20 = (f32[1,2,128,128]{3,2,1,0:T(8,128)S(1)}, f32[1,2,128,128]{3,2,1,0:T(8,128)S(1)}, u32[]{:S(2)}, u32[]{:S(2)}) collective-permute-start(f32[1,2,128,128]{3,2,1,0:T(8,128)S(1)} %get-tuple-element.42.refs_4_), channel_id=1, source_target_pairs={{0,2},{1,3},{2,0},{3,1},{4,6},{5,7},{6,4},{7,5},{8,10},{9,11},{10,... | collective-permute-start | bytes 393224 | tf_op jit(solution)/shard_map/ppermute | solution.py:244
  171.1 7.5 %collective-permute-start.21 = (f32[1,2,128,128]{3,2,1,0:T(8,128)S(1)}, f32[1,2,128,128]{3,2,1,0:T(8,128)S(1)}, u32[]{:S(2)}, u32[]{:S(2)}) collective-permute-start(f32[1,2,128,128]{3,2,1,0:T(8,128)S(1)} %get-tuple-element.42.refs_4_), channel_id=1, source_target_pairs={{0,3},{1,2},{2,1},{3,0},{4,7},{5,6},{6,5},{7,4},{8,11},{9,10},{10,... | collective-permute-start | bytes 393224 | tf_op jit(solution)/shard_map/ppermute | solution.py:244
  172.2 30.2 %collective-permute-start.11 = (f32[1,2,128,128]{3,2,1,0:T(8,128)S(1)}, f32[1,2,128,128]{3,2,1,0:T(8,128)S(1)}, u32[]{:S(2)}, u32[]{:S(2)}) collective-permute-start(f32[1,2,128,128]{3,2,1,0:T(8,128)S(1)} %get-tuple-element.37.refs_4_), channel_id=1, source_target_pairs={{0,1},{1,0},{2,3},{3,2},{4,5},{5,4},{6,7},{7,6},{8,9},{9,8},{10,11... | collective-permute-start | bytes 393224 | tf_op jit(solution)/shard_map/ppermute | solution.py:244
  176.6 25.7 %collective-permute-start.12 = (f32[1,2,128,128]{3,2,1,0:T(8,128)S(1)}, f32[1,2,128,128]{3,2,1,0:T(8,128)S(1)}, u32[]{:S(2)}, u32[]{:S(2)}) collective-permute-start(f32[1,2,128,128]{3,2,1,0:T(8,128)S(1)} %get-tuple-element.37.refs_4_), channel_id=1, source_target_pairs={{0,2},{1,3},{2,0},{3,1},{4,6},{5,7},{6,4},{7,5},{8,10},{9,11},{10,... | collective-permute-start | bytes 393224 | tf_op jit(solution)/shard_map/ppermute | solution.py:244
  178.7 23.7 %collective-permute-start.13 = (f32[1,2,128,128]{3,2,1,0:T(8,128)S(1)}, f32[1,2,128,128]{3,2,1,0:T(8,128)S(1)}, u32[]{:S(2)}, u32[]{:S(2)}) collective-permute-start(f32[1,2,128,128]{3,2,1,0:T(8,128)S(1)} %get-tuple-element.37.refs_4_), channel_id=1, source_target_pairs={{0,3},{1,2},{2,1},{3,0},{4,7},{5,6},{6,5},{7,4},{8,11},{9,10},{10,... | collective-permute-start | bytes 393224 | tf_op jit(solution)/shard_map/ppermute | solution.py:244
  202.3 26.1 %collective-permute-start.24 = (bf16[1024,128]{1,0:T(8,128)(2,1)S(1)}, bf16[1024,128]{1,0:T(8,128)(2,1)S(1)}, u32[]{:S(2)}, u32[]{:S(2)}) collective-permute-start(bf16[1024,128]{1,0:T(8,128)(2,1)S(1)} %get-tuple-element.47), channel_id=1, source_target_pairs={{0,8},{4,12},{8,0},{12,4},{1,9},{5,13},{9,1},{13,5},{2,10},{6,14},... | collective-permute-start | bytes 786440 | tf_op jit(solution)/shard_map/ppermute | solution.py:247
  219.1 14.7 %collective-permute-start.23 = (bf16[1024,128]{1,0:T(8,128)(2,1)S(1)}, bf16[1024,128]{1,0:T(8,128)(2,1)S(1)}, u32[]{:S(2)}, u32[]{:S(2)}) collective-permute-start(bf16[1024,128]{1,0:T(8,128)(2,1)S(1)} %get-tuple-element.46), channel_id=1, source_target_pairs={{0,8},{4,12},{8,0},{12,4},{1,9},{5,13},{9,1},{13,5},{2,10},{6,14},... | collective-permute-start | bytes 786440 | tf_op jit(solution)/shard_map/ppermute | solution.py:247

commit v2 on v1

--- a/solution.py
+++ b/solution.py
@@ -9,10 +9,11 @@
 
 BLOCK = 128
 STRETCH = 256
-CHUNKS = (2, 2, 2, 1, 1)
-LAG = 2
+CHUNKS = (1,2,2,2,1,)
+LAG = 3
 
 ANY = pl.BlockSpec(memory_space=pl.ANY)
+HBM = pl.BlockSpec(memory_space=pltpu.HBM)
 VMEM = pl.BlockSpec(memory_space=pltpu.VMEM)
 SMEM = pl.BlockSpec(memory_space=pltpu.SMEM)
 
@@ -28,7 +29,7 @@
     me = lax.axis_index("outer")
 
     def one(c, counts):
-        first, second = blocks_ref[c, 0], blocks_ref[c, 1]
+        first, second = blocks_ref[0, c], blocks_ref[1, c]
         firsts, seconds = counts
         place_ref[0, firsts] = lax.rem(first, per_dev)
         scale_ref[0, firsts] = 4.0 * weight_ref[c]
@@ -37,7 +38,7 @@
         seconds += (lax.div(second, per_dev) == me).astype(jnp.int32)
         return firsts, seconds
 
-    lax.fori_loop(0, blocks_ref.shape[0], one, (jnp.int32(0), jnp.int32(0)))
+    lax.fori_loop(0, blocks_ref.shape[1], one, (jnp.int32(0), jnp.int32(0)))
 
 
 def opening_kernel(per_dev, starts, sizes, blocks_ref, weight_ref, decoder_ref, place_ref, scale_ref, *rest):
@@ -90,7 +91,7 @@
     final_in = take() if spec["final"] else None
     parts = [take() for _ in range(spec["ranks"])] if spec["final"] else None
     back_in = take() if spec["back"] else None
-    if spec["aliased"]:
+    for _ in range(spec["unread"]):
         take()
     gram_out = take() if spec["gram"] else None
     send_out = take() if spec["final"] or spec["pack"] else None
@@ -185,12 +186,13 @@
         in_specs=[SMEM, SMEM, ANY],
         out_specs=[SMEM, SMEM] + [ANY] * LAG,
         scratch_shapes=[pltpu.SemaphoreType.DMA((per_dev,))],
+        compiler_params=pltpu.CompilerParams(vmem_limit_bytes=8 * 2**20),
         name="opening",
-    )(stretch_blocks, stretch_weight, decoder)
+    )(stretch_blocks.T, stretch_weight, decoder)
 
     sends = [lax.ppermute(part, "outer", to_first) for part in raw]
     parts = {}
-    out = None
+    out = chain = None
     for step in range(2 * count):
         arrived = sends[step]
         gram = chunk(step) if step < count else None
@@ -198,8 +200,8 @@
         turn = step + LAG - count
         final = chunk(turn) if 0 <= turn < count else None
         back = chunk(step - count) if step >= count else None
-        spec = {"gram": gram, "pack": pack, "final": final, "back": back, "ranks": ranks, "aliased": out is not None}
-        args, specs = [place, scale, decoder], [SMEM, SMEM, ANY]
+        spec = {"gram": gram, "pack": pack, "final": final, "back": back, "ranks": ranks, "unread": 0}
+        args, specs = [place, scale, decoder], [SMEM, SMEM, HBM]
         shapes, out_specs, aliases = [], [], {}
         if gram:
             args, specs = args + [arrived], specs + [ANY]
@@ -215,9 +217,13 @@
         if final or back:
             if out is not None:
                 aliases = {len(args): len(shapes)}
-                args, specs = args + [out], specs + [ANY]
+                args, specs, chain = args + [out], specs + [ANY], None
+                spec["unread"] += 1
             shapes.append(out_shape)
             out_specs.append(ANY)
+        if chain is not None:
+            args, specs = args + [chain], specs + [ANY]
+            spec["unread"] += 1
         slot = max(sizes)
         results = list(
             pl.pallas_call(
@@ -239,7 +245,7 @@
             )(*args)
         )
         if gram:
-            mine = results.pop(0)
+            chain = mine = results.pop(0)
             parts[step] = [mine] + [
                 lax.ppermute(mine, "inner", [(i, i ^ hop) for i in range(ranks)]) for hop in range(1, ranks)
             ]

time: 236 us -> 192 us (0.81)
  Pallas kernels: 57.2 us -> 25.3 us
  starting transfers between devices: 31.3 us -> 22.5 us
    pallas_call x1, Pallas kernels: 35 us -> 2.25 us  [shards(): pl.pallas_call(functools.partial(opening_kernel, per_dev, starts[:LAG], s...]
    ppermute x8 -> x7, waiting for transfers between devices: 95.3 us -> 78 us  [shards(): lax.ppermute(results.pop(0), 'outer', to_second if final else to_first)]
    ppermute x2 -> x3, waiting for transfers between devices: 38.1 us -> 53.8 us  [shards(): sends = [lax.ppermute(part, 'outer', to_first) for part in raw]]
    ppermute x15, starting transfers between devices: 21 us -> 12.4 us  [shards(): lax.ppermute(mine, 'inner', [(i, i ^ hop) for i in range(ranks)])]
    ppermute x8 -> x7, starting transfers between devices: 6.11 us -> 3.05 us  [shards(): lax.ppermute(results.pop(0), 'outer', to_second if final else to_first)]
    ppermute x2 -> x3, starting transfers between devices: 4.18 us -> 7.02 us  [shards(): sends = [lax.ppermute(part, 'outer', to_first) for part in raw]]
    unnamed x7 -> x8, local copies, waits for them, and re-layouts: 4.82 us -> 3.52 us
  transfers between devices with their start and end apart: 25 -> 25, of which waited for: 12 -> 13; matrix products, arithmetic and copies ran while one was open for 0% -> 0% of each run, Pallas kernels for 9% -> 11%
where the time goes in v2:
time: 192 us
  waiting for transfers between devices  140 us (73%)
  Pallas kernels  25.3 us (13%)
  starting transfers between devices  22.5 us (12%)
  local copies, waits for them, and re-layouts  3.52 us (2%)
    ppermute x7, waiting for transfers between devices, shards(): lax.ppermute(results.pop(0), 'outer', to_second if final else to_first)  78 us
    ppermute x3, waiting for transfers between devices, shards(): sends = [lax.ppermute(part, 'outer', to_first) for part in raw]  53.8 us
    pallas_call x10, Pallas kernels, shards(): pl.pallas_call(functools.partial(step_kernel, spec), out_shape=shapes, in...  23.1 us
    ppermute x15, starting transfers between devices, shards(): lax.ppermute(mine, 'inner', [(i, i ^ hop) for i in range(ranks)])  12.4 us
    ppermute x15, waiting for transfers between devices, shards(): lax.ppermute(mine, 'inner', [(i, i ^ hop) for i in range(ranks)])  8.34 us
    ppermute x3, starting transfers between devices, shards(): sends = [lax.ppermute(part, 'outer', to_first) for part in raw]  7.02 us
  transfers between devices with their start and end apart: 25, of which 13 were waited for; matrix products, arithmetic and copies ran while one was open for 0% of the time, Pallas kernels for 11%

profile of v2, /device:TPU:0, one launch (start us, length us, event | category | flops | bytes accessed | tf_op | source)
XLA Modules:
  0.0 191.7 jit_solution(5932462871309208353)
XLA Ops:
  0.0 2.2 %copy-done = bf16[1024,2048]{1,0:T(8,128)(2,1)S(1)} copy-done((bf16[1024,2048]{1,0:T(8,128)(2,1)S(1)}, bf16[1024,2048]{1,0:T(8,128)(2,1)}, u32[]{:S(2)}) %copy-start) | copy-done | bytes 4194328
  3.5 2.3 %opening.1 = (s32[2,9]{1,0:T(2,128)S(1)}, f32[1,9]{1,0:T(1,128)S(1)}, bf16[1024,128]{1,0:T(8,128)(2,1)S(1)}, bf16[1024,256]{1,0:T(8,128)(2,1)S(1)}, bf16[1024,256]{1,0:T(8,128)(2,1)S(1)}) custom-call(s32[2,32]{1,0:T(2,128)S(1)} %bitcast.1, f32[32]{0:T(128)S(1)} %copy-done.3, bf16[1024,2048]{1,0:T(8,128)(2,1)S(1)} %copy-done), custom_call_target="tpu_custom_call" | custom-call | tf_op jit(solution)/shard_map/opening/pallas_call | solution.py:179
  5.8 4.1 %collective-permute-start = (bf16[1024,256]{1,0:T(8,128)(2,1)S(1)}, bf16[1024,256]{1,0:T(8,128)(2,1)S(1)}, u32[]{:S(2)}, u32[]{:S(2)}) collective-permute-start(bf16[1024,256]{1,0:T(8,128)(2,1)S(1)} %get-tuple-element.29), channel_id=1, source_target_pairs={{0,8},{4,12},{8,0},{12,4},{1,9},{5,13},{9,1},{13,5},{2,10},{6,14},... | collective-permute-start | bytes 1572872 | tf_op jit(solution)/shard_map/ppermute | solution.py:193
  10.0 2.8 %collective-permute-start.3 = (bf16[1024,256]{1,0:T(8,128)(2,1)S(1)}, bf16[1024,256]{1,0:T(8,128)(2,1)S(1)}, u32[]{:S(2)}, u32[]{:S(2)}) collective-permute-start(bf16[1024,256]{1,0:T(8,128)(2,1)S(1)} %get-tuple-element.33), channel_id=1, source_target_pairs={{0,8},{4,12},{8,0},{12,4},{1,9},{5,13},{9,1},{13,5},{2,10},{6,14},... | collective-permute-start | bytes 1572872 | tf_op jit(solution)/shard_map/ppermute | solution.py:193
  12.8 43.5 %collective-permute-done.1.refs_3_.refs_4_ = bf16[1024,128]{1,0:T(8,128)(2,1)S(1)} collective-permute-done((bf16[1024,128]{1,0:T(8,128)(2,1)S(1)}, bf16[1024,128]{1,0:T(8,128)(2,1)S(1)}, u32[]{:S(2)}, u32[]{:S(2)}) %collective-permute-start.1) | collective-permute-done | bytes 262176 | tf_op jit(solution)/shard_map/ppermute | solution.py:193
  57.8 1.9 collective-permute-start.5
  59.7 1.9 step.11
  62.0 2.2 %collective-permute-done.5.refs_7_ = f32[1,2,128,128]{3,2,1,0:T(8,128)S(1)} collective-permute-done((f32[1,2,128,128]{3,2,1,0:T(8,128)S(1)}, f32[1,2,128,128]{3,2,1,0:T(8,128)S(1)}, u32[]{:S(2)}, u32[]{:S(2)}) %collective-permute-start.5) | collective-permute-done | bytes 131104 | tf_op jit(solution)/shard_map/ppermute | solution.py:250
  64.1 1.9 collective-permute-start.12
  66.3 2.2 %collective-permute-start.13 = (f32[2,2,128,128]{3,2,1,0:T(8,128)S(1)}, f32[2,2,128,128]{3,2,1,0:T(8,128)S(1)}, u32[]{:S(2)}, u32[]{:S(2)}) collective-permute-start(f32[2,2,128,128]{3,2,1,0:T(8,128)S(1)} %get-tuple-element.34.refs_9_.refs_5_), channel_id=1, source_target_pairs={{0,3},{1,2},{2,1},{3,0},{4,7},{5,6},{6,5},{7,4},{8,11},{9,10},{10,... | collective-permute-start | bytes 786440 | tf_op jit(solution)/shard_map/ppermute | solution.py:250
  68.5 10.3 %collective-permute-done.3.refs_3_.refs_4_ = bf16[1024,256]{1,0:T(8,128)(2,1)S(1)} collective-permute-done((bf16[1024,256]{1,0:T(8,128)(2,1)S(1)}, bf16[1024,256]{1,0:T(8,128)(2,1)S(1)}, u32[]{:S(2)}, u32[]{:S(2)}) %collective-permute-start.3) | collective-permute-done | bytes 524320 | tf_op jit(solution)/shard_map/ppermute | solution.py:193
  78.8 3.1 %step.12 = (f32[2,2,128,128]{3,2,1,0:T(8,128)S(1)}, bf16[1024,128]{1,0:T(8,128)(2,1)S(1)}, bf16[1024,2048]{1,0:T(8,128)(2,1)}) custom-call(s32[2,9]{1,0:T(2,128)S(1)} %get-tuple-element.27.refs_0_, f32[1,9]{1,0:T(1,128)S(1)} %get-tuple-element.28.refs_1_, bf16[1024,2048]{1,0:T(8,128)(2,1)S(1)} %copy-done.1, ...), custom_call_target="tpu_custom_call" | custom-call | tf_op jit(solution)/shard_map/step/pallas_call | solution.py:229
  82.1 1.9 collective-permute-start.8
  84.1 11.6 %collective-permute-done.10.refs_3_ = bf16[1024,256]{1,0:T(8,128)(2,1)S(1)} collective-permute-done((bf16[1024,256]{1,0:T(8,128)(2,1)S(1)}, bf16[1024,256]{1,0:T(8,128)(2,1)S(1)}, u32[]{:S(2)}, u32[]{:S(2)}) %collective-permute-start.10) | collective-permute-done | bytes 524320 | tf_op jit(solution)/shard_map/ppermute | solution.py:253
  95.7 4.1 %step.13 = (f32[2,2,128,128]{3,2,1,0:T(8,128)S(1)}, bf16[1024,256]{1,0:T(8,128)(2,1)S(1)}, bf16[1024,2048]{1,0:T(8,128)(2,1)}) custom-call(s32[2,9]{1,0:T(2,128)S(1)} %get-tuple-element.27.refs_0_, f32[1,9]{1,0:T(1,128)S(1)} %get-tuple-element.28.refs_1_, bf16[1024,2048]{1,0:T(8,128)(2,1)S(1)} %copy-done.1, ...), custom_call_target="tpu_custom_call", output_to_operand_aliasing={{2}: (9, {})} | custom-call | tf_op jit(solution)/shard_map/step/pallas_call | solution.py:229
  99.8 1.9 collective-permute-start.19
  101.8 5.1 %collective-permute-done.2.refs_3_ = bf16[1024,128]{1,0:T(8,128)(2,1)S(1)} collective-permute-done((bf16[1024,128]{1,0:T(8,128)(2,1)S(1)}, bf16[1024,128]{1,0:T(8,128)(2,1)S(1)}, u32[]{:S(2)}, u32[]{:S(2)}) %collective-permute-start.2) | collective-permute-done | bytes 262176 | tf_op jit(solution)/shard_map/ppermute | solution.py:253
  106.9 3.3 %step.14 = (f32[1,2,128,128]{3,2,1,0:T(8,128)S(1)}, bf16[1024,256]{1,0:T(8,128)(2,1)S(1)}, bf16[1024,2048]{1,0:T(8,128)(2,1)}) custom-call(s32[2,9]{1,0:T(2,128)S(1)} %get-tuple-element.27.refs_0_, f32[1,9]{1,0:T(1,128)S(1)} %get-tuple-element.28.refs_1_, bf16[1024,2048]{1,0:T(8,128)(2,1)S(1)} %copy-done.1, ...), custom_call_target="tpu_custom_call", output_to_operand_aliasing={{2}: (9, {})} | custom-call | tf_op jit(solution)/shard_map/step/pallas_call | solution.py:229
  110.2 13.5 %collective-permute-done.21.refs_8_ = bf16[1024,128]{1,0:T(8,128)(2,1)S(1)} collective-permute-done((bf16[1024,128]{1,0:T(8,128)(2,1)S(1)}, bf16[1024,128]{1,0:T(8,128)(2,1)S(1)}, u32[]{:S(2)}, u32[]{:S(2)}) %collective-permute-start.21) | collective-permute-done | bytes 262176 | tf_op jit(solution)/shard_map/ppermute | solution.py:253
  123.8 2.9 %step.15 = (bf16[1024,256]{1,0:T(8,128)(2,1)S(1)}, bf16[1024,2048]{1,0:T(8,128)(2,1)}) custom-call(s32[2,9]{1,0:T(2,128)S(1)} %get-tuple-element.27.refs_0_, f32[1,9]{1,0:T(1,128)S(1)} %get-tuple-element.28.refs_1_, bf16[1024,2048]{1,0:T(8,128)(2,1)S(1)} %copy-done.1, ...), custom_call_target="tpu_custom_call", output_to_operand_aliasing={{1}: (9, {})} | custom-call | tf_op jit(solution)/shard_map/step/pallas_call | solution.py:229
  126.7 3.0 %collective-permute-start.23 = (bf16[1024,256]{1,0:T(8,128)(2,1)S(1)}, bf16[1024,256]{1,0:T(8,128)(2,1)S(1)}, u32[]{:S(2)}, u32[]{:S(2)}) collective-permute-start(bf16[1024,256]{1,0:T(8,128)(2,1)S(1)} %get-tuple-element.46), channel_id=1, source_target_pairs={{0,8},{4,12},{8,0},{12,4},{1,9},{5,13},{9,1},{13,5},{2,10},{6,14},... | collective-permute-start | bytes 1572872 | tf_op jit(solution)/shard_map/ppermute | solution.py:253
  129.7 1.8 collective-permute-start.15
  131.6 4.2 %collective-permute-done.15.refs_6_ = f32[1,2,128,128]{3,2,1,0:T(8,128)S(1)} collective-permute-done((f32[1,2,128,128]{3,2,1,0:T(8,128)S(1)}, f32[1,2,128,128]{3,2,1,0:T(8,128)S(1)}, u32[]{:S(2)}, u32[]{:S(2)}) %collective-permute-start.15) | collective-permute-done | bytes 131104 | tf_op jit(solution)/shard_map/ppermute | solution.py:250
  135.7 1.7 collective-permute-done.16.refs_7_
  137.4 20.1 %collective-permute-done.17.refs_8_ = bf16[1024,256]{1,0:T(8,128)(2,1)S(1)} collective-permute-done((bf16[1024,256]{1,0:T(8,128)(2,1)S(1)}, bf16[1024,256]{1,0:T(8,128)(2,1)S(1)}, u32[]{:S(2)}, u32[]{:S(2)}) %collective-permute-start.17) | collective-permute-done | bytes 524320 | tf_op jit(solution)/shard_map/ppermute | solution.py:253
  157.5 2.0 %step.16 = (bf16[1024,128]{1,0:T(8,128)(2,1)S(1)}, bf16[1024,2048]{1,0:T(8,128)(2,1)}) custom-call(s32[2,9]{1,0:T(2,128)S(1)} %get-tuple-element.27.refs_0_, f32[1,9]{1,0:T(1,128)S(1)} %get-tuple-element.28.refs_1_, bf16[1024,2048]{1,0:T(8,128)(2,1)S(1)} %copy-done.1, ...), custom_call_target="tpu_custom_call", output_to_operand_aliasing={{1}: (9, {})} | custom-call | tf_op jit(solution)/shard_map/step/pallas_call | solution.py:229
  159.6 14.7 %collective-permute-done.24.refs_3_ = bf16[1024,256]{1,0:T(8,128)(2,1)S(1)} collective-permute-done((bf16[1024,256]{1,0:T(8,128)(2,1)S(1)}, bf16[1024,256]{1,0:T(8,128)(2,1)S(1)}, u32[]{:S(2)}, u32[]{:S(2)}) %collective-permute-start.24) | collective-permute-done | bytes 524320 | tf_op jit(solution)/shard_map/ppermute | solution.py:253
  174.3 1.5 step.17.refs_4_
  175.8 9.7 %collective-permute-done.23.refs_3_ = bf16[1024,256]{1,0:T(8,128)(2,1)S(1)} collective-permute-done((bf16[1024,256]{1,0:T(8,128)(2,1)S(1)}, bf16[1024,256]{1,0:T(8,128)(2,1)S(1)}, u32[]{:S(2)}, u32[]{:S(2)}) %collective-permute-start.23) | collective-permute-done | bytes 524320 | tf_op jit(solution)/shard_map/ppermute | solution.py:253
  185.5 1.5 step.18.refs_4_
  187.0 3.3 %collective-permute-done.22.refs_3_ = bf16[1024,128]{1,0:T(8,128)(2,1)S(1)} collective-permute-done((bf16[1024,128]{1,0:T(8,128)(2,1)S(1)}, bf16[1024,128]{1,0:T(8,128)(2,1)S(1)}, u32[]{:S(2)}, u32[]{:S(2)}) %collective-permute-start.22) | collective-permute-done | bytes 262176 | tf_op jit(solution)/shard_map/ppermute | solution.py:253
  190.3 1.4 step.19
  (37 shorter events, 4.0 us)
Async XLA Ops:
  0.0 2.2 %copy-start = (bf16[1024,2048]{1,0:T(8,128)(2,1)S(1)}, bf16[1024,2048]{1,0:T(8,128)(2,1)}, u32[]{:S(2)}) copy-start(bf16[1024,2048]{1,0:T(8,128)(2,1)} %refs_2_.19) | copy-start | bytes 12582916
  2.2 0.7 copy-start.2
  2.9 0.7 copy-start.3
  3.5 52.8 %copy-start.1 = (bf16[1024,2048]{1,0:T(8,128)(2,1)S(1)}, bf16[1024,2048]{1,0:T(8,128)(2,1)}, u32[]{:S(2)}) copy-start(bf16[1024,2048]{1,0:T(8,128)(2,1)} %refs_2_.19) | copy-start | bytes 12582916
  5.8 54.0 %collective-permute-start = (bf16[1024,256]{1,0:T(8,128)(2,1)S(1)}, bf16[1024,256]{1,0:T(8,128)(2,1)S(1)}, u32[]{:S(2)}, u32[]{:S(2)}) collective-permute-start(bf16[1024,256]{1,0:T(8,128)(2,1)S(1)} %get-tuple-element.29), channel_id=1, source_target_pairs={{0,8},{4,12},{8,0},{12,4},{1,9},{5,13},{9,1},{13,5},{2,10},{6,14},... | collective-permute-start | bytes 1572872 | tf_op jit(solution)/shard_map/ppermute | solution.py:193
  9.9 46.5 %collective-permute-start.1 = (bf16[1024,128]{1,0:T(8,128)(2,1)S(1)}, bf16[1024,128]{1,0:T(8,128)(2,1)S(1)}, u32[]{:S(2)}, u32[]{:S(2)}) collective-permute-start(bf16[1024,128]{1,0:T(8,128)(2,1)S(1)} %get-tuple-element.30), channel_id=1, source_target_pairs={{0,8},{4,12},{8,0},{12,4},{1,9},{5,13},{9,1},{13,5},{2,10},{6,14},... | collective-permute-start | bytes 786440 | tf_op jit(solution)/shard_map/ppermute | solution.py:193
  10.0 68.8 %collective-permute-start.3 = (bf16[1024,256]{1,0:T(8,128)(2,1)S(1)}, bf16[1024,256]{1,0:T(8,128)(2,1)S(1)}, u32[]{:S(2)}, u32[]{:S(2)}) collective-permute-start(bf16[1024,256]{1,0:T(8,128)(2,1)S(1)} %get-tuple-element.33), channel_id=1, source_target_pairs={{0,8},{4,12},{8,0},{12,4},{1,9},{5,13},{9,1},{13,5},{2,10},{6,14},... | collective-permute-start | bytes 1572872 | tf_op jit(solution)/shard_map/ppermute | solution.py:193
  57.7 4.0 %collective-permute-start.4 = (f32[1,2,128,128]{3,2,1,0:T(8,128)S(1)}, f32[1,2,128,128]{3,2,1,0:T(8,128)S(1)}, u32[]{:S(2)}, u32[]{:S(2)}) collective-permute-start(f32[1,2,128,128]{3,2,1,0:T(8,128)S(1)} %get-tuple-element.31.refs_4_.refs_5_), channel_id=1, source_target_pairs={{0,1},{1,0},{2,3},{3,2},{4,5},{5,4},{6,7},{7,6},{8,9},{9,8},{10,11... | collective-permute-start | bytes 393224 | tf_op jit(solution)/shard_map/ppermute | solution.py:250
  57.8 6.4 %collective-permute-start.5 = (f32[1,2,128,128]{3,2,1,0:T(8,128)S(1)}, f32[1,2,128,128]{3,2,1,0:T(8,128)S(1)}, u32[]{:S(2)}, u32[]{:S(2)}) collective-permute-start(f32[1,2,128,128]{3,2,1,0:T(8,128)S(1)} %get-tuple-element.31.refs_4_.refs_5_), channel_id=1, source_target_pairs={{0,2},{1,3},{2,0},{3,1},{4,6},{5,7},{6,4},{7,5},{8,10},{9,11},{10,... | collective-permute-start | bytes 393224 | tf_op jit(solution)/shard_map/ppermute | solution.py:250
  59.7 6.6 %collective-permute-start.6 = (f32[1,2,128,128]{3,2,1,0:T(8,128)S(1)}, f32[1,2,128,128]{3,2,1,0:T(8,128)S(1)}, u32[]{:S(2)}, u32[]{:S(2)}) collective-permute-start(f32[1,2,128,128]{3,2,1,0:T(8,128)S(1)} %get-tuple-element.31.refs_4_.refs_5_), channel_id=1, source_target_pairs={{0,3},{1,2},{2,1},{3,0},{4,7},{5,6},{6,5},{7,4},{8,11},{9,10},{10,... | collective-permute-start | bytes 393224 | tf_op jit(solution)/shard_map/ppermute | solution.py:250
  59.7 35.9 %collective-permute-start.10 = (bf16[1024,256]{1,0:T(8,128)(2,1)S(1)}, bf16[1024,256]{1,0:T(8,128)(2,1)S(1)}, u32[]{:S(2)}, u32[]{:S(2)}) collective-permute-start(bf16[1024,256]{1,0:T(8,128)(2,1)S(1)} %get-tuple-element.36), channel_id=1, source_target_pairs={{0,8},{4,12},{8,0},{12,4},{1,9},{5,13},{9,1},{13,5},{2,10},{6,14},... | collective-permute-start | bytes 1572872 | tf_op jit(solution)/shard_map/ppermute | solution.py:253
  61.7 20.4 %collective-permute-start.11 = (f32[2,2,128,128]{3,2,1,0:T(8,128)S(1)}, f32[2,2,128,128]{3,2,1,0:T(8,128)S(1)}, u32[]{:S(2)}, u32[]{:S(2)}) collective-permute-start(f32[2,2,128,128]{3,2,1,0:T(8,128)S(1)} %get-tuple-element.34.refs_9_.refs_5_), channel_id=1, source_target_pairs={{0,1},{1,0},{2,3},{3,2},{4,5},{5,4},{6,7},{7,6},{8,9},{9,8},{10,11... | collective-permute-start | bytes 786440 | tf_op jit(solution)/shard_map/ppermute | solution.py:250
  64.1 19.9 %collective-permute-start.12 = (f32[2,2,128,128]{3,2,1,0:T(8,128)S(1)}, f32[2,2,128,128]{3,2,1,0:T(8,128)S(1)}, u32[]{:S(2)}, u32[]{:S(2)}) collective-permute-start(f32[2,2,128,128]{3,2,1,0:T(8,128)S(1)} %get-tuple-element.34.refs_9_.refs_5_), channel_id=1, source_target_pairs={{0,2},{1,3},{2,0},{3,1},{4,6},{5,7},{6,4},{7,5},{8,10},{9,11},{10,... | collective-permute-start | bytes 786440 | tf_op jit(solution)/shard_map/ppermute | solution.py:250
  66.3 17.8 %collective-permute-start.13 = (f32[2,2,128,128]{3,2,1,0:T(8,128)S(1)}, f32[2,2,128,128]{3,2,1,0:T(8,128)S(1)}, u32[]{:S(2)}, u32[]{:S(2)}) collective-permute-start(f32[2,2,128,128]{3,2,1,0:T(8,128)S(1)} %get-tuple-element.34.refs_9_.refs_5_), channel_id=1, source_target_pairs={{0,3},{1,2},{2,1},{3,0},{4,7},{5,6},{6,5},{7,4},{8,11},{9,10},{10,... | collective-permute-start | bytes 786440 | tf_op jit(solution)/shard_map/ppermute | solution.py:250
  82.0 17.8 %collective-permute-start.7 = (f32[2,2,128,128]{3,2,1,0:T(8,128)S(1)}, f32[2,2,128,128]{3,2,1,0:T(8,128)S(1)}, u32[]{:S(2)}, u32[]{:S(2)}) collective-permute-start(f32[2,2,128,128]{3,2,1,0:T(8,128)S(1)} %get-tuple-element.35.refs_5_), channel_id=1, source_target_pairs={{0,1},{1,0},{2,3},{3,2},{4,5},{5,4},{6,7},{7,6},{8,9},{9,8},{10,11... | collective-permute-start | bytes 786440 | tf_op jit(solution)/shard_map/ppermute | solution.py:250
  82.1 17.8 %collective-permute-start.8 = (f32[2,2,128,128]{3,2,1,0:T(8,128)S(1)}, f32[2,2,128,128]{3,2,1,0:T(8,128)S(1)}, u32[]{:S(2)}, u32[]{:S(2)}) collective-permute-start(f32[2,2,128,128]{3,2,1,0:T(8,128)S(1)} %get-tuple-element.35.refs_5_), channel_id=1, source_target_pairs={{0,2},{1,3},{2,0},{3,1},{4,6},{5,7},{6,4},{7,5},{8,10},{9,11},{10,... | collective-permute-start | bytes 786440 | tf_op jit(solution)/shard_map/ppermute | solution.py:250
  84.0 17.8 %collective-permute-start.9 = (f32[2,2,128,128]{3,2,1,0:T(8,128)S(1)}, f32[2,2,128,128]{3,2,1,0:T(8,128)S(1)}, u32[]{:S(2)}, u32[]{:S(2)}) collective-permute-start(f32[2,2,128,128]{3,2,1,0:T(8,128)S(1)} %get-tuple-element.35.refs_5_), channel_id=1, source_target_pairs={{0,3},{1,2},{2,1},{3,0},{4,7},{5,6},{6,5},{7,4},{8,11},{9,10},{10,... | collective-permute-start | bytes 786440 | tf_op jit(solution)/shard_map/ppermute | solution.py:250
  84.1 22.8 %collective-permute-start.2 = (bf16[1024,128]{1,0:T(8,128)(2,1)S(1)}, bf16[1024,128]{1,0:T(8,128)(2,1)S(1)}, u32[]{:S(2)}, u32[]{:S(2)}) collective-permute-start(bf16[1024,128]{1,0:T(8,128)(2,1)S(1)} %get-tuple-element.32), channel_id=1, source_target_pairs={{0,8},{4,12},{8,0},{12,4},{1,9},{5,13},{9,1},{13,5},{2,10},{6,14},... | collective-permute-start | bytes 786440 | tf_op jit(solution)/shard_map/ppermute | solution.py:253
  95.7 28.1 %collective-permute-start.21 = (bf16[1024,128]{1,0:T(8,128)(2,1)S(1)}, bf16[1024,128]{1,0:T(8,128)(2,1)S(1)}, u32[]{:S(2)}, u32[]{:S(2)}) collective-permute-start(bf16[1024,128]{1,0:T(8,128)(2,1)S(1)} %get-tuple-element.42), channel_id=1, source_target_pairs={{0,8},{4,12},{8,0},{12,4},{1,9},{5,13},{9,1},{13,5},{2,10},{6,14},... | collective-permute-start | bytes 786440 | tf_op jit(solution)/shard_map/ppermute | solution.py:253
  99.7 24.0 %collective-permute-start.18 = (f32[2,2,128,128]{3,2,1,0:T(8,128)S(1)}, f32[2,2,128,128]{3,2,1,0:T(8,128)S(1)}, u32[]{:S(2)}, u32[]{:S(2)}) collective-permute-start(f32[2,2,128,128]{3,2,1,0:T(8,128)S(1)} %get-tuple-element.41.refs_4_), channel_id=1, source_target_pairs={{0,1},{1,0},{2,3},{3,2},{4,5},{5,4},{6,7},{7,6},{8,9},{9,8},{10,11... | collective-permute-start | bytes 786440 | tf_op jit(solution)/shard_map/ppermute | solution.py:250
  99.8 23.9 %collective-permute-start.19 = (f32[2,2,128,128]{3,2,1,0:T(8,128)S(1)}, f32[2,2,128,128]{3,2,1,0:T(8,128)S(1)}, u32[]{:S(2)}, u32[]{:S(2)}) collective-permute-start(f32[2,2,128,128]{3,2,1,0:T(8,128)S(1)} %get-tuple-element.41.refs_4_), channel_id=1, source_target_pairs={{0,2},{1,3},{2,0},{3,1},{4,6},{5,7},{6,4},{7,5},{8,10},{9,11},{10,... | collective-permute-start | bytes 786440 | tf_op jit(solution)/shard_map/ppermute | solution.py:250
  101.7 22.0 %collective-permute-start.20 = (f32[2,2,128,128]{3,2,1,0:T(8,128)S(1)}, f32[2,2,128,128]{3,2,1,0:T(8,128)S(1)}, u32[]{:S(2)}, u32[]{:S(2)}) collective-permute-start(f32[2,2,128,128]{3,2,1,0:T(8,128)S(1)} %get-tuple-element.41.refs_4_), channel_id=1, source_target_pairs={{0,3},{1,2},{2,1},{3,0},{4,7},{5,6},{6,5},{7,4},{8,11},{9,10},{10,... | collective-permute-start | bytes 786440 | tf_op jit(solution)/shard_map/ppermute | solution.py:250
  106.9 50.6 %collective-permute-start.17 = (bf16[1024,256]{1,0:T(8,128)(2,1)S(1)}, bf16[1024,256]{1,0:T(8,128)(2,1)S(1)}, u32[]{:S(2)}, u32[]{:S(2)}) collective-permute-start(bf16[1024,256]{1,0:T(8,128)(2,1)S(1)} %get-tuple-element.40), channel_id=1, source_target_pairs={{0,8},{4,12},{8,0},{12,4},{1,9},{5,13},{9,1},{13,5},{2,10},{6,14},... | collective-permute-start | bytes 1572872 | tf_op jit(solution)/shard_map/ppermute | solution.py:253
  123.8 7.8 %collective-permute-start.14 = (f32[1,2,128,128]{3,2,1,0:T(8,128)S(1)}, f32[1,2,128,128]{3,2,1,0:T(8,128)S(1)}, u32[]{:S(2)}, u32[]{:S(2)}) collective-permute-start(f32[1,2,128,128]{3,2,1,0:T(8,128)S(1)} %get-tuple-element.39.refs_4_), channel_id=1, source_target_pairs={{0,1},{1,0},{2,3},{3,2},{4,5},{5,4},{6,7},{7,6},{8,9},{9,8},{10,11... | collective-permute-start | bytes 393224 | tf_op jit(solution)/shard_map/ppermute | solution.py:250
  123.8 50.6 %collective-permute-start.24 = (bf16[1024,256]{1,0:T(8,128)(2,1)S(1)}, bf16[1024,256]{1,0:T(8,128)(2,1)S(1)}, u32[]{:S(2)}, u32[]{:S(2)}) collective-permute-start(bf16[1024,256]{1,0:T(8,128)(2,1)S(1)} %get-tuple-element.47), channel_id=1, source_target_pairs={{0,8},{4,12},{8,0},{12,4},{1,9},{5,13},{9,1},{13,5},{2,10},{6,14},... | collective-permute-start | bytes 1572872 | tf_op jit(solution)/shard_map/ppermute | solution.py:253
  126.7 58.8 %collective-permute-start.23 = (bf16[1024,256]{1,0:T(8,128)(2,1)S(1)}, bf16[1024,256]{1,0:T(8,128)(2,1)S(1)}, u32[]{:S(2)}, u32[]{:S(2)}) collective-permute-start(bf16[1024,256]{1,0:T(8,128)(2,1)S(1)} %get-tuple-element.46), channel_id=1, source_target_pairs={{0,8},{4,12},{8,0},{12,4},{1,9},{5,13},{9,1},{13,5},{2,10},{6,14},... | collective-permute-start | bytes 1572872 | tf_op jit(solution)/shard_map/ppermute | solution.py:253
  129.7 6.0 %collective-permute-start.15 = (f32[1,2,128,128]{3,2,1,0:T(8,128)S(1)}, f32[1,2,128,128]{3,2,1,0:T(8,128)S(1)}, u32[]{:S(2)}, u32[]{:S(2)}) collective-permute-start(f32[1,2,128,128]{3,2,1,0:T(8,128)S(1)} %get-tuple-element.39.refs_4_), channel_id=1, source_target_pairs={{0,2},{1,3},{2,0},{3,1},{4,6},{5,7},{6,4},{7,5},{8,10},{9,11},{10,... | collective-permute-start | bytes 393224 | tf_op jit(solution)/shard_map/ppermute | solution.py:250
  131.5 5.8 %collective-permute-start.16 = (f32[1,2,128,128]{3,2,1,0:T(8,128)S(1)}, f32[1,2,128,128]{3,2,1,0:T(8,128)S(1)}, u32[]{:S(2)}, u32[]{:S(2)}) collective-permute-start(f32[1,2,128,128]{3,2,1,0:T(8,128)S(1)} %get-tuple-element.39.refs_4_), channel_id=1, source_target_pairs={{0,3},{1,2},{2,1},{3,0},{4,7},{5,6},{6,5},{7,4},{8,11},{9,10},{10,... | collective-permute-start | bytes 393224 | tf_op jit(solution)/shard_map/ppermute | solution.py:250
  159.5 30.9 %collective-permute-start.22 = (bf16[1024,128]{1,0:T(8,128)(2,1)S(1)}, bf16[1024,128]{1,0:T(8,128)(2,1)S(1)}, u32[]{:S(2)}, u32[]{:S(2)}) collective-permute-start(bf16[1024,128]{1,0:T(8,128)(2,1)S(1)} %get-tuple-element.45), channel_id=1, source_target_pairs={{0,8},{4,12},{8,0},{12,4},{1,9},{5,13},{9,1},{13,5},{2,10},{6,14},... | collective-permute-start | bytes 786440 | tf_op jit(solution)/shard_map/ppermute | solution.py:253

commit v3 on v2

--- a/solution.py
+++ b/solution.py
@@ -9,8 +9,8 @@
 
 BLOCK = 128
 STRETCH = 256
-CHUNKS = (1,2,2,2,1,)
-LAG = 3
+CHUNKS = (2,2,2,2,)
+LAG = 2
 
 ANY = pl.BlockSpec(memory_space=pl.ANY)
 HBM = pl.BlockSpec(memory_space=pltpu.HBM)
@@ -41,20 +41,37 @@
     lax.fori_loop(0, blocks_ref.shape[1], one, (jnp.int32(0), jnp.int32(0)))
 
 
-def opening_kernel(per_dev, starts, sizes, blocks_ref, weight_ref, decoder_ref, place_ref, scale_ref, *rest):
-    outs, sem = rest[:-1], rest[-1]
-    plan(per_dev, blocks_ref, weight_ref, place_ref, scale_ref)
+def gather(decoder_ref, blocks, outs, sizes, sem):
     copies = []
-    for start, size, out in zip(starts, sizes, outs):
+    for size, out in zip(sizes, outs):
         for j in range(size):
             copies.append(
                 pltpu.make_async_copy(
-                    column(decoder_ref, place_ref[1, start + j]), column(out, j), sem.at[len(copies)]
+                    column(decoder_ref, blocks[len(copies)]), column(out, j), sem.at[len(copies)]
                 )
             )
             copies[-1].start()
     for copy in copies:
         copy.wait()
+
+
+def opening_kernel(per_dev, sizes, blocks_ref, decoder_ref, out_ref, held_ref, sem):
+    me = lax.axis_index("outer")
+    fetch = pltpu.make_async_copy(blocks_ref, held_ref, sem.at[0])
+    fetch.start()
+    fetch.wait()
+    blocks, c = [], jnp.int32(0)
+    for _ in range(sizes[0]):
+        c = lax.while_loop(lambda c: lax.div(held_ref[1, c], per_dev) != me, lambda c: c + 1, c)
+        blocks.append(lax.rem(held_ref[1, c], per_dev))
+        c += 1
+    gather(decoder_ref, blocks, [out_ref], sizes, sem)
+
+
+def planning_kernel(per_dev, start, sizes, blocks_ref, weight_ref, decoder_ref, first_ref, place_ref, scale_ref, *rest):
+    outs, sem = rest[:-1], rest[-1]
+    plan(per_dev, blocks_ref, weight_ref, place_ref, scale_ref)
+    gather(decoder_ref, [place_ref[1, start + j] for j in range(sum(sizes))], outs, sizes, sem)
 
 
 def gram_parts(x):
@@ -176,21 +193,32 @@
     to_first = [(o, (o + stride) % owners) for o in range(owners)]
     to_second = [(o, (o - stride) % owners) for o in range(owners)]
 
+    stay = lambda x: pltpu.with_memory_space_constraint(x, pltpu.HBM)
+    pairs, decoder = stay(stretch_blocks.T), stay(decoder)
+    first = pl.pallas_call(
+        functools.partial(opening_kernel, per_dev, sizes[:1]),
+        out_shape=array(0),
+        in_specs=[HBM, HBM],
+        out_specs=ANY,
+        scratch_shapes=[pltpu.SMEM(pairs.shape, jnp.int32), pltpu.SemaphoreType.DMA((sizes[0],))],
+        compiler_params=pltpu.CompilerParams(vmem_limit_bytes=8 * 2**20),
+        name="opening",
+    )(pairs, decoder)
     place, scale, *raw = pl.pallas_call(
-        functools.partial(opening_kernel, per_dev, starts[:LAG], sizes[:LAG]),
+        functools.partial(planning_kernel, per_dev, starts[1], sizes[1:LAG]),
         out_shape=[
             jax.ShapeDtypeStruct((2, half + 1), jnp.int32),
             jax.ShapeDtypeStruct((1, half + 1), jnp.float32),
         ]
-        + [array(k) for k in range(LAG)],
-        in_specs=[SMEM, SMEM, ANY],
-        out_specs=[SMEM, SMEM] + [ANY] * LAG,
+        + [array(k) for k in range(1, LAG)],
+        in_specs=[SMEM, SMEM, HBM, ANY],
+        out_specs=[SMEM, SMEM] + [ANY] * (LAG - 1),
         scratch_shapes=[pltpu.SemaphoreType.DMA((per_dev,))],
         compiler_params=pltpu.CompilerParams(vmem_limit_bytes=8 * 2**20),
-        name="opening",
-    )(stretch_blocks.T, stretch_weight, decoder)
-
-    sends = [lax.ppermute(part, "outer", to_first) for part in raw]
+        name="planning",
+    )(stretch_blocks.T, stretch_weight, decoder, first)
+
+    sends = [lax.ppermute(part, "outer", to_first) for part in [first] + raw]
     parts = {}
     out = chain = None
     for step in range(2 * count):

time: 192 us -> 188 us (0.979)
  starting transfers between devices: 22.5 us -> 13.3 us
  waiting for transfers between devices: 140 us -> 145 us
  Pallas kernels: 25.3 us -> 29.4 us
  local copies, waits for them, and re-layouts: 3.52 us -> 0.01 us
    ppermute x7 -> x6, waiting for transfers between devices: 78 us -> 95.2 us  [shards(): lax.ppermute(results.pop(0), 'outer', to_second if final else to_first)]
    ppermute x15 -> x12, waiting for transfers between devices: 8.34 us -> 0.03 us  [shards(): lax.ppermute(mine, 'inner', [(i, i ^ hop) for i in range(ranks)])]
    ppermute x3 -> x2, waiting for transfers between devices: 53.8 us -> 49.8 us  [shards(): sends = [lax.ppermute(part, 'outer', to_first) for part in [first] + raw]]
    ppermute x15 -> x12, starting transfers between devices: 12.4 us -> 8.8 us  [shards(): lax.ppermute(mine, 'inner', [(i, i ^ hop) for i in range(ranks)])]
    unnamed x8 -> x4, local copies, waits for them, and re-layouts: 3.52 us -> 0.01 us
    ppermute x3 -> x2, starting transfers between devices: 7.02 us -> 4.09 us  [shards(): sends = [lax.ppermute(part, 'outer', to_first) for part in [first] + raw]]
    pallas_call x1 -> x2, Pallas kernels: 2.25 us -> 4.92 us  [the longest x1 2.91 us: shards(): pl.pallas_call(functools.partial(planning_kernel, per_dev, starts[1], siz...]
    ppermute x7 -> x6, starting transfers between devices: 3.05 us -> 0.43 us  [shards(): lax.ppermute(results.pop(0), 'outer', to_second if final else to_first)]
  transfers between devices with their start and end apart: 25 -> 20, of which waited for: 13 -> 8; matrix products, arithmetic and copies ran while one was open for 0% -> 0% of each run, Pallas kernels for 11% -> 14%
where the time goes in v3:
time: 188 us
  waiting for transfers between devices  145 us (77%)
  Pallas kernels  29.4 us (16%)
  starting transfers between devices  13.3 us (7%)
    ppermute x6, waiting for transfers between devices, shards(): lax.ppermute(results.pop(0), 'outer', to_second if final else to_first)  95.2 us
    ppermute x2, waiting for transfers between devices, shards(): sends = [lax.ppermute(part, 'outer', to_first) for part in [first] + raw]  49.8 us
    pallas_call x8, Pallas kernels, shards(): pl.pallas_call(functools.partial(step_kernel, spec), out_shape=shapes, in...  24.4 us
    ppermute x12, starting transfers between devices, shards(): lax.ppermute(mine, 'inner', [(i, i ^ hop) for i in range(ranks)])  8.8 us
    ppermute x2, starting transfers between devices, shards(): sends = [lax.ppermute(part, 'outer', to_first) for part in [first] + raw]  4.09 us
  transfers between devices with their start and end apart: 20, of which 8 were waited for; matrix products, arithmetic and copies ran while one was open for 0% of the time, Pallas kernels for 14%

profile of v3, /device:TPU:0, one launch (start us, length us, event | category | flops | bytes accessed | tf_op | source)
XLA Modules:
  0.0 188.0 jit_solution(14781081862600854126)
XLA Ops:
  0.0 2.0 %opening.1.first_ref = bf16[1024,256]{1,0:T(8,128)(2,1)S(1)} custom-call(s32[2,32]{1,0:T(2,128)} %bitcast.1, bf16[1024,2048]{1,0:T(8,128)(2,1)} %refs_2_.15), custom_call_target="tpu_custom_call" | custom-call | tf_op jit(solution)/shard_map/opening/pallas_call | solution.py:198
  2.0 4.0 %collective-permute-start.1 = (bf16[1024,256]{1,0:T(8,128)(2,1)S(1)}, bf16[1024,256]{1,0:T(8,128)(2,1)S(1)}, u32[]{:S(2)}, u32[]{:S(2)}) collective-permute-start(bf16[1024,256]{1,0:T(8,128)(2,1)S(1)} %opening.1.first_ref), channel_id=1, source_target_pairs={{0,8},{4,12},{8,0},{12,4},{1,9},{5,13},{9,1},{13,5},{2,10},{6,14},... | collective-permute-start | bytes 1572872 | tf_op jit(solution)/shard_map/ppermute | solution.py:221
  6.0 2.9 %planning.1 = (s32[2,9]{1,0:T(2,128)S(1)}, f32[1,9]{1,0:T(1,128)S(1)}, bf16[1024,256]{1,0:T(8,128)(2,1)S(1)}) custom-call(s32[2,32]{1,0:T(2,128)S(1)} %bitcast.2, f32[32]{0:T(128)S(1)} %copy-done.1, bf16[1024,2048]{1,0:T(8,128)(2,1)} %refs_2_.15, bf16[1024,256]{1,0:T(8,128)(2,1)S(1)} %opening.1.first_ref), custom_call_target="tpu_custom_call" | custom-call | tf_op jit(solution)/shard_map/planning/pallas_call | solution.py:207
  8.9 0.1 collective-permute-start
  9.0 32.2 %collective-permute-done.1.refs_3_.refs_4_ = bf16[1024,256]{1,0:T(8,128)(2,1)S(1)} collective-permute-done((bf16[1024,256]{1,0:T(8,128)(2,1)S(1)}, bf16[1024,256]{1,0:T(8,128)(2,1)S(1)}, u32[]{:S(2)}, u32[]{:S(2)}) %collective-permute-start.1) | collective-permute-done | bytes 524320 | tf_op jit(solution)/shard_map/ppermute | solution.py:221
  41.2 2.6 %step.8 = (f32[2,2,128,128]{3,2,1,0:T(8,128)S(1)}, bf16[1024,256]{1,0:T(8,128)(2,1)S(1)}) custom-call(s32[2,9]{1,0:T(2,128)S(1)} %get-tuple-element.22.refs_0_, f32[1,9]{1,0:T(1,128)S(1)} %get-tuple-element.23.refs_1_, bf16[1024,2048]{1,0:T(8,128)(2,1)} %refs_2_.15, bf16[1024,256]{1,0:T(8,128)(2,1)S(1)} %collective-permute-done.1.refs_3_.refs_4_), custom_call_target="tpu_custom_call" | custom-call | tf_op jit(solution)/shard_map/step/pallas_call | solution.py:257
  43.9 0.1 collective-permute-start.6
  44.0 0.1 collective-permute-start.7
  44.0 2.0 %collective-permute-start.8 = (f32[2,2,128,128]{3,2,1,0:T(8,128)S(1)}, f32[2,2,128,128]{3,2,1,0:T(8,128)S(1)}, u32[]{:S(2)}, u32[]{:S(2)}) collective-permute-start(f32[2,2,128,128]{3,2,1,0:T(8,128)S(1)} %get-tuple-element.25.refs_4_.refs_5_), channel_id=1, source_target_pairs={{0,2},{1,3},{2,0},{3,1},{4,6},{5,7},{6,4},{7,5},{8,10},{9,11},{10,... | collective-permute-start | bytes 786440 | tf_op jit(solution)/shard_map/ppermute | solution.py:278
  46.1 17.6 %collective-permute-done.refs_3_.refs_4_ = bf16[1024,256]{1,0:T(8,128)(2,1)S(1)} collective-permute-done((bf16[1024,256]{1,0:T(8,128)(2,1)S(1)}, bf16[1024,256]{1,0:T(8,128)(2,1)S(1)}, u32[]{:S(2)}, u32[]{:S(2)}) %collective-permute-start) | collective-permute-done | bytes 524320 | tf_op jit(solution)/shard_map/ppermute | solution.py:221
  63.7 2.6 %step.9 = (f32[2,2,128,128]{3,2,1,0:T(8,128)S(1)}, bf16[1024,256]{1,0:T(8,128)(2,1)S(1)}) custom-call(s32[2,9]{1,0:T(2,128)S(1)} %get-tuple-element.22.refs_0_, f32[1,9]{1,0:T(1,128)S(1)} %get-tuple-element.23.refs_1_, bf16[1024,2048]{1,0:T(8,128)(2,1)} %refs_2_.15, bf16[1024,256]{1,0:T(8,128)(2,1)S(1)} %collective-permute-done.refs_3_.refs_4_, ...), custom_call_target="tpu_custom_call" | custom-call | tf_op jit(solution)/shard_map/step/pallas_call | solution.py:257
  66.4 0.1 collective-permute-start.3
  66.5 2.0 %collective-permute-start.4 = (f32[2,2,128,128]{3,2,1,0:T(8,128)S(1)}, f32[2,2,128,128]{3,2,1,0:T(8,128)S(1)}, u32[]{:S(2)}, u32[]{:S(2)}) collective-permute-start(f32[2,2,128,128]{3,2,1,0:T(8,128)S(1)} %get-tuple-element.27.refs_9_.refs_5_), channel_id=1, source_target_pairs={{0,2},{1,3},{2,0},{3,1},{4,6},{5,7},{6,4},{7,5},{8,10},{9,11},{10,... | collective-permute-start | bytes 786440 | tf_op jit(solution)/shard_map/ppermute | solution.py:278
  68.5 0.1 collective-permute-start.5
  68.7 17.5 %collective-permute-done.6.refs_3_ = bf16[1024,256]{1,0:T(8,128)(2,1)S(1)} collective-permute-done((bf16[1024,256]{1,0:T(8,128)(2,1)S(1)}, bf16[1024,256]{1,0:T(8,128)(2,1)S(1)}, u32[]{:S(2)}, u32[]{:S(2)}) %collective-permute-start.6) | collective-permute-done | bytes 524320 | tf_op jit(solution)/shard_map/ppermute | solution.py:281
  86.2 4.5 %step.10 = (f32[2,2,128,128]{3,2,1,0:T(8,128)S(1)}, bf16[1024,256]{1,0:T(8,128)(2,1)S(1)}, bf16[1024,2048]{1,0:T(8,128)(2,1)}) custom-call(s32[2,9]{1,0:T(2,128)S(1)} %get-tuple-element.22.refs_0_, f32[1,9]{1,0:T(1,128)S(1)} %get-tuple-element.23.refs_1_, bf16[1024,2048]{1,0:T(8,128)(2,1)} %refs_2_.15, bf16[1024,256]{1,0:T(8,128)(2,1)S(1)} %collective-permute-done.6.refs_3_, ...), custom_call_target="tpu_custom_call" | custom-call | tf_op jit(solution)/shard_map/step/pallas_call | solution.py:257
  90.7 0.1 collective-permute-start.17
  90.9 2.0 %collective-permute-start.15 = (f32[2,2,128,128]{3,2,1,0:T(8,128)S(1)}, f32[2,2,128,128]{3,2,1,0:T(8,128)S(1)}, u32[]{:S(2)}, u32[]{:S(2)}) collective-permute-start(f32[2,2,128,128]{3,2,1,0:T(8,128)S(1)} %get-tuple-element.32.refs_4_), channel_id=1, source_target_pairs={{0,2},{1,3},{2,0},{3,1},{4,6},{5,7},{6,4},{7,5},{8,10},{9,11},{10,... | collective-permute-start | bytes 786440 | tf_op jit(solution)/shard_map/ppermute | solution.py:278
  92.9 0.1 collective-permute-start.16
  93.0 15.6 %collective-permute-done.2.refs_3_ = bf16[1024,256]{1,0:T(8,128)(2,1)S(1)} collective-permute-done((bf16[1024,256]{1,0:T(8,128)(2,1)S(1)}, bf16[1024,256]{1,0:T(8,128)(2,1)S(1)}, u32[]{:S(2)}, u32[]{:S(2)}) %collective-permute-start.2) | collective-permute-done | bytes 524320 | tf_op jit(solution)/shard_map/ppermute | solution.py:281
  108.7 4.5 %step.11 = (f32[2,2,128,128]{3,2,1,0:T(8,128)S(1)}, bf16[1024,256]{1,0:T(8,128)(2,1)S(1)}, bf16[1024,2048]{1,0:T(8,128)(2,1)}) custom-call(s32[2,9]{1,0:T(2,128)S(1)} %get-tuple-element.22.refs_0_, f32[1,9]{1,0:T(1,128)S(1)} %get-tuple-element.23.refs_1_, bf16[1024,2048]{1,0:T(8,128)(2,1)} %refs_2_.15, ...), custom_call_target="tpu_custom_call", output_to_operand_aliasing={{2}: (9, {})} | custom-call | tf_op jit(solution)/shard_map/step/pallas_call | solution.py:257
  113.2 0.1 collective-permute-start.13
  113.3 2.0 %collective-permute-start.11 = (f32[2,2,128,128]{3,2,1,0:T(8,128)S(1)}, f32[2,2,128,128]{3,2,1,0:T(8,128)S(1)}, u32[]{:S(2)}, u32[]{:S(2)}) collective-permute-start(f32[2,2,128,128]{3,2,1,0:T(8,128)S(1)} %get-tuple-element.30.refs_4_), channel_id=1, source_target_pairs={{0,2},{1,3},{2,0},{3,1},{4,6},{5,7},{6,4},{7,5},{8,10},{9,11},{10,... | collective-permute-start | bytes 786440 | tf_op jit(solution)/shard_map/ppermute | solution.py:278
  115.4 0.1 collective-permute-start.12
  115.5 15.6 %collective-permute-done.17.refs_8_ = bf16[1024,256]{1,0:T(8,128)(2,1)S(1)} collective-permute-done((bf16[1024,256]{1,0:T(8,128)(2,1)S(1)}, bf16[1024,256]{1,0:T(8,128)(2,1)S(1)}, u32[]{:S(2)}, u32[]{:S(2)}) %collective-permute-start.17) | collective-permute-done | bytes 524320 | tf_op jit(solution)/shard_map/ppermute | solution.py:281
  131.1 3.6 %step.12 = (bf16[1024,256]{1,0:T(8,128)(2,1)S(1)}, bf16[1024,2048]{1,0:T(8,128)(2,1)}) custom-call(s32[2,9]{1,0:T(2,128)S(1)} %get-tuple-element.22.refs_0_, f32[1,9]{1,0:T(1,128)S(1)} %get-tuple-element.23.refs_1_, bf16[1024,2048]{1,0:T(8,128)(2,1)} %refs_2_.15, ...), custom_call_target="tpu_custom_call", output_to_operand_aliasing={{1}: (9, {})} | custom-call | tf_op jit(solution)/shard_map/step/pallas_call | solution.py:257
  134.9 18.7 %collective-permute-done.13.refs_8_ = bf16[1024,256]{1,0:T(8,128)(2,1)S(1)} collective-permute-done((bf16[1024,256]{1,0:T(8,128)(2,1)S(1)}, bf16[1024,256]{1,0:T(8,128)(2,1)S(1)}, u32[]{:S(2)}, u32[]{:S(2)}) %collective-permute-start.13) | collective-permute-done | bytes 524320 | tf_op jit(solution)/shard_map/ppermute | solution.py:281
  153.6 3.6 %step.13 = (bf16[1024,256]{1,0:T(8,128)(2,1)S(1)}, bf16[1024,2048]{1,0:T(8,128)(2,1)}) custom-call(s32[2,9]{1,0:T(2,128)S(1)} %get-tuple-element.22.refs_0_, f32[1,9]{1,0:T(1,128)S(1)} %get-tuple-element.23.refs_1_, bf16[1024,2048]{1,0:T(8,128)(2,1)} %refs_2_.15, ...), custom_call_target="tpu_custom_call", output_to_operand_aliasing={{1}: (9, {})} | custom-call | tf_op jit(solution)/shard_map/step/pallas_call | solution.py:257
  157.3 18.8 %collective-permute-done.19.refs_3_ = bf16[1024,256]{1,0:T(8,128)(2,1)S(1)} collective-permute-done((bf16[1024,256]{1,0:T(8,128)(2,1)S(1)}, bf16[1024,256]{1,0:T(8,128)(2,1)S(1)}, u32[]{:S(2)}, u32[]{:S(2)}) %collective-permute-start.19) | collective-permute-done | bytes 524320 | tf_op jit(solution)/shard_map/ppermute | solution.py:281
  176.1 1.5 step.14.refs_4_
  177.6 8.9 %collective-permute-done.18.refs_3_ = bf16[1024,256]{1,0:T(8,128)(2,1)S(1)} collective-permute-done((bf16[1024,256]{1,0:T(8,128)(2,1)S(1)}, bf16[1024,256]{1,0:T(8,128)(2,1)S(1)}, u32[]{:S(2)}, u32[]{:S(2)}) %collective-permute-start.18) | collective-permute-done | bytes 524320 | tf_op jit(solution)/shard_map/ppermute | solution.py:281
  186.5 1.5 step.15
  (22 shorter events, 0.5 us)
Async XLA Ops:
  0.0 6.0 %copy-start = (s32[32,2]{0,1:T(2,128)S(1)}, s32[32,2]{0,1:T(2,128)}, u32[]{:S(2)}) copy-start(s32[32,2]{0,1:T(2,128)} %param.4) | copy-start | bytes 772
  0.0 6.0 %copy-start.1 = (f32[32]{0:T(128)S(1)}, f32[32]{0:T(128)}, u32[]{:S(2)}) copy-start(f32[32]{0:T(128)} %weight_ref.1) | copy-start | bytes 388
  2.0 39.2 %collective-permute-start.1 = (bf16[1024,256]{1,0:T(8,128)(2,1)S(1)}, bf16[1024,256]{1,0:T(8,128)(2,1)S(1)}, u32[]{:S(2)}, u32[]{:S(2)}) collective-permute-start(bf16[1024,256]{1,0:T(8,128)(2,1)S(1)} %opening.1.first_ref), channel_id=1, source_target_pairs={{0,8},{4,12},{8,0},{12,4},{1,9},{5,13},{9,1},{13,5},{2,10},{6,14},... | collective-permute-start | bytes 1572872 | tf_op jit(solution)/shard_map/ppermute | solution.py:221
  8.9 54.8 %collective-permute-start = (bf16[1024,256]{1,0:T(8,128)(2,1)S(1)}, bf16[1024,256]{1,0:T(8,128)(2,1)S(1)}, u32[]{:S(2)}, u32[]{:S(2)}) collective-permute-start(bf16[1024,256]{1,0:T(8,128)(2,1)S(1)} %get-tuple-element.24), channel_id=1, source_target_pairs={{0,8},{4,12},{8,0},{12,4},{1,9},{5,13},{9,1},{13,5},{2,10},{6,14},... | collective-permute-start | bytes 1572872 | tf_op jit(solution)/shard_map/ppermute | solution.py:221
  43.9 42.3 %collective-permute-start.6 = (bf16[1024,256]{1,0:T(8,128)(2,1)S(1)}, bf16[1024,256]{1,0:T(8,128)(2,1)S(1)}, u32[]{:S(2)}, u32[]{:S(2)}) collective-permute-start(bf16[1024,256]{1,0:T(8,128)(2,1)S(1)} %get-tuple-element.28), channel_id=1, source_target_pairs={{0,8},{4,12},{8,0},{12,4},{1,9},{5,13},{9,1},{13,5},{2,10},{6,14},... | collective-permute-start | bytes 1572872 | tf_op jit(solution)/shard_map/ppermute | solution.py:281
  44.0 22.5 %collective-permute-start.7 = (f32[2,2,128,128]{3,2,1,0:T(8,128)S(1)}, f32[2,2,128,128]{3,2,1,0:T(8,128)S(1)}, u32[]{:S(2)}, u32[]{:S(2)}) collective-permute-start(f32[2,2,128,128]{3,2,1,0:T(8,128)S(1)} %get-tuple-element.25.refs_4_.refs_5_), channel_id=1, source_target_pairs={{0,1},{1,0},{2,3},{3,2},{4,5},{5,4},{6,7},{7,6},{8,9},{9,8},{10,11... | collective-permute-start | bytes 786440 | tf_op jit(solution)/shard_map/ppermute | solution.py:278
  44.0 22.5 %collective-permute-start.8 = (f32[2,2,128,128]{3,2,1,0:T(8,128)S(1)}, f32[2,2,128,128]{3,2,1,0:T(8,128)S(1)}, u32[]{:S(2)}, u32[]{:S(2)}) collective-permute-start(f32[2,2,128,128]{3,2,1,0:T(8,128)S(1)} %get-tuple-element.25.refs_4_.refs_5_), channel_id=1, source_target_pairs={{0,2},{1,3},{2,0},{3,1},{4,6},{5,7},{6,4},{7,5},{8,10},{9,11},{10,... | collective-permute-start | bytes 786440 | tf_op jit(solution)/shard_map/ppermute | solution.py:278
  46.1 22.5 %collective-permute-start.9 = (f32[2,2,128,128]{3,2,1,0:T(8,128)S(1)}, f32[2,2,128,128]{3,2,1,0:T(8,128)S(1)}, u32[]{:S(2)}, u32[]{:S(2)}) collective-permute-start(f32[2,2,128,128]{3,2,1,0:T(8,128)S(1)} %get-tuple-element.25.refs_4_.refs_5_), channel_id=1, source_target_pairs={{0,3},{1,2},{2,1},{3,0},{4,7},{5,6},{6,5},{7,4},{8,11},{9,10},{10,... | collective-permute-start | bytes 786440 | tf_op jit(solution)/shard_map/ppermute | solution.py:278
  66.3 42.3 %collective-permute-start.2 = (bf16[1024,256]{1,0:T(8,128)(2,1)S(1)}, bf16[1024,256]{1,0:T(8,128)(2,1)S(1)}, u32[]{:S(2)}, u32[]{:S(2)}) collective-permute-start(bf16[1024,256]{1,0:T(8,128)(2,1)S(1)} %get-tuple-element.26), channel_id=1, source_target_pairs={{0,8},{4,12},{8,0},{12,4},{1,9},{5,13},{9,1},{13,5},{2,10},{6,14},... | collective-permute-start | bytes 1572872 | tf_op jit(solution)/shard_map/ppermute | solution.py:281
  66.4 24.3 %collective-permute-start.3 = (f32[2,2,128,128]{3,2,1,0:T(8,128)S(1)}, f32[2,2,128,128]{3,2,1,0:T(8,128)S(1)}, u32[]{:S(2)}, u32[]{:S(2)}) collective-permute-start(f32[2,2,128,128]{3,2,1,0:T(8,128)S(1)} %get-tuple-element.27.refs_9_.refs_5_), channel_id=1, source_target_pairs={{0,1},{1,0},{2,3},{3,2},{4,5},{5,4},{6,7},{7,6},{8,9},{9,8},{10,11... | collective-permute-start | bytes 786440 | tf_op jit(solution)/shard_map/ppermute | solution.py:278
  66.5 24.3 %collective-permute-start.4 = (f32[2,2,128,128]{3,2,1,0:T(8,128)S(1)}, f32[2,2,128,128]{3,2,1,0:T(8,128)S(1)}, u32[]{:S(2)}, u32[]{:S(2)}) collective-permute-start(f32[2,2,128,128]{3,2,1,0:T(8,128)S(1)} %get-tuple-element.27.refs_9_.refs_5_), channel_id=1, source_target_pairs={{0,2},{1,3},{2,0},{3,1},{4,6},{5,7},{6,4},{7,5},{8,10},{9,11},{10,... | collective-permute-start | bytes 786440 | tf_op jit(solution)/shard_map/ppermute | solution.py:278
  68.5 24.3 %collective-permute-start.5 = (f32[2,2,128,128]{3,2,1,0:T(8,128)S(1)}, f32[2,2,128,128]{3,2,1,0:T(8,128)S(1)}, u32[]{:S(2)}, u32[]{:S(2)}) collective-permute-start(f32[2,2,128,128]{3,2,1,0:T(8,128)S(1)} %get-tuple-element.27.refs_9_.refs_5_), channel_id=1, source_target_pairs={{0,3},{1,2},{2,1},{3,0},{4,7},{5,6},{6,5},{7,4},{8,11},{9,10},{10,... | collective-permute-start | bytes 786440 | tf_op jit(solution)/shard_map/ppermute | solution.py:278
  90.7 40.4 %collective-permute-start.17 = (bf16[1024,256]{1,0:T(8,128)(2,1)S(1)}, bf16[1024,256]{1,0:T(8,128)(2,1)S(1)}, u32[]{:S(2)}, u32[]{:S(2)}) collective-permute-start(bf16[1024,256]{1,0:T(8,128)(2,1)S(1)} %get-tuple-element.33), channel_id=1, source_target_pairs={{0,8},{4,12},{8,0},{12,4},{1,9},{5,13},{9,1},{13,5},{2,10},{6,14},... | collective-permute-start | bytes 1572872 | tf_op jit(solution)/shard_map/ppermute | solution.py:281
  90.8 22.5 %collective-permute-start.14 = (f32[2,2,128,128]{3,2,1,0:T(8,128)S(1)}, f32[2,2,128,128]{3,2,1,0:T(8,128)S(1)}, u32[]{:S(2)}, u32[]{:S(2)}) collective-permute-start(f32[2,2,128,128]{3,2,1,0:T(8,128)S(1)} %get-tuple-element.32.refs_4_), channel_id=1, source_target_pairs={{0,1},{1,0},{2,3},{3,2},{4,5},{5,4},{6,7},{7,6},{8,9},{9,8},{10,11... | collective-permute-start | bytes 786440 | tf_op jit(solution)/shard_map/ppermute | solution.py:278
  90.9 22.5 %collective-permute-start.15 = (f32[2,2,128,128]{3,2,1,0:T(8,128)S(1)}, f32[2,2,128,128]{3,2,1,0:T(8,128)S(1)}, u32[]{:S(2)}, u32[]{:S(2)}) collective-permute-start(f32[2,2,128,128]{3,2,1,0:T(8,128)S(1)} %get-tuple-element.32.refs_4_), channel_id=1, source_target_pairs={{0,2},{1,3},{2,0},{3,1},{4,6},{5,7},{6,4},{7,5},{8,10},{9,11},{10,... | collective-permute-start | bytes 786440 | tf_op jit(solution)/shard_map/ppermute | solution.py:278
  92.9 22.5 %collective-permute-start.16 = (f32[2,2,128,128]{3,2,1,0:T(8,128)S(1)}, f32[2,2,128,128]{3,2,1,0:T(8,128)S(1)}, u32[]{:S(2)}, u32[]{:S(2)}) collective-permute-start(f32[2,2,128,128]{3,2,1,0:T(8,128)S(1)} %get-tuple-element.32.refs_4_), channel_id=1, source_target_pairs={{0,3},{1,2},{2,1},{3,0},{4,7},{5,6},{6,5},{7,4},{8,11},{9,10},{10,... | collective-permute-start | bytes 786440 | tf_op jit(solution)/shard_map/ppermute | solution.py:278
  113.2 40.4 %collective-permute-start.13 = (bf16[1024,256]{1,0:T(8,128)(2,1)S(1)}, bf16[1024,256]{1,0:T(8,128)(2,1)S(1)}, u32[]{:S(2)}, u32[]{:S(2)}) collective-permute-start(bf16[1024,256]{1,0:T(8,128)(2,1)S(1)} %get-tuple-element.31), channel_id=1, source_target_pairs={{0,8},{4,12},{8,0},{12,4},{1,9},{5,13},{9,1},{13,5},{2,10},{6,14},... | collective-permute-start | bytes 1572872 | tf_op jit(solution)/shard_map/ppermute | solution.py:281
  113.3 21.6 %collective-permute-start.10 = (f32[2,2,128,128]{3,2,1,0:T(8,128)S(1)}, f32[2,2,128,128]{3,2,1,0:T(8,128)S(1)}, u32[]{:S(2)}, u32[]{:S(2)}) collective-permute-start(f32[2,2,128,128]{3,2,1,0:T(8,128)S(1)} %get-tuple-element.30.refs_4_), channel_id=1, source_target_pairs={{0,1},{1,0},{2,3},{3,2},{4,5},{5,4},{6,7},{7,6},{8,9},{9,8},{10,11... | collective-permute-start | bytes 786440 | tf_op jit(solution)/shard_map/ppermute | solution.py:278
  113.3 21.5 %collective-permute-start.11 = (f32[2,2,128,128]{3,2,1,0:T(8,128)S(1)}, f32[2,2,128,128]{3,2,1,0:T(8,128)S(1)}, u32[]{:S(2)}, u32[]{:S(2)}) collective-permute-start(f32[2,2,128,128]{3,2,1,0:T(8,128)S(1)} %get-tuple-element.30.refs_4_), channel_id=1, source_target_pairs={{0,2},{1,3},{2,0},{3,1},{4,6},{5,7},{6,4},{7,5},{8,10},{9,11},{10,... | collective-permute-start | bytes 786440 | tf_op jit(solution)/shard_map/ppermute | solution.py:278
  115.4 19.5 %collective-permute-start.12 = (f32[2,2,128,128]{3,2,1,0:T(8,128)S(1)}, f32[2,2,128,128]{3,2,1,0:T(8,128)S(1)}, u32[]{:S(2)}, u32[]{:S(2)}) collective-permute-start(f32[2,2,128,128]{3,2,1,0:T(8,128)S(1)} %get-tuple-element.30.refs_4_), channel_id=1, source_target_pairs={{0,3},{1,2},{2,1},{3,0},{4,7},{5,6},{6,5},{7,4},{8,11},{9,10},{10,... | collective-permute-start | bytes 786440 | tf_op jit(solution)/shard_map/ppermute | solution.py:278
  134.8 41.3 %collective-permute-start.19 = (bf16[1024,256]{1,0:T(8,128)(2,1)S(1)}, bf16[1024,256]{1,0:T(8,128)(2,1)S(1)}, u32[]{:S(2)}, u32[]{:S(2)}) collective-permute-start(bf16[1024,256]{1,0:T(8,128)(2,1)S(1)} %get-tuple-element.37), channel_id=1, source_target_pairs={{0,8},{4,12},{8,0},{12,4},{1,9},{5,13},{9,1},{13,5},{2,10},{6,14},... | collective-permute-start | bytes 1572872 | tf_op jit(solution)/shard_map/ppermute | solution.py:281
  157.2 29.3 %collective-permute-start.18 = (bf16[1024,256]{1,0:T(8,128)(2,1)S(1)}, bf16[1024,256]{1,0:T(8,128)(2,1)S(1)}, u32[]{:S(2)}, u32[]{:S(2)}) collective-permute-start(bf16[1024,256]{1,0:T(8,128)(2,1)S(1)} %get-tuple-element.36), channel_id=1, source_target_pairs={{0,8},{4,12},{8,0},{12,4},{1,9},{5,13},{9,1},{13,5},{2,10},{6,14},... | collective-permute-start | bytes 1572872 | tf_op jit(solution)/shard_map/ppermute | solution.py:281

commit v4 on v3

--- a/solution.py
+++ b/solution.py
@@ -9,7 +9,7 @@
 
 BLOCK = 128
 STRETCH = 256
-CHUNKS = (2,2,2,2,)
+CHUNKS = (2, 2, 2, 2)
 LAG = 2
 
 ANY = pl.BlockSpec(memory_space=pl.ANY)
@@ -25,8 +25,26 @@
     return ref.at[:, pl.ds(start, BLOCK)]
 
 
-def plan(per_dev, blocks_ref, weight_ref, place_ref, scale_ref):
-    me = lax.axis_index("outer")
+def plan(per_dev, stride, blocks_ref, weight_ref, place_ref, scale_ref):
+    me, owners = lax.axis_index("outer"), lax.axis_size("outer")
+    half = per_dev // 2
+
+    def mated(c, carry):
+        first, second = blocks_ref[0, c], blocks_ref[1, c]
+        first_mine = lax.div(first, per_dev) == me
+        mine = jnp.where(first_mine, first, second)
+        other = lax.rem(jnp.where(first_mine, second, first), per_dev)
+        upper = me >= stride
+        local = lax.rem(mine, per_dev)
+        key = jnp.where(upper, local, other)
+        spare = lax.div(mine, per_dev) != me
+        keeps = (key >= half) == upper
+        slot = lax.rem(key, half)
+        kept = jnp.where(spare | jnp.logical_not(keeps), half, slot)
+        place_ref[0, kept] = local
+        scale_ref[0, kept] = 4.0 * weight_ref[c]
+        place_ref[1, jnp.where(spare | keeps, half, slot)] = local
+        return carry
 
     def one(c, counts):
         first, second = blocks_ref[0, c], blocks_ref[1, c]
@@ -38,7 +56,10 @@
         seconds += (lax.div(second, per_dev) == me).astype(jnp.int32)
         return firsts, seconds
 
-    lax.fori_loop(0, blocks_ref.shape[1], one, (jnp.int32(0), jnp.int32(0)))
+    if owners == 2 * stride:
+        lax.fori_loop(0, blocks_ref.shape[1], mated, jnp.int32(0))
+    else:
+        lax.fori_loop(0, blocks_ref.shape[1], one, (jnp.int32(0), jnp.int32(0)))
 
 
 def gather(decoder_ref, blocks, outs, sizes, sem):
@@ -55,22 +76,47 @@
         copy.wait()
 
 
-def opening_kernel(per_dev, sizes, blocks_ref, decoder_ref, out_ref, held_ref, sem):
-    me = lax.axis_index("outer")
-    fetch = pltpu.make_async_copy(blocks_ref, held_ref, sem.at[0])
-    fetch.start()
-    fetch.wait()
-    blocks, c = [], jnp.int32(0)
-    for _ in range(sizes[0]):
-        c = lax.while_loop(lambda c: lax.div(held_ref[1, c], per_dev) != me, lambda c: c + 1, c)
-        blocks.append(lax.rem(held_ref[1, c], per_dev))
-        c += 1
-    gather(decoder_ref, blocks, [out_ref], sizes, sem)
-
-
-def planning_kernel(per_dev, start, sizes, blocks_ref, weight_ref, decoder_ref, first_ref, place_ref, scale_ref, *rest):
+def opening_kernel(per_dev, stride, sizes, blocks_ref, decoder_ref, out_ref, held_ref, sem):
+    me, owners = lax.axis_index("outer"), lax.axis_size("outer")
+    half = per_dev // 2
+
+    def fetch():
+        copy = pltpu.make_async_copy(blocks_ref, held_ref, sem.at[0])
+        copy.start()
+        copy.wait()
+
+    if owners == 2 * stride:
+
+        @pl.when(me >= stride)
+        def _():
+            gather(decoder_ref, range(sizes[0]), [out_ref], sizes, sem)
+
+        @pl.when(me < stride)
+        def _():
+            fetch()
+            blocks = []
+            for j in range(sizes[0]):
+                wanted = (me + stride) * per_dev + half + j
+                c = lax.while_loop(
+                    lambda c: (held_ref[0, c] != wanted) & (held_ref[1, c] != wanted), lambda c: c + 1, jnp.int32(0)
+                )
+                mate = jnp.where(held_ref[0, c] == wanted, held_ref[1, c], held_ref[0, c])
+                blocks.append(lax.rem(mate, per_dev))
+            gather(decoder_ref, blocks, [out_ref], sizes, sem)
+
+    else:
+        fetch()
+        blocks, c = [], jnp.int32(0)
+        for _ in range(sizes[0]):
+            c = lax.while_loop(lambda c: lax.div(held_ref[1, c], per_dev) != me, lambda c: c + 1, c)
+            blocks.append(lax.rem(held_ref[1, c], per_dev))
+            c += 1
+        gather(decoder_ref, blocks, [out_ref], sizes, sem)
+
+
+def planning_kernel(per_dev, stride, start, sizes, blocks_ref, weight_ref, decoder_ref, first_ref, place_ref, scale_ref, *rest):
     outs, sem = rest[:-1], rest[-1]
-    plan(per_dev, blocks_ref, weight_ref, place_ref, scale_ref)
+    plan(per_dev, stride, blocks_ref, weight_ref, place_ref, scale_ref)
     gather(decoder_ref, [place_ref[1, start + j] for j in range(sum(sizes))], outs, sizes, sem)
 
 
@@ -103,7 +149,8 @@
 def step_kernel(spec, *refs):
     refs = list(refs)
     take = lambda: refs.pop(0)
-    place_ref, scale_ref, decoder_ref = take(), take(), take()
+    place_ref = take()
+    scale_ref, decoder_ref = (None, None) if spec["lean"] else (take(), take())
     gram_in = take() if spec["gram"] else None
     final_in = take() if spec["final"] else None
     parts = [take() for _ in range(spec["ranks"])] if spec["final"] else None
@@ -111,9 +158,9 @@
     for _ in range(spec["unread"]):
         take()
     gram_out = take() if spec["gram"] else None
-    send_out = take() if spec["final"] or spec["pack"] else None
+    send_outs = [take() for _ in range(spec["sends"])]
     out_ref = take() if spec["final"] or spec["back"] else None
-    gram_x, final_x, final_t, load_sem, move_sem, store_sem = refs
+    gram_x, final_x, final_t, load_sem, move_sem, store_sem = (None,) * 4 + (refs[0], None) if spec["lean"] else refs
 
     loads = {}
 
@@ -142,7 +189,7 @@
     if spec["pack"]:
         start, size = spec["pack"]
         for j in range(size):
-            move(column(decoder_ref, place_ref[1, start + j]), column(send_out, j))
+            move(column(decoder_ref, place_ref[1, start + j]), column(send_outs[0], j))
     if spec["gram"]:
         load("gram", gram_x, gram_in, *spec["gram"])
     if spec["final"]:
@@ -167,7 +214,8 @@
             a, b, c, d = (part[j] for part in parts)
             total = (a + b) + (c + d)
             final_t[j] = tangents(final_x[j], total[0], total[1], scale_ref[0, start + j])
-            for target, half in ((column(out_ref, place_ref[0, start + j]), 0), (column(send_out, j), 1)):
+            returned = column(send_outs[0], j) if len(send_outs) == 1 else send_outs[j]
+            for target, half in ((column(out_ref, place_ref[0, start + j]), 0), (returned, 1)):
                 stores.append(
                     pltpu.make_async_copy(
                         final_t.at[j, :, pl.ds(half * BLOCK, BLOCK)], target, store_sem.at[len(stores)]
@@ -196,7 +244,7 @@
     stay = lambda x: pltpu.with_memory_space_constraint(x, pltpu.HBM)
     pairs, decoder = stay(stretch_blocks.T), stay(decoder)
     first = pl.pallas_call(
-        functools.partial(opening_kernel, per_dev, sizes[:1]),
+        functools.partial(opening_kernel, per_dev, stride, sizes[:1]),
         out_shape=array(0),
         in_specs=[HBM, HBM],
         out_specs=ANY,
@@ -205,7 +253,7 @@
         name="opening",
     )(pairs, decoder)
     place, scale, *raw = pl.pallas_call(
-        functools.partial(planning_kernel, per_dev, starts[1], sizes[1:LAG]),
+        functools.partial(planning_kernel, per_dev, stride, starts[1], sizes[1:LAG]),
         out_shape=[
             jax.ShapeDtypeStruct((2, half + 1), jnp.int32),
             jax.ShapeDtypeStruct((1, half + 1), jnp.float32),
@@ -221,7 +269,7 @@
     sends = [lax.ppermute(part, "outer", to_first) for part in [first] + raw]
     parts = {}
     out = chain = None
-    for step in range(2 * count):
+    for step in range(2 * count - 1):
         arrived = sends[step]
         gram = chunk(step) if step < count else None
         pack = chunk(step + LAG) if step + LAG < count else None
@@ -229,7 +277,10 @@
         final = chunk(turn) if 0 <= turn < count else None
         back = chunk(step - count) if step >= count else None
         spec = {"gram": gram, "pack": pack, "final": final, "back": back, "ranks": ranks, "unread": 0}
-        args, specs = [place, scale, decoder], [SMEM, SMEM, HBM]
+        spec["lean"] = not (gram or pack or final)
+        args, specs = [place], [SMEM]
+        if not spec["lean"]:
+            args, specs = args + [scale, decoder], specs + [SMEM, HBM]
         shapes, out_specs, aliases = [], [], {}
         if gram:
             args, specs = args + [arrived], specs + [ANY]
@@ -239,7 +290,12 @@
             args, specs = args + [sends[turn]] + parts.pop(turn), specs + [ANY] + [VMEM] * ranks
         if back:
             args, specs = args + [arrived], specs + [ANY]
-        if final or pack:
+        spec["sends"] = int(bool(final or pack))
+        if turn == count - 1:
+            spec["sends"] = sizes[turn]
+            shapes += [jax.ShapeDtypeStruct((width, BLOCK), decoder.dtype)] * sizes[turn]
+            out_specs += [ANY] * sizes[turn]
+        elif final or pack:
             shapes.append(array(turn if final else step + LAG))
             out_specs.append(ANY)
         if final or back:
@@ -260,7 +316,9 @@
                 in_specs=specs,
                 out_specs=out_specs,
                 input_output_aliases=aliases,
-                scratch_shapes=[
+                scratch_shapes=[pltpu.SemaphoreType.DMA((2 * slot,))]
+                if spec["lean"]
+                else [
                     pltpu.VMEM((slot, width, STRETCH), decoder.dtype),
                     pltpu.VMEM((slot, width, STRETCH), decoder.dtype),
                     pltpu.VMEM((slot, width, STRETCH), decoder.dtype),
@@ -277,10 +335,12 @@
             parts[step] = [mine] + [
                 lax.ppermute(mine, "inner", [(i, i ^ hop) for i in range(ranks)]) for hop in range(1, ranks)
             ]
-        if final or pack:
+        for _ in range(spec["sends"]):
             sends.append(lax.ppermute(results.pop(0), "outer", to_second if final else to_first))
         if final or back:
             out = results.pop(0)
+    for j in range(sizes[-1]):
+        out = lax.dynamic_update_slice(out, sends[j - sizes[-1]], (0, place[1, half - sizes[-1] + j] * BLOCK))
     return out
 
 

time: 188 us -> 187 us (level)
  waiting for transfers between devices: 145 us -> 136 us
  starting transfers between devices: 13.3 us -> 19.1 us
  local copies, waits for them, and re-layouts: 0.01 us -> 2.06 us
    ppermute x6 -> x7, waiting for transfers between devices: 95.2 us -> 87.3 us  [shards(): lax.ppermute(results.pop(0), 'outer', to_second if final else to_first)]
    ppermute x12, starting transfers between devices: 8.8 us -> 12.5 us  [shards(): lax.ppermute(mine, 'inner', [(i, i ^ hop) for i in range(ranks)])]
    ppermute x6 -> x7, starting transfers between devices: 0.43 us -> 3.34 us  [shards(): lax.ppermute(results.pop(0), 'outer', to_second if final else to_first)]
    pallas_call x8 -> x7, Pallas kernels: 24.4 us -> 22.9 us  [shards(): pl.pallas_call(functools.partial(step_kernel, spec), out_shape=shapes, in...]
  transfers between devices with their start and end apart: 20 -> 21, of which waited for: 8 -> 9; matrix products, arithmetic and copies ran while one was open for 0% -> 1% of each run, Pallas kernels for 14% -> 14%
where the time goes in v4:
time: 187 us
  waiting for transfers between devices  136 us (73%)
  Pallas kernels  28.1 us (15%)
  starting transfers between devices  19.1 us (10%)
  local copies, waits for them, and re-layouts  2.06 us (1%)
    ppermute x7, waiting for transfers between devices, shards(): lax.ppermute(results.pop(0), 'outer', to_second if final else to_first)  87.3 us
    ppermute x2, waiting for transfers between devices, shards(): sends = [lax.ppermute(part, 'outer', to_first) for part in [first] + raw]  48.6 us
    pallas_call x7, Pallas kernels, shards(): pl.pallas_call(functools.partial(step_kernel, spec), out_shape=shapes, in...  22.9 us
    ppermute x12, starting transfers between devices, shards(): lax.ppermute(mine, 'inner', [(i, i ^ hop) for i in range(ranks)])  12.5 us
  transfers between devices with their start and end apart: 21, of which 9 were waited for; matrix products, arithmetic and copies ran while one was open for 1% of the time, Pallas kernels for 14%

profile of v4, /device:TPU:0, one launch (start us, length us, event | category | flops | bytes accessed | tf_op | source)
XLA Modules:
  0.0 186.6 jit_solution(7987114379042216413)
XLA Ops:
  0.0 2.1 %opening.1.first_ref = bf16[1024,256]{1,0:T(8,128)(2,1)S(1)} custom-call(s32[2,32]{1,0:T(2,128)} %bitcast.3, bf16[1024,2048]{1,0:T(8,128)(2,1)} %refs_2_.11), custom_call_target="tpu_custom_call" | custom-call | tf_op jit(solution)/shard_map/opening/pallas_call | solution.py:246
  2.1 3.1 %collective-permute-start = (bf16[1024,256]{1,0:T(8,128)(2,1)S(1)}, bf16[1024,256]{1,0:T(8,128)(2,1)S(1)}, u32[]{:S(2)}, u32[]{:S(2)}) collective-permute-start(bf16[1024,256]{1,0:T(8,128)(2,1)S(1)} %opening.1.first_ref), channel_id=1, source_target_pairs={{0,8},{4,12},{8,0},{12,4},{1,9},{5,13},{9,1},{13,5},{2,10},{6,14},... | collective-permute-start | bytes 1572872 | tf_op jit(solution)/shard_map/ppermute | solution.py:269
  5.2 3.2 %planning.1 = (s32[2,9]{1,0:T(2,128)S(1)}, f32[1,9]{1,0:T(1,128)S(1)}, bf16[1024,256]{1,0:T(8,128)(2,1)S(1)}) custom-call(s32[2,32]{1,0:T(2,128)S(1)} %bitcast.4, f32[32]{0:T(128)S(1)} %copy-done.1, bf16[1024,2048]{1,0:T(8,128)(2,1)} %refs_2_.11, bf16[1024,256]{1,0:T(8,128)(2,1)S(1)} %opening.1.first_ref), custom_call_target="tpu_custom_call" | custom-call | tf_op jit(solution)/shard_map/planning/pallas_call | solution.py:255
  8.4 0.1 collective-permute-start.5
  8.5 31.9 %collective-permute-done.refs_3_.refs_4_ = bf16[1024,256]{1,0:T(8,128)(2,1)S(1)} collective-permute-done((bf16[1024,256]{1,0:T(8,128)(2,1)S(1)}, bf16[1024,256]{1,0:T(8,128)(2,1)S(1)}, u32[]{:S(2)}, u32[]{:S(2)}) %collective-permute-start) | collective-permute-done | bytes 524320 | tf_op jit(solution)/shard_map/ppermute | solution.py:269
  40.4 2.6 %step.7 = (f32[2,2,128,128]{3,2,1,0:T(8,128)S(1)}, bf16[1024,256]{1,0:T(8,128)(2,1)S(1)}) custom-call(s32[2,9]{1,0:T(2,128)S(1)} %get-tuple-element.23.refs_0_, f32[1,9]{1,0:T(1,128)S(1)} %get-tuple-element.24.refs_1_, bf16[1024,2048]{1,0:T(8,128)(2,1)} %refs_2_.11, bf16[1024,256]{1,0:T(8,128)(2,1)S(1)} %collective-permute-done.refs_3_.refs_4_), custom_call_target="tpu_custom_call" | custom-call | tf_op jit(solution)/shard_map/step/pallas_call | solution.py:313
  43.0 0.1 collective-permute-start.1
  43.2 3.0 %collective-permute-start.3 = (f32[2,2,128,128]{3,2,1,0:T(8,128)S(1)}, f32[2,2,128,128]{3,2,1,0:T(8,128)S(1)}, u32[]{:S(2)}, u32[]{:S(2)}) collective-permute-start(f32[2,2,128,128]{3,2,1,0:T(8,128)S(1)} %get-tuple-element.26.refs_4_.refs_5_), channel_id=1, source_target_pairs={{0,2},{1,3},{2,0},{3,1},{4,6},{5,7},{6,4},{7,5},{8,10},{9,11},{10,... | collective-permute-start | bytes 786440 | tf_op jit(solution)/shard_map/ppermute | solution.py:336
  46.2 16.7 %collective-permute-done.5.refs_3_.refs_4_ = bf16[1024,256]{1,0:T(8,128)(2,1)S(1)} collective-permute-done((bf16[1024,256]{1,0:T(8,128)(2,1)S(1)}, bf16[1024,256]{1,0:T(8,128)(2,1)S(1)}, u32[]{:S(2)}, u32[]{:S(2)}) %collective-permute-start.5) | collective-permute-done | bytes 524320 | tf_op jit(solution)/shard_map/ppermute | solution.py:269
  62.9 2.6 %step.8 = (f32[2,2,128,128]{3,2,1,0:T(8,128)S(1)}, bf16[1024,256]{1,0:T(8,128)(2,1)S(1)}) custom-call(s32[2,9]{1,0:T(2,128)S(1)} %get-tuple-element.23.refs_0_, f32[1,9]{1,0:T(1,128)S(1)} %get-tuple-element.24.refs_1_, bf16[1024,2048]{1,0:T(8,128)(2,1)} %refs_2_.11, bf16[1024,256]{1,0:T(8,128)(2,1)S(1)} %collective-permute-done.5.refs_3_.refs_4_, ...), custom_call_target="tpu_custom_call" | custom-call | tf_op jit(solution)/shard_map/step/pallas_call | solution.py:313
  65.7 3.0 %collective-permute-start.12 = (f32[2,2,128,128]{3,2,1,0:T(8,128)S(1)}, f32[2,2,128,128]{3,2,1,0:T(8,128)S(1)}, u32[]{:S(2)}, u32[]{:S(2)}) collective-permute-start(f32[2,2,128,128]{3,2,1,0:T(8,128)S(1)} %get-tuple-element.28.refs_9_.refs_5_), channel_id=1, source_target_pairs={{0,2},{1,3},{2,0},{3,1},{4,6},{5,7},{6,4},{7,5},{8,10},{9,11},{10,... | collective-permute-start | bytes 786440 | tf_op jit(solution)/shard_map/ppermute | solution.py:336
  68.6 0.1 collective-permute-start.13
  68.7 16.6 %collective-permute-done.1.refs_3_ = bf16[1024,256]{1,0:T(8,128)(2,1)S(1)} collective-permute-done((bf16[1024,256]{1,0:T(8,128)(2,1)S(1)}, bf16[1024,256]{1,0:T(8,128)(2,1)S(1)}, u32[]{:S(2)}, u32[]{:S(2)}) %collective-permute-start.1) | collective-permute-done | bytes 524320 | tf_op jit(solution)/shard_map/ppermute | solution.py:339
  85.3 4.5 %step.9 = (f32[2,2,128,128]{3,2,1,0:T(8,128)S(1)}, bf16[1024,256]{1,0:T(8,128)(2,1)S(1)}, bf16[1024,2048]{1,0:T(8,128)(2,1)}) custom-call(s32[2,9]{1,0:T(2,128)S(1)} %get-tuple-element.23.refs_0_, f32[1,9]{1,0:T(1,128)S(1)} %get-tuple-element.24.refs_1_, bf16[1024,2048]{1,0:T(8,128)(2,1)} %refs_2_.11, bf16[1024,256]{1,0:T(8,128)(2,1)S(1)} %collective-permute-done.1.refs_3_, ...), custom_call_target="tpu_custom_call" | custom-call | tf_op jit(solution)/shard_map/step/pallas_call | solution.py:313
  90.0 3.0 %collective-permute-start.7 = (f32[2,2,128,128]{3,2,1,0:T(8,128)S(1)}, f32[2,2,128,128]{3,2,1,0:T(8,128)S(1)}, u32[]{:S(2)}, u32[]{:S(2)}) collective-permute-start(f32[2,2,128,128]{3,2,1,0:T(8,128)S(1)} %get-tuple-element.29.refs_4_), channel_id=1, source_target_pairs={{0,2},{1,3},{2,0},{3,1},{4,6},{5,7},{6,4},{7,5},{8,10},{9,11},{10,... | collective-permute-start | bytes 786440 | tf_op jit(solution)/shard_map/ppermute | solution.py:336
  93.0 0.1 collective-permute-start.8
  93.1 14.7 %collective-permute-done.10.refs_3_ = bf16[1024,256]{1,0:T(8,128)(2,1)S(1)} collective-permute-done((bf16[1024,256]{1,0:T(8,128)(2,1)S(1)}, bf16[1024,256]{1,0:T(8,128)(2,1)S(1)}, u32[]{:S(2)}, u32[]{:S(2)}) %collective-permute-start.10) | collective-permute-done | bytes 524320 | tf_op jit(solution)/shard_map/ppermute | solution.py:339
  107.8 4.5 %step.10 = (f32[2,2,128,128]{3,2,1,0:T(8,128)S(1)}, bf16[1024,256]{1,0:T(8,128)(2,1)S(1)}, bf16[1024,2048]{1,0:T(8,128)(2,1)}) custom-call(s32[2,9]{1,0:T(2,128)S(1)} %get-tuple-element.23.refs_0_, f32[1,9]{1,0:T(1,128)S(1)} %get-tuple-element.24.refs_1_, bf16[1024,2048]{1,0:T(8,128)(2,1)} %refs_2_.11, ...), custom_call_target="tpu_custom_call", output_to_operand_aliasing={{2}: (9, {})} | custom-call | tf_op jit(solution)/shard_map/step/pallas_call | solution.py:313
  112.5 3.0 %collective-permute-start.16 = (f32[2,2,128,128]{3,2,1,0:T(8,128)S(1)}, f32[2,2,128,128]{3,2,1,0:T(8,128)S(1)}, u32[]{:S(2)}, u32[]{:S(2)}) collective-permute-start(f32[2,2,128,128]{3,2,1,0:T(8,128)S(1)} %get-tuple-element.35.refs_4_), channel_id=1, source_target_pairs={{0,2},{1,3},{2,0},{3,1},{4,6},{5,7},{6,4},{7,5},{8,10},{9,11},{10,... | collective-permute-start | bytes 786440 | tf_op jit(solution)/shard_map/ppermute | solution.py:336
  115.4 0.1 collective-permute-start.17
  115.6 14.7 %collective-permute-done.9.refs_8_ = bf16[1024,256]{1,0:T(8,128)(2,1)S(1)} collective-permute-done((bf16[1024,256]{1,0:T(8,128)(2,1)S(1)}, bf16[1024,256]{1,0:T(8,128)(2,1)S(1)}, u32[]{:S(2)}, u32[]{:S(2)}) %collective-permute-start.9) | collective-permute-done | bytes 524320 | tf_op jit(solution)/shard_map/ppermute | solution.py:339
  130.3 3.6 %step.11 = (bf16[1024,256]{1,0:T(8,128)(2,1)S(1)}, bf16[1024,2048]{1,0:T(8,128)(2,1)}) custom-call(s32[2,9]{1,0:T(2,128)S(1)} %get-tuple-element.23.refs_0_, f32[1,9]{1,0:T(1,128)S(1)} %get-tuple-element.24.refs_1_, bf16[1024,2048]{1,0:T(8,128)(2,1)} %refs_2_.11, ...), custom_call_target="tpu_custom_call", output_to_operand_aliasing={{1}: (9, {})} | custom-call | tf_op jit(solution)/shard_map/step/pallas_call | solution.py:313
  134.0 18.7 %collective-permute-done.18.refs_8_ = bf16[1024,256]{1,0:T(8,128)(2,1)S(1)} collective-permute-done((bf16[1024,256]{1,0:T(8,128)(2,1)S(1)}, bf16[1024,256]{1,0:T(8,128)(2,1)S(1)}, u32[]{:S(2)}, u32[]{:S(2)}) %collective-permute-start.18) | collective-permute-done | bytes 524320 | tf_op jit(solution)/shard_map/ppermute | solution.py:339
  152.7 3.6 %step.12 = (bf16[1024,128]{1,0:T(8,128)(2,1)S(1)}, bf16[1024,128]{1,0:T(8,128)(2,1)S(1)}, bf16[1024,2048]{1,0:T(8,128)(2,1)}) custom-call(s32[2,9]{1,0:T(2,128)S(1)} %get-tuple-element.23.refs_0_, f32[1,9]{1,0:T(1,128)S(1)} %get-tuple-element.24.refs_1_, bf16[1024,2048]{1,0:T(8,128)(2,1)} %refs_2_.11, ...), custom_call_target="tpu_custom_call", output_to_operand_aliasing={{2}: (9, {})} | custom-call | tf_op jit(solution)/shard_map/step/pallas_call | solution.py:313
  156.4 2.9 %collective-permute-start.20 = (bf16[1024,128]{1,0:T(8,128)(2,1)S(1)}, bf16[1024,128]{1,0:T(8,128)(2,1)S(1)}, u32[]{:S(2)}, u32[]{:S(2)}) collective-permute-start(bf16[1024,128]{1,0:T(8,128)(2,1)S(1)} %get-tuple-element.40), channel_id=1, source_target_pairs={{0,8},{4,12},{8,0},{12,4},{1,9},{5,13},{9,1},{13,5},{2,10},{6,14},... | collective-permute-start | bytes 786440 | tf_op jit(solution)/shard_map/ppermute | solution.py:339
  159.4 0.6 fusion
  161.2 14.0 %collective-permute-done.14.refs_1_ = bf16[1024,256]{1,0:T(8,128)(2,1)S(1)} collective-permute-done((bf16[1024,256]{1,0:T(8,128)(2,1)S(1)}, bf16[1024,256]{1,0:T(8,128)(2,1)S(1)}, u32[]{:S(2)}, u32[]{:S(2)}) %collective-permute-start.14) | collective-permute-done | bytes 524320 | tf_op jit(solution)/shard_map/ppermute | solution.py:339
  175.2 1.4 step.13
  176.6 4.2 %collective-permute-done.19 = bf16[1024,128]{1,0:T(8,128)(2,1)S(1)} collective-permute-done((bf16[1024,128]{1,0:T(8,128)(2,1)S(1)}, bf16[1024,128]{1,0:T(8,128)(2,1)S(1)}, u32[]{:S(2)}, u32[]{:S(2)}) %collective-permute-start.19) | collective-permute-done | bytes 262176 | tf_op jit(solution)/shard_map/ppermute | solution.py:339
  180.8 0.7 constant_dynamic-update-slice_fusion.1
  181.5 4.3 %collective-permute-done.20 = bf16[1024,128]{1,0:T(8,128)(2,1)S(1)} collective-permute-done((bf16[1024,128]{1,0:T(8,128)(2,1)S(1)}, bf16[1024,128]{1,0:T(8,128)(2,1)S(1)}, u32[]{:S(2)}, u32[]{:S(2)}) %collective-permute-start.20) | collective-permute-done | bytes 262176 | tf_op jit(solution)/shard_map/ppermute | solution.py:339
  185.9 0.7 constant_dynamic-update-slice_fusion
  (26 shorter events, 0.7 us)
Async XLA Ops:
  0.0 5.2 %copy-start = (s32[32,2]{0,1:T(2,128)S(1)}, s32[32,2]{0,1:T(2,128)}, u32[]{:S(2)}) copy-start(s32[32,2]{0,1:T(2,128)} %param.4) | copy-start | bytes 772
  0.0 5.2 %copy-start.1 = (f32[32]{0:T(128)S(1)}, f32[32]{0:T(128)}, u32[]{:S(2)}) copy-start(f32[32]{0:T(128)} %weight_ref.1) | copy-start | bytes 388
  2.1 38.3 %collective-permute-start = (bf16[1024,256]{1,0:T(8,128)(2,1)S(1)}, bf16[1024,256]{1,0:T(8,128)(2,1)S(1)}, u32[]{:S(2)}, u32[]{:S(2)}) collective-permute-start(bf16[1024,256]{1,0:T(8,128)(2,1)S(1)} %opening.1.first_ref), channel_id=1, source_target_pairs={{0,8},{4,12},{8,0},{12,4},{1,9},{5,13},{9,1},{13,5},{2,10},{6,14},... | collective-permute-start | bytes 1572872 | tf_op jit(solution)/shard_map/ppermute | solution.py:269
  8.4 54.5 %collective-permute-start.5 = (bf16[1024,256]{1,0:T(8,128)(2,1)S(1)}, bf16[1024,256]{1,0:T(8,128)(2,1)S(1)}, u32[]{:S(2)}, u32[]{:S(2)}) collective-permute-start(bf16[1024,256]{1,0:T(8,128)(2,1)S(1)} %get-tuple-element.27), channel_id=1, source_target_pairs={{0,8},{4,12},{8,0},{12,4},{1,9},{5,13},{9,1},{13,5},{2,10},{6,14},... | collective-permute-start | bytes 1572872 | tf_op jit(solution)/shard_map/ppermute | solution.py:269
  43.0 42.3 %collective-permute-start.1 = (bf16[1024,256]{1,0:T(8,128)(2,1)S(1)}, bf16[1024,256]{1,0:T(8,128)(2,1)S(1)}, u32[]{:S(2)}, u32[]{:S(2)}) collective-permute-start(bf16[1024,256]{1,0:T(8,128)(2,1)S(1)} %get-tuple-element.25), channel_id=1, source_target_pairs={{0,8},{4,12},{8,0},{12,4},{1,9},{5,13},{9,1},{13,5},{2,10},{6,14},... | collective-permute-start | bytes 1572872 | tf_op jit(solution)/shard_map/ppermute | solution.py:339
  43.1 22.5 %collective-permute-start.2 = (f32[2,2,128,128]{3,2,1,0:T(8,128)S(1)}, f32[2,2,128,128]{3,2,1,0:T(8,128)S(1)}, u32[]{:S(2)}, u32[]{:S(2)}) collective-permute-start(f32[2,2,128,128]{3,2,1,0:T(8,128)S(1)} %get-tuple-element.26.refs_4_.refs_5_), channel_id=1, source_target_pairs={{0,1},{1,0},{2,3},{3,2},{4,5},{5,4},{6,7},{7,6},{8,9},{9,8},{10,11... | collective-permute-start | bytes 786440 | tf_op jit(solution)/shard_map/ppermute | solution.py:336
  43.2 22.5 %collective-permute-start.3 = (f32[2,2,128,128]{3,2,1,0:T(8,128)S(1)}, f32[2,2,128,128]{3,2,1,0:T(8,128)S(1)}, u32[]{:S(2)}, u32[]{:S(2)}) collective-permute-start(f32[2,2,128,128]{3,2,1,0:T(8,128)S(1)} %get-tuple-element.26.refs_4_.refs_5_), channel_id=1, source_target_pairs={{0,2},{1,3},{2,0},{3,1},{4,6},{5,7},{6,4},{7,5},{8,10},{9,11},{10,... | collective-permute-start | bytes 786440 | tf_op jit(solution)/shard_map/ppermute | solution.py:336
  46.1 22.5 %collective-permute-start.4 = (f32[2,2,128,128]{3,2,1,0:T(8,128)S(1)}, f32[2,2,128,128]{3,2,1,0:T(8,128)S(1)}, u32[]{:S(2)}, u32[]{:S(2)}) collective-permute-start(f32[2,2,128,128]{3,2,1,0:T(8,128)S(1)} %get-tuple-element.26.refs_4_.refs_5_), channel_id=1, source_target_pairs={{0,3},{1,2},{2,1},{3,0},{4,7},{5,6},{6,5},{7,4},{8,11},{9,10},{10,... | collective-permute-start | bytes 786440 | tf_op jit(solution)/shard_map/ppermute | solution.py:336
  65.5 42.3 %collective-permute-start.10 = (bf16[1024,256]{1,0:T(8,128)(2,1)S(1)}, bf16[1024,256]{1,0:T(8,128)(2,1)S(1)}, u32[]{:S(2)}, u32[]{:S(2)}) collective-permute-start(bf16[1024,256]{1,0:T(8,128)(2,1)S(1)} %get-tuple-element.31), channel_id=1, source_target_pairs={{0,8},{4,12},{8,0},{12,4},{1,9},{5,13},{9,1},{13,5},{2,10},{6,14},... | collective-permute-start | bytes 1572872 | tf_op jit(solution)/shard_map/ppermute | solution.py:339
  65.6 24.3 %collective-permute-start.11 = (f32[2,2,128,128]{3,2,1,0:T(8,128)S(1)}, f32[2,2,128,128]{3,2,1,0:T(8,128)S(1)}, u32[]{:S(2)}, u32[]{:S(2)}) collective-permute-start(f32[2,2,128,128]{3,2,1,0:T(8,128)S(1)} %get-tuple-element.28.refs_9_.refs_5_), channel_id=1, source_target_pairs={{0,1},{1,0},{2,3},{3,2},{4,5},{5,4},{6,7},{7,6},{8,9},{9,8},{10,11... | collective-permute-start | bytes 786440 | tf_op jit(solution)/shard_map/ppermute | solution.py:336
  65.7 24.3 %collective-permute-start.12 = (f32[2,2,128,128]{3,2,1,0:T(8,128)S(1)}, f32[2,2,128,128]{3,2,1,0:T(8,128)S(1)}, u32[]{:S(2)}, u32[]{:S(2)}) collective-permute-start(f32[2,2,128,128]{3,2,1,0:T(8,128)S(1)} %get-tuple-element.28.refs_9_.refs_5_), channel_id=1, source_target_pairs={{0,2},{1,3},{2,0},{3,1},{4,6},{5,7},{6,4},{7,5},{8,10},{9,11},{10,... | collective-permute-start | bytes 786440 | tf_op jit(solution)/shard_map/ppermute | solution.py:336
  68.6 24.3 %collective-permute-start.13 = (f32[2,2,128,128]{3,2,1,0:T(8,128)S(1)}, f32[2,2,128,128]{3,2,1,0:T(8,128)S(1)}, u32[]{:S(2)}, u32[]{:S(2)}) collective-permute-start(f32[2,2,128,128]{3,2,1,0:T(8,128)S(1)} %get-tuple-element.28.refs_9_.refs_5_), channel_id=1, source_target_pairs={{0,3},{1,2},{2,1},{3,0},{4,7},{5,6},{6,5},{7,4},{8,11},{9,10},{10,... | collective-permute-start | bytes 786440 | tf_op jit(solution)/shard_map/ppermute | solution.py:336
  89.8 40.4 %collective-permute-start.9 = (bf16[1024,256]{1,0:T(8,128)(2,1)S(1)}, bf16[1024,256]{1,0:T(8,128)(2,1)S(1)}, u32[]{:S(2)}, u32[]{:S(2)}) collective-permute-start(bf16[1024,256]{1,0:T(8,128)(2,1)S(1)} %get-tuple-element.30), channel_id=1, source_target_pairs={{0,8},{4,12},{8,0},{12,4},{1,9},{5,13},{9,1},{13,5},{2,10},{6,14},... | collective-permute-start | bytes 1572872 | tf_op jit(solution)/shard_map/ppermute | solution.py:339
  89.9 22.5 %collective-permute-start.6 = (f32[2,2,128,128]{3,2,1,0:T(8,128)S(1)}, f32[2,2,128,128]{3,2,1,0:T(8,128)S(1)}, u32[]{:S(2)}, u32[]{:S(2)}) collective-permute-start(f32[2,2,128,128]{3,2,1,0:T(8,128)S(1)} %get-tuple-element.29.refs_4_), channel_id=1, source_target_pairs={{0,1},{1,0},{2,3},{3,2},{4,5},{5,4},{6,7},{7,6},{8,9},{9,8},{10,11... | collective-permute-start | bytes 786440 | tf_op jit(solution)/shard_map/ppermute | solution.py:336
  90.0 22.5 %collective-permute-start.7 = (f32[2,2,128,128]{3,2,1,0:T(8,128)S(1)}, f32[2,2,128,128]{3,2,1,0:T(8,128)S(1)}, u32[]{:S(2)}, u32[]{:S(2)}) collective-permute-start(f32[2,2,128,128]{3,2,1,0:T(8,128)S(1)} %get-tuple-element.29.refs_4_), channel_id=1, source_target_pairs={{0,2},{1,3},{2,0},{3,1},{4,6},{5,7},{6,4},{7,5},{8,10},{9,11},{10,... | collective-permute-start | bytes 786440 | tf_op jit(solution)/shard_map/ppermute | solution.py:336
  93.0 22.5 %collective-permute-start.8 = (f32[2,2,128,128]{3,2,1,0:T(8,128)S(1)}, f32[2,2,128,128]{3,2,1,0:T(8,128)S(1)}, u32[]{:S(2)}, u32[]{:S(2)}) collective-permute-start(f32[2,2,128,128]{3,2,1,0:T(8,128)S(1)} %get-tuple-element.29.refs_4_), channel_id=1, source_target_pairs={{0,3},{1,2},{2,1},{3,0},{4,7},{5,6},{6,5},{7,4},{8,11},{9,10},{10,... | collective-permute-start | bytes 786440 | tf_op jit(solution)/shard_map/ppermute | solution.py:336
  112.3 40.4 %collective-permute-start.18 = (bf16[1024,256]{1,0:T(8,128)(2,1)S(1)}, bf16[1024,256]{1,0:T(8,128)(2,1)S(1)}, u32[]{:S(2)}, u32[]{:S(2)}) collective-permute-start(bf16[1024,256]{1,0:T(8,128)(2,1)S(1)} %get-tuple-element.36), channel_id=1, source_target_pairs={{0,8},{4,12},{8,0},{12,4},{1,9},{5,13},{9,1},{13,5},{2,10},{6,14},... | collective-permute-start | bytes 1572872 | tf_op jit(solution)/shard_map/ppermute | solution.py:339
  112.4 21.6 %collective-permute-start.15 = (f32[2,2,128,128]{3,2,1,0:T(8,128)S(1)}, f32[2,2,128,128]{3,2,1,0:T(8,128)S(1)}, u32[]{:S(2)}, u32[]{:S(2)}) collective-permute-start(f32[2,2,128,128]{3,2,1,0:T(8,128)S(1)} %get-tuple-element.35.refs_4_), channel_id=1, source_target_pairs={{0,1},{1,0},{2,3},{3,2},{4,5},{5,4},{6,7},{7,6},{8,9},{9,8},{10,11... | collective-permute-start | bytes 786440 | tf_op jit(solution)/shard_map/ppermute | solution.py:336
  112.5 21.5 %collective-permute-start.16 = (f32[2,2,128,128]{3,2,1,0:T(8,128)S(1)}, f32[2,2,128,128]{3,2,1,0:T(8,128)S(1)}, u32[]{:S(2)}, u32[]{:S(2)}) collective-permute-start(f32[2,2,128,128]{3,2,1,0:T(8,128)S(1)} %get-tuple-element.35.refs_4_), channel_id=1, source_target_pairs={{0,2},{1,3},{2,0},{3,1},{4,6},{5,7},{6,4},{7,5},{8,10},{9,11},{10,... | collective-permute-start | bytes 786440 | tf_op jit(solution)/shard_map/ppermute | solution.py:336
  115.4 18.6 %collective-permute-start.17 = (f32[2,2,128,128]{3,2,1,0:T(8,128)S(1)}, f32[2,2,128,128]{3,2,1,0:T(8,128)S(1)}, u32[]{:S(2)}, u32[]{:S(2)}) collective-permute-start(f32[2,2,128,128]{3,2,1,0:T(8,128)S(1)} %get-tuple-element.35.refs_4_), channel_id=1, source_target_pairs={{0,3},{1,2},{2,1},{3,0},{4,7},{5,6},{6,5},{7,4},{8,11},{9,10},{10,... | collective-permute-start | bytes 786440 | tf_op jit(solution)/shard_map/ppermute | solution.py:336
  133.9 41.3 %collective-permute-start.14 = (bf16[1024,256]{1,0:T(8,128)(2,1)S(1)}, bf16[1024,256]{1,0:T(8,128)(2,1)S(1)}, u32[]{:S(2)}, u32[]{:S(2)}) collective-permute-start(bf16[1024,256]{1,0:T(8,128)(2,1)S(1)} %get-tuple-element.34), channel_id=1, source_target_pairs={{0,8},{4,12},{8,0},{12,4},{1,9},{5,13},{9,1},{13,5},{2,10},{6,14},... | collective-permute-start | bytes 1572872 | tf_op jit(solution)/shard_map/ppermute | solution.py:339
  156.4 24.5 %collective-permute-start.19 = (bf16[1024,128]{1,0:T(8,128)(2,1)S(1)}, bf16[1024,128]{1,0:T(8,128)(2,1)S(1)}, u32[]{:S(2)}, u32[]{:S(2)}) collective-permute-start(bf16[1024,128]{1,0:T(8,128)(2,1)S(1)} %get-tuple-element.39), channel_id=1, source_target_pairs={{0,8},{4,12},{8,0},{12,4},{1,9},{5,13},{9,1},{13,5},{2,10},{6,14},... | collective-permute-start | bytes 786440 | tf_op jit(solution)/shard_map/ppermute | solution.py:339
  156.4 29.4 %collective-permute-start.20 = (bf16[1024,128]{1,0:T(8,128)(2,1)S(1)}, bf16[1024,128]{1,0:T(8,128)(2,1)S(1)}, u32[]{:S(2)}, u32[]{:S(2)}) collective-permute-start(bf16[1024,128]{1,0:T(8,128)(2,1)S(1)} %get-tuple-element.40), channel_id=1, source_target_pairs={{0,8},{4,12},{8,0},{12,4},{1,9},{5,13},{9,1},{13,5},{2,10},{6,14},... | collective-permute-start | bytes 786440 | tf_op jit(solution)/shard_map/ppermute | solution.py:339

commit v5 on v4

--- a/solution.py
+++ b/solution.py
@@ -94,15 +94,19 @@
         @pl.when(me < stride)
         def _():
             fetch()
-            blocks = []
+            copies = []
             for j in range(sizes[0]):
                 wanted = (me + stride) * per_dev + half + j
-                c = lax.while_loop(
-                    lambda c: (held_ref[0, c] != wanted) & (held_ref[1, c] != wanted), lambda c: c + 1, jnp.int32(0)
+                mate = jnp.int32(0)
+                for c in range(held_ref.shape[1]):
+                    first, second = held_ref[0, c], held_ref[1, c]
+                    mate = jnp.where(first == wanted, second, jnp.where(second == wanted, first, mate))
+                copies.append(
+                    pltpu.make_async_copy(column(decoder_ref, lax.rem(mate, per_dev)), column(out_ref, j), sem.at[j])
                 )
-                mate = jnp.where(held_ref[0, c] == wanted, held_ref[1, c], held_ref[0, c])
-                blocks.append(lax.rem(mate, per_dev))
-            gather(decoder_ref, blocks, [out_ref], sizes, sem)
+                copies[-1].start()
+            for copy in copies:
+                copy.wait()
 
     else:
         fetch()

time: 187 us -> 187 us (level)
  no operation moved by 1% of the time
where the time goes in v5:
time: 187 us; the launch traced here: 186 us
  waiting for transfers between devices  136 us (73%)
  Pallas kernels  28 us (15%)
  starting transfers between devices  18.6 us (10%)
  local copies, waits for them, and re-layouts  2.06 us (1%)
    ppermute x7, waiting for transfers between devices, shards(): lax.ppermute(results.pop(0), 'outer', to_second if final else to_first)  87.7 us
    ppermute x2, waiting for transfers between devices, shards(): sends = [lax.ppermute(part, 'outer', to_first) for part in [first] + raw]  48.7 us
    pallas_call x7, Pallas kernels, shards(): pl.pallas_call(functools.partial(step_kernel, spec), out_shape=shapes, in...  22.9 us
    ppermute x12, starting transfers between devices, shards(): lax.ppermute(mine, 'inner', [(i, i ^ hop) for i in range(ranks)])  11.9 us
  transfers between devices with their start and end apart: 21, of which 9 were waited for; matrix products, arithmetic and copies ran while one was open for 1% of the time, Pallas kernels for 14%

profile of v5, /device:TPU:0, one launch (start us, length us, event | category | flops | bytes accessed | tf_op | source)
XLA Modules:
  0.0 186.5 jit_solution(4632957822667335324)
XLA Ops:
  0.0 2.0 %opening.1.first_ref = bf16[1024,256]{1,0:T(8,128)(2,1)S(1)} custom-call(s32[2,32]{1,0:T(2,128)} %bitcast.3, bf16[1024,2048]{1,0:T(8,128)(2,1)} %refs_2_.11), custom_call_target="tpu_custom_call" | custom-call | tf_op jit(solution)/shard_map/opening/pallas_call | solution.py:250
  2.0 3.2 %collective-permute-start = (bf16[1024,256]{1,0:T(8,128)(2,1)S(1)}, bf16[1024,256]{1,0:T(8,128)(2,1)S(1)}, u32[]{:S(2)}, u32[]{:S(2)}) collective-permute-start(bf16[1024,256]{1,0:T(8,128)(2,1)S(1)} %opening.1.first_ref), channel_id=1, source_target_pairs={{0,8},{4,12},{8,0},{12,4},{1,9},{5,13},{9,1},{13,5},{2,10},{6,14},... | collective-permute-start | bytes 1572872 | tf_op jit(solution)/shard_map/ppermute | solution.py:273
  5.2 3.2 %planning.1 = (s32[2,9]{1,0:T(2,128)S(1)}, f32[1,9]{1,0:T(1,128)S(1)}, bf16[1024,256]{1,0:T(8,128)(2,1)S(1)}) custom-call(s32[2,32]{1,0:T(2,128)S(1)} %bitcast.4, f32[32]{0:T(128)S(1)} %copy-done.1, bf16[1024,2048]{1,0:T(8,128)(2,1)} %refs_2_.11, bf16[1024,256]{1,0:T(8,128)(2,1)S(1)} %opening.1.first_ref), custom_call_target="tpu_custom_call" | custom-call | tf_op jit(solution)/shard_map/planning/pallas_call | solution.py:259
  8.4 0.1 collective-permute-start.5
  8.5 31.9 %collective-permute-done.refs_3_.refs_4_ = bf16[1024,256]{1,0:T(8,128)(2,1)S(1)} collective-permute-done((bf16[1024,256]{1,0:T(8,128)(2,1)S(1)}, bf16[1024,256]{1,0:T(8,128)(2,1)S(1)}, u32[]{:S(2)}, u32[]{:S(2)}) %collective-permute-start) | collective-permute-done | bytes 524320 | tf_op jit(solution)/shard_map/ppermute | solution.py:273
  40.4 2.6 %step.7 = (f32[2,2,128,128]{3,2,1,0:T(8,128)S(1)}, bf16[1024,256]{1,0:T(8,128)(2,1)S(1)}) custom-call(s32[2,9]{1,0:T(2,128)S(1)} %get-tuple-element.23.refs_0_, f32[1,9]{1,0:T(1,128)S(1)} %get-tuple-element.24.refs_1_, bf16[1024,2048]{1,0:T(8,128)(2,1)} %refs_2_.11, bf16[1024,256]{1,0:T(8,128)(2,1)S(1)} %collective-permute-done.refs_3_.refs_4_), custom_call_target="tpu_custom_call" | custom-call | tf_op jit(solution)/shard_map/step/pallas_call | solution.py:317
  43.0 0.1 collective-permute-start.1
  43.2 2.8 %collective-permute-start.3 = (f32[2,2,128,128]{3,2,1,0:T(8,128)S(1)}, f32[2,2,128,128]{3,2,1,0:T(8,128)S(1)}, u32[]{:S(2)}, u32[]{:S(2)}) collective-permute-start(f32[2,2,128,128]{3,2,1,0:T(8,128)S(1)} %get-tuple-element.26.refs_4_.refs_5_), channel_id=1, source_target_pairs={{0,2},{1,3},{2,0},{3,1},{4,6},{5,7},{6,4},{7,5},{8,10},{9,11},{10,... | collective-permute-start | bytes 786440 | tf_op jit(solution)/shard_map/ppermute | solution.py:340
  46.1 16.8 %collective-permute-done.5.refs_3_.refs_4_ = bf16[1024,256]{1,0:T(8,128)(2,1)S(1)} collective-permute-done((bf16[1024,256]{1,0:T(8,128)(2,1)S(1)}, bf16[1024,256]{1,0:T(8,128)(2,1)S(1)}, u32[]{:S(2)}, u32[]{:S(2)}) %collective-permute-start.5) | collective-permute-done | bytes 524320 | tf_op jit(solution)/shard_map/ppermute | solution.py:273
  62.9 2.6 %step.8 = (f32[2,2,128,128]{3,2,1,0:T(8,128)S(1)}, bf16[1024,256]{1,0:T(8,128)(2,1)S(1)}) custom-call(s32[2,9]{1,0:T(2,128)S(1)} %get-tuple-element.23.refs_0_, f32[1,9]{1,0:T(1,128)S(1)} %get-tuple-element.24.refs_1_, bf16[1024,2048]{1,0:T(8,128)(2,1)} %refs_2_.11, bf16[1024,256]{1,0:T(8,128)(2,1)S(1)} %collective-permute-done.5.refs_3_.refs_4_, ...), custom_call_target="tpu_custom_call" | custom-call | tf_op jit(solution)/shard_map/step/pallas_call | solution.py:317
  65.7 2.8 %collective-permute-start.12 = (f32[2,2,128,128]{3,2,1,0:T(8,128)S(1)}, f32[2,2,128,128]{3,2,1,0:T(8,128)S(1)}, u32[]{:S(2)}, u32[]{:S(2)}) collective-permute-start(f32[2,2,128,128]{3,2,1,0:T(8,128)S(1)} %get-tuple-element.28.refs_9_.refs_5_), channel_id=1, source_target_pairs={{0,2},{1,3},{2,0},{3,1},{4,6},{5,7},{6,4},{7,5},{8,10},{9,11},{10,... | collective-permute-start | bytes 786440 | tf_op jit(solution)/shard_map/ppermute | solution.py:340
  68.5 0.1 collective-permute-start.13
  68.6 16.7 %collective-permute-done.1.refs_3_ = bf16[1024,256]{1,0:T(8,128)(2,1)S(1)} collective-permute-done((bf16[1024,256]{1,0:T(8,128)(2,1)S(1)}, bf16[1024,256]{1,0:T(8,128)(2,1)S(1)}, u32[]{:S(2)}, u32[]{:S(2)}) %collective-permute-start.1) | collective-permute-done | bytes 524320 | tf_op jit(solution)/shard_map/ppermute | solution.py:343
  85.3 4.5 %step.9 = (f32[2,2,128,128]{3,2,1,0:T(8,128)S(1)}, bf16[1024,256]{1,0:T(8,128)(2,1)S(1)}, bf16[1024,2048]{1,0:T(8,128)(2,1)}) custom-call(s32[2,9]{1,0:T(2,128)S(1)} %get-tuple-element.23.refs_0_, f32[1,9]{1,0:T(1,128)S(1)} %get-tuple-element.24.refs_1_, bf16[1024,2048]{1,0:T(8,128)(2,1)} %refs_2_.11, bf16[1024,256]{1,0:T(8,128)(2,1)S(1)} %collective-permute-done.1.refs_3_, ...), custom_call_target="tpu_custom_call" | custom-call | tf_op jit(solution)/shard_map/step/pallas_call | solution.py:317
  90.0 2.8 %collective-permute-start.7 = (f32[2,2,128,128]{3,2,1,0:T(8,128)S(1)}, f32[2,2,128,128]{3,2,1,0:T(8,128)S(1)}, u32[]{:S(2)}, u32[]{:S(2)}) collective-permute-start(f32[2,2,128,128]{3,2,1,0:T(8,128)S(1)} %get-tuple-element.29.refs_4_), channel_id=1, source_target_pairs={{0,2},{1,3},{2,0},{3,1},{4,6},{5,7},{6,4},{7,5},{8,10},{9,11},{10,... | collective-permute-start | bytes 786440 | tf_op jit(solution)/shard_map/ppermute | solution.py:340
  92.8 0.1 collective-permute-start.8
  93.0 14.9 %collective-permute-done.10.refs_3_ = bf16[1024,256]{1,0:T(8,128)(2,1)S(1)} collective-permute-done((bf16[1024,256]{1,0:T(8,128)(2,1)S(1)}, bf16[1024,256]{1,0:T(8,128)(2,1)S(1)}, u32[]{:S(2)}, u32[]{:S(2)}) %collective-permute-start.10) | collective-permute-done | bytes 524320 | tf_op jit(solution)/shard_map/ppermute | solution.py:343
  107.8 4.5 %step.10 = (f32[2,2,128,128]{3,2,1,0:T(8,128)S(1)}, bf16[1024,256]{1,0:T(8,128)(2,1)S(1)}, bf16[1024,2048]{1,0:T(8,128)(2,1)}) custom-call(s32[2,9]{1,0:T(2,128)S(1)} %get-tuple-element.23.refs_0_, f32[1,9]{1,0:T(1,128)S(1)} %get-tuple-element.24.refs_1_, bf16[1024,2048]{1,0:T(8,128)(2,1)} %refs_2_.11, ...), custom_call_target="tpu_custom_call", output_to_operand_aliasing={{2}: (9, {})} | custom-call | tf_op jit(solution)/shard_map/step/pallas_call | solution.py:317
  112.5 2.8 %collective-permute-start.16 = (f32[2,2,128,128]{3,2,1,0:T(8,128)S(1)}, f32[2,2,128,128]{3,2,1,0:T(8,128)S(1)}, u32[]{:S(2)}, u32[]{:S(2)}) collective-permute-start(f32[2,2,128,128]{3,2,1,0:T(8,128)S(1)} %get-tuple-element.35.refs_4_), channel_id=1, source_target_pairs={{0,2},{1,3},{2,0},{3,1},{4,6},{5,7},{6,4},{7,5},{8,10},{9,11},{10,... | collective-permute-start | bytes 786440 | tf_op jit(solution)/shard_map/ppermute | solution.py:340
  115.3 0.1 collective-permute-start.17
  115.4 14.9 %collective-permute-done.9.refs_8_ = bf16[1024,256]{1,0:T(8,128)(2,1)S(1)} collective-permute-done((bf16[1024,256]{1,0:T(8,128)(2,1)S(1)}, bf16[1024,256]{1,0:T(8,128)(2,1)S(1)}, u32[]{:S(2)}, u32[]{:S(2)}) %collective-permute-start.9) | collective-permute-done | bytes 524320 | tf_op jit(solution)/shard_map/ppermute | solution.py:343
  130.3 3.6 %step.11 = (bf16[1024,256]{1,0:T(8,128)(2,1)S(1)}, bf16[1024,2048]{1,0:T(8,128)(2,1)}) custom-call(s32[2,9]{1,0:T(2,128)S(1)} %get-tuple-element.23.refs_0_, f32[1,9]{1,0:T(1,128)S(1)} %get-tuple-element.24.refs_1_, bf16[1024,2048]{1,0:T(8,128)(2,1)} %refs_2_.11, ...), custom_call_target="tpu_custom_call", output_to_operand_aliasing={{1}: (9, {})} | custom-call | tf_op jit(solution)/shard_map/step/pallas_call | solution.py:317
  134.0 18.7 %collective-permute-done.18.refs_8_ = bf16[1024,256]{1,0:T(8,128)(2,1)S(1)} collective-permute-done((bf16[1024,256]{1,0:T(8,128)(2,1)S(1)}, bf16[1024,256]{1,0:T(8,128)(2,1)S(1)}, u32[]{:S(2)}, u32[]{:S(2)}) %collective-permute-start.18) | collective-permute-done | bytes 524320 | tf_op jit(solution)/shard_map/ppermute | solution.py:343
  152.8 3.6 %step.12 = (bf16[1024,128]{1,0:T(8,128)(2,1)S(1)}, bf16[1024,128]{1,0:T(8,128)(2,1)S(1)}, bf16[1024,2048]{1,0:T(8,128)(2,1)}) custom-call(s32[2,9]{1,0:T(2,128)S(1)} %get-tuple-element.23.refs_0_, f32[1,9]{1,0:T(1,128)S(1)} %get-tuple-element.24.refs_1_, bf16[1024,2048]{1,0:T(8,128)(2,1)} %refs_2_.11, ...), custom_call_target="tpu_custom_call", output_to_operand_aliasing={{2}: (9, {})} | custom-call | tf_op jit(solution)/shard_map/step/pallas_call | solution.py:317
  156.5 2.9 %collective-permute-start.20 = (bf16[1024,128]{1,0:T(8,128)(2,1)S(1)}, bf16[1024,128]{1,0:T(8,128)(2,1)S(1)}, u32[]{:S(2)}, u32[]{:S(2)}) collective-permute-start(bf16[1024,128]{1,0:T(8,128)(2,1)S(1)} %get-tuple-element.40), channel_id=1, source_target_pairs={{0,8},{4,12},{8,0},{12,4},{1,9},{5,13},{9,1},{13,5},{2,10},{6,14},... | collective-permute-start | bytes 786440 | tf_op jit(solution)/shard_map/ppermute | solution.py:343
  159.4 0.6 fusion
  161.2 14.0 %collective-permute-done.14.refs_1_ = bf16[1024,256]{1,0:T(8,128)(2,1)S(1)} collective-permute-done((bf16[1024,256]{1,0:T(8,128)(2,1)S(1)}, bf16[1024,256]{1,0:T(8,128)(2,1)S(1)}, u32[]{:S(2)}, u32[]{:S(2)}) %collective-permute-start.14) | collective-permute-done | bytes 524320 | tf_op jit(solution)/shard_map/ppermute | solution.py:343
  175.2 1.4 step.13
  176.6 4.2 %collective-permute-done.19 = bf16[1024,128]{1,0:T(8,128)(2,1)S(1)} collective-permute-done((bf16[1024,128]{1,0:T(8,128)(2,1)S(1)}, bf16[1024,128]{1,0:T(8,128)(2,1)S(1)}, u32[]{:S(2)}, u32[]{:S(2)}) %collective-permute-start.19) | collective-permute-done | bytes 262176 | tf_op jit(solution)/shard_map/ppermute | solution.py:343
  180.8 0.7 constant_dynamic-update-slice_fusion.1
  181.6 4.2 %collective-permute-done.20 = bf16[1024,128]{1,0:T(8,128)(2,1)S(1)} collective-permute-done((bf16[1024,128]{1,0:T(8,128)(2,1)S(1)}, bf16[1024,128]{1,0:T(8,128)(2,1)S(1)}, u32[]{:S(2)}, u32[]{:S(2)}) %collective-permute-start.20) | collective-permute-done | bytes 262176 | tf_op jit(solution)/shard_map/ppermute | solution.py:343
  185.8 0.7 constant_dynamic-update-slice_fusion
  (26 shorter events, 0.7 us)
Async XLA Ops:
  0.0 5.2 %copy-start = (s32[32,2]{0,1:T(2,128)S(1)}, s32[32,2]{0,1:T(2,128)}, u32[]{:S(2)}) copy-start(s32[32,2]{0,1:T(2,128)} %param.4) | copy-start | bytes 772
  0.0 5.2 %copy-start.1 = (f32[32]{0:T(128)S(1)}, f32[32]{0:T(128)}, u32[]{:S(2)}) copy-start(f32[32]{0:T(128)} %weight_ref.1) | copy-start | bytes 388
  2.0 38.4 %collective-permute-start = (bf16[1024,256]{1,0:T(8,128)(2,1)S(1)}, bf16[1024,256]{1,0:T(8,128)(2,1)S(1)}, u32[]{:S(2)}, u32[]{:S(2)}) collective-permute-start(bf16[1024,256]{1,0:T(8,128)(2,1)S(1)} %opening.1.first_ref), channel_id=1, source_target_pairs={{0,8},{4,12},{8,0},{12,4},{1,9},{5,13},{9,1},{13,5},{2,10},{6,14},... | collective-permute-start | bytes 1572872 | tf_op jit(solution)/shard_map/ppermute | solution.py:273
  8.4 54.5 %collective-permute-start.5 = (bf16[1024,256]{1,0:T(8,128)(2,1)S(1)}, bf16[1024,256]{1,0:T(8,128)(2,1)S(1)}, u32[]{:S(2)}, u32[]{:S(2)}) collective-permute-start(bf16[1024,256]{1,0:T(8,128)(2,1)S(1)} %get-tuple-element.27), channel_id=1, source_target_pairs={{0,8},{4,12},{8,0},{12,4},{1,9},{5,13},{9,1},{13,5},{2,10},{6,14},... | collective-permute-start | bytes 1572872 | tf_op jit(solution)/shard_map/ppermute | solution.py:273
  43.0 42.3 %collective-permute-start.1 = (bf16[1024,256]{1,0:T(8,128)(2,1)S(1)}, bf16[1024,256]{1,0:T(8,128)(2,1)S(1)}, u32[]{:S(2)}, u32[]{:S(2)}) collective-permute-start(bf16[1024,256]{1,0:T(8,128)(2,1)S(1)} %get-tuple-element.25), channel_id=1, source_target_pairs={{0,8},{4,12},{8,0},{12,4},{1,9},{5,13},{9,1},{13,5},{2,10},{6,14},... | collective-permute-start | bytes 1572872 | tf_op jit(solution)/shard_map/ppermute | solution.py:343
  43.1 22.5 %collective-permute-start.2 = (f32[2,2,128,128]{3,2,1,0:T(8,128)S(1)}, f32[2,2,128,128]{3,2,1,0:T(8,128)S(1)}, u32[]{:S(2)}, u32[]{:S(2)}) collective-permute-start(f32[2,2,128,128]{3,2,1,0:T(8,128)S(1)} %get-tuple-element.26.refs_4_.refs_5_), channel_id=1, source_target_pairs={{0,1},{1,0},{2,3},{3,2},{4,5},{5,4},{6,7},{7,6},{8,9},{9,8},{10,11... | collective-permute-start | bytes 786440 | tf_op jit(solution)/shard_map/ppermute | solution.py:340
  43.2 22.5 %collective-permute-start.3 = (f32[2,2,128,128]{3,2,1,0:T(8,128)S(1)}, f32[2,2,128,128]{3,2,1,0:T(8,128)S(1)}, u32[]{:S(2)}, u32[]{:S(2)}) collective-permute-start(f32[2,2,128,128]{3,2,1,0:T(8,128)S(1)} %get-tuple-element.26.refs_4_.refs_5_), channel_id=1, source_target_pairs={{0,2},{1,3},{2,0},{3,1},{4,6},{5,7},{6,4},{7,5},{8,10},{9,11},{10,... | collective-permute-start | bytes 786440 | tf_op jit(solution)/shard_map/ppermute | solution.py:340
  46.0 22.5 %collective-permute-start.4 = (f32[2,2,128,128]{3,2,1,0:T(8,128)S(1)}, f32[2,2,128,128]{3,2,1,0:T(8,128)S(1)}, u32[]{:S(2)}, u32[]{:S(2)}) collective-permute-start(f32[2,2,128,128]{3,2,1,0:T(8,128)S(1)} %get-tuple-element.26.refs_4_.refs_5_), channel_id=1, source_target_pairs={{0,3},{1,2},{2,1},{3,0},{4,7},{5,6},{6,5},{7,4},{8,11},{9,10},{10,... | collective-permute-start | bytes 786440 | tf_op jit(solution)/shard_map/ppermute | solution.py:340
  65.5 42.3 %collective-permute-start.10 = (bf16[1024,256]{1,0:T(8,128)(2,1)S(1)}, bf16[1024,256]{1,0:T(8,128)(2,1)S(1)}, u32[]{:S(2)}, u32[]{:S(2)}) collective-permute-start(bf16[1024,256]{1,0:T(8,128)(2,1)S(1)} %get-tuple-element.31), channel_id=1, source_target_pairs={{0,8},{4,12},{8,0},{12,4},{1,9},{5,13},{9,1},{13,5},{2,10},{6,14},... | collective-permute-start | bytes 1572872 | tf_op jit(solution)/shard_map/ppermute | solution.py:343
  65.6 24.3 %collective-permute-start.11 = (f32[2,2,128,128]{3,2,1,0:T(8,128)S(1)}, f32[2,2,128,128]{3,2,1,0:T(8,128)S(1)}, u32[]{:S(2)}, u32[]{:S(2)}) collective-permute-start(f32[2,2,128,128]{3,2,1,0:T(8,128)S(1)} %get-tuple-element.28.refs_9_.refs_5_), channel_id=1, source_target_pairs={{0,1},{1,0},{2,3},{3,2},{4,5},{5,4},{6,7},{7,6},{8,9},{9,8},{10,11... | collective-permute-start | bytes 786440 | tf_op jit(solution)/shard_map/ppermute | solution.py:340
  65.7 24.3 %collective-permute-start.12 = (f32[2,2,128,128]{3,2,1,0:T(8,128)S(1)}, f32[2,2,128,128]{3,2,1,0:T(8,128)S(1)}, u32[]{:S(2)}, u32[]{:S(2)}) collective-permute-start(f32[2,2,128,128]{3,2,1,0:T(8,128)S(1)} %get-tuple-element.28.refs_9_.refs_5_), channel_id=1, source_target_pairs={{0,2},{1,3},{2,0},{3,1},{4,6},{5,7},{6,4},{7,5},{8,10},{9,11},{10,... | collective-permute-start | bytes 786440 | tf_op jit(solution)/shard_map/ppermute | solution.py:340
  68.5 24.3 %collective-permute-start.13 = (f32[2,2,128,128]{3,2,1,0:T(8,128)S(1)}, f32[2,2,128,128]{3,2,1,0:T(8,128)S(1)}, u32[]{:S(2)}, u32[]{:S(2)}) collective-permute-start(f32[2,2,128,128]{3,2,1,0:T(8,128)S(1)} %get-tuple-element.28.refs_9_.refs_5_), channel_id=1, source_target_pairs={{0,3},{1,2},{2,1},{3,0},{4,7},{5,6},{6,5},{7,4},{8,11},{9,10},{10,... | collective-permute-start | bytes 786440 | tf_op jit(solution)/shard_map/ppermute | solution.py:340
  89.9 40.4 %collective-permute-start.9 = (bf16[1024,256]{1,0:T(8,128)(2,1)S(1)}, bf16[1024,256]{1,0:T(8,128)(2,1)S(1)}, u32[]{:S(2)}, u32[]{:S(2)}) collective-permute-start(bf16[1024,256]{1,0:T(8,128)(2,1)S(1)} %get-tuple-element.30), channel_id=1, source_target_pairs={{0,8},{4,12},{8,0},{12,4},{1,9},{5,13},{9,1},{13,5},{2,10},{6,14},... | collective-permute-start | bytes 1572872 | tf_op jit(solution)/shard_map/ppermute | solution.py:343
  89.9 22.5 %collective-permute-start.6 = (f32[2,2,128,128]{3,2,1,0:T(8,128)S(1)}, f32[2,2,128,128]{3,2,1,0:T(8,128)S(1)}, u32[]{:S(2)}, u32[]{:S(2)}) collective-permute-start(f32[2,2,128,128]{3,2,1,0:T(8,128)S(1)} %get-tuple-element.29.refs_4_), channel_id=1, source_target_pairs={{0,1},{1,0},{2,3},{3,2},{4,5},{5,4},{6,7},{7,6},{8,9},{9,8},{10,11... | collective-permute-start | bytes 786440 | tf_op jit(solution)/shard_map/ppermute | solution.py:340
  90.0 22.5 %collective-permute-start.7 = (f32[2,2,128,128]{3,2,1,0:T(8,128)S(1)}, f32[2,2,128,128]{3,2,1,0:T(8,128)S(1)}, u32[]{:S(2)}, u32[]{:S(2)}) collective-permute-start(f32[2,2,128,128]{3,2,1,0:T(8,128)S(1)} %get-tuple-element.29.refs_4_), channel_id=1, source_target_pairs={{0,2},{1,3},{2,0},{3,1},{4,6},{5,7},{6,4},{7,5},{8,10},{9,11},{10,... | collective-permute-start | bytes 786440 | tf_op jit(solution)/shard_map/ppermute | solution.py:340
  92.8 22.5 %collective-permute-start.8 = (f32[2,2,128,128]{3,2,1,0:T(8,128)S(1)}, f32[2,2,128,128]{3,2,1,0:T(8,128)S(1)}, u32[]{:S(2)}, u32[]{:S(2)}) collective-permute-start(f32[2,2,128,128]{3,2,1,0:T(8,128)S(1)} %get-tuple-element.29.refs_4_), channel_id=1, source_target_pairs={{0,3},{1,2},{2,1},{3,0},{4,7},{5,6},{6,5},{7,4},{8,11},{9,10},{10,... | collective-permute-start | bytes 786440 | tf_op jit(solution)/shard_map/ppermute | solution.py:340
  112.3 40.4 %collective-permute-start.18 = (bf16[1024,256]{1,0:T(8,128)(2,1)S(1)}, bf16[1024,256]{1,0:T(8,128)(2,1)S(1)}, u32[]{:S(2)}, u32[]{:S(2)}) collective-permute-start(bf16[1024,256]{1,0:T(8,128)(2,1)S(1)} %get-tuple-element.36), channel_id=1, source_target_pairs={{0,8},{4,12},{8,0},{12,4},{1,9},{5,13},{9,1},{13,5},{2,10},{6,14},... | collective-permute-start | bytes 1572872 | tf_op jit(solution)/shard_map/ppermute | solution.py:343
  112.4 21.6 %collective-permute-start.15 = (f32[2,2,128,128]{3,2,1,0:T(8,128)S(1)}, f32[2,2,128,128]{3,2,1,0:T(8,128)S(1)}, u32[]{:S(2)}, u32[]{:S(2)}) collective-permute-start(f32[2,2,128,128]{3,2,1,0:T(8,128)S(1)} %get-tuple-element.35.refs_4_), channel_id=1, source_target_pairs={{0,1},{1,0},{2,3},{3,2},{4,5},{5,4},{6,7},{7,6},{8,9},{9,8},{10,11... | collective-permute-start | bytes 786440 | tf_op jit(solution)/shard_map/ppermute | solution.py:340
  112.5 21.5 %collective-permute-start.16 = (f32[2,2,128,128]{3,2,1,0:T(8,128)S(1)}, f32[2,2,128,128]{3,2,1,0:T(8,128)S(1)}, u32[]{:S(2)}, u32[]{:S(2)}) collective-permute-start(f32[2,2,128,128]{3,2,1,0:T(8,128)S(1)} %get-tuple-element.35.refs_4_), channel_id=1, source_target_pairs={{0,2},{1,3},{2,0},{3,1},{4,6},{5,7},{6,4},{7,5},{8,10},{9,11},{10,... | collective-permute-start | bytes 786440 | tf_op jit(solution)/shard_map/ppermute | solution.py:340
  115.3 18.7 %collective-permute-start.17 = (f32[2,2,128,128]{3,2,1,0:T(8,128)S(1)}, f32[2,2,128,128]{3,2,1,0:T(8,128)S(1)}, u32[]{:S(2)}, u32[]{:S(2)}) collective-permute-start(f32[2,2,128,128]{3,2,1,0:T(8,128)S(1)} %get-tuple-element.35.refs_4_), channel_id=1, source_target_pairs={{0,3},{1,2},{2,1},{3,0},{4,7},{5,6},{6,5},{7,4},{8,11},{9,10},{10,... | collective-permute-start | bytes 786440 | tf_op jit(solution)/shard_map/ppermute | solution.py:340
  133.9 41.3 %collective-permute-start.14 = (bf16[1024,256]{1,0:T(8,128)(2,1)S(1)}, bf16[1024,256]{1,0:T(8,128)(2,1)S(1)}, u32[]{:S(2)}, u32[]{:S(2)}) collective-permute-start(bf16[1024,256]{1,0:T(8,128)(2,1)S(1)} %get-tuple-element.34), channel_id=1, source_target_pairs={{0,8},{4,12},{8,0},{12,4},{1,9},{5,13},{9,1},{13,5},{2,10},{6,14},... | collective-permute-start | bytes 1572872 | tf_op jit(solution)/shard_map/ppermute | solution.py:343
  156.4 24.5 %collective-permute-start.19 = (bf16[1024,128]{1,0:T(8,128)(2,1)S(1)}, bf16[1024,128]{1,0:T(8,128)(2,1)S(1)}, u32[]{:S(2)}, u32[]{:S(2)}) collective-permute-start(bf16[1024,128]{1,0:T(8,128)(2,1)S(1)} %get-tuple-element.39), channel_id=1, source_target_pairs={{0,8},{4,12},{8,0},{12,4},{1,9},{5,13},{9,1},{13,5},{2,10},{6,14},... | collective-permute-start | bytes 786440 | tf_op jit(solution)/shard_map/ppermute | solution.py:343
  156.5 29.3 %collective-permute-start.20 = (bf16[1024,128]{1,0:T(8,128)(2,1)S(1)}, bf16[1024,128]{1,0:T(8,128)(2,1)S(1)}, u32[]{:S(2)}, u32[]{:S(2)}) collective-permute-start(bf16[1024,128]{1,0:T(8,128)(2,1)S(1)} %get-tuple-element.40), channel_id=1, source_target_pairs={{0,8},{4,12},{8,0},{12,4},{1,9},{5,13},{9,1},{13,5},{2,10},{6,14},... | collective-permute-start | bytes 786440 | tf_op jit(solution)/shard_map/ppermute | solution.py:343

commit v6 on v5

--- a/solution.py
+++ b/solution.py
@@ -10,6 +10,7 @@
 BLOCK = 128
 STRETCH = 256
 CHUNKS = (2, 2, 2, 2)
+LAST = 4
 LAG = 2
 
 ANY = pl.BlockSpec(memory_space=pl.ANY)
@@ -89,7 +90,9 @@
 
         @pl.when(me >= stride)
         def _():
-            gather(decoder_ref, range(sizes[0]), [out_ref], sizes, sem)
+            copy = pltpu.make_async_copy(decoder_ref.at[:, pl.ds(0, sizes[0] * BLOCK)], out_ref, sem.at[0])
+            copy.start()
+            copy.wait()
 
         @pl.when(me < stride)
         def _():
@@ -218,11 +221,18 @@
             a, b, c, d = (part[j] for part in parts)
             total = (a + b) + (c + d)
             final_t[j] = tangents(final_x[j], total[0], total[1], scale_ref[0, start + j])
-            returned = column(send_outs[0], j) if len(send_outs) == 1 else send_outs[j]
-            for target, half in ((column(out_ref, place_ref[0, start + j]), 0), (returned, 1)):
+            everything = (0, final_t.shape[1])
+            targets = [(column(out_ref, place_ref[0, start + j]), 0, everything)]
+            if spec["pieces"]:
+                targets += [
+                    (out, BLOCK, rows) for out, (block, rows) in zip(send_outs, spec["pieces"]) if block == j
+                ]
+            else:
+                targets.append((column(send_outs[0], j), BLOCK, everything))
+            for target, side, rows in targets:
                 stores.append(
                     pltpu.make_async_copy(
-                        final_t.at[j, :, pl.ds(half * BLOCK, BLOCK)], target, store_sem.at[len(stores)]
+                        final_t.at[j, pl.ds(*rows), pl.ds(side, BLOCK)], target, store_sem.at[len(stores)]
                     )
                 )
                 stores[-1].start()
@@ -271,6 +281,9 @@
     )(stretch_blocks.T, stretch_weight, decoder, first)
 
     sends = [lax.ppermute(part, "outer", to_first) for part in [first] + raw]
+    last = width // LAST
+    pieces = [(j, (0, width)) for j in range(sizes[-1] - 1)]
+    pieces += [(sizes[-1] - 1, (0, width - last)), (sizes[-1] - 1, (width - last, last))]
     parts = {}
     out = chain = None
     for step in range(2 * count - 1):
@@ -294,11 +307,11 @@
             args, specs = args + [sends[turn]] + parts.pop(turn), specs + [ANY] + [VMEM] * ranks
         if back:
             args, specs = args + [arrived], specs + [ANY]
-        spec["sends"] = int(bool(final or pack))
+        spec["sends"], spec["pieces"] = int(bool(final or pack)), None
         if turn == count - 1:
-            spec["sends"] = sizes[turn]
-            shapes += [jax.ShapeDtypeStruct((width, BLOCK), decoder.dtype)] * sizes[turn]
-            out_specs += [ANY] * sizes[turn]
+            spec["sends"], spec["pieces"] = len(pieces), pieces
+            shapes += [jax.ShapeDtypeStruct((size, BLOCK), decoder.dtype) for _, (_, size) in pieces]
+            out_specs += [ANY] * len(pieces)
         elif final or pack:
             shapes.append(array(turn if final else step + LAG))
             out_specs.append(ANY)
@@ -328,7 +341,7 @@
                     pltpu.VMEM((slot, width, STRETCH), decoder.dtype),
                     pltpu.SemaphoreType.DMA((2 * slot, 2)),
                     pltpu.SemaphoreType.DMA((2 * slot,)),
-                    pltpu.SemaphoreType.DMA((2 * slot,)),
+                    pltpu.SemaphoreType.DMA((2 * slot + 1,)),
                 ],
                 compiler_params=pltpu.CompilerParams(vmem_limit_bytes=32 * 2**20),
                 name="step",
@@ -343,8 +356,8 @@
             sends.append(lax.ppermute(results.pop(0), "outer", to_second if final else to_first))
         if final or back:
             out = results.pop(0)
-    for j in range(sizes[-1]):
-        out = lax.dynamic_update_slice(out, sends[j - sizes[-1]], (0, place[1, half - sizes[-1] + j] * BLOCK))
+    for piece, (block, rows) in zip(sends[-len(pieces) :], pieces):
+        out = lax.dynamic_update_slice(out, piece, (rows[0], place[1, starts[-1] + block] * BLOCK))
     return out
 
 

time: 187 us -> 187 us (level)
    ppermute x7 -> x8, waiting for transfers between devices: 87.7 us -> 86.6 us  [shards(): lax.ppermute(results.pop(0), 'outer', to_second if final else to_first)]
  transfers between devices with their start and end apart: 21 -> 22, of which waited for: 9 -> 9; matrix products, arithmetic and copies ran while one was open for 1% -> 1% of each run, Pallas kernels for 14% -> 14%
where the time goes in v6:
time: 187 us; the launch traced here: 186 us
  waiting for transfers between devices  135 us (72%)
  Pallas kernels  28 us (15%)
  starting transfers between devices  18.7 us (10%)
  local copies, waits for them, and re-layouts  2.71 us (1%)
    ppermute x8, waiting for transfers between devices, shards(): lax.ppermute(results.pop(0), 'outer', to_second if final else to_first)  86.6 us
    ppermute x2, waiting for transfers between devices, shards(): sends = [lax.ppermute(part, 'outer', to_first) for part in [first] + raw]  48.7 us
    pallas_call x7, Pallas kernels, shards(): pl.pallas_call(functools.partial(step_kernel, spec), out_shape=shapes, in...  22.9 us
    ppermute x12, starting transfers between devices, shards(): lax.ppermute(mine, 'inner', [(i, i ^ hop) for i in range(ranks)])  11.9 us
  transfers between devices with their start and end apart: 22, of which 9 were waited for; matrix products, arithmetic and copies ran while one was open for 1% of the time, Pallas kernels for 14%

profile of v6, /device:TPU:0, one launch (start us, length us, event | category | flops | bytes accessed | tf_op | source)
XLA Modules:
  0.0 186.4 jit_solution(11120245942830009358)
XLA Ops:
  0.0 2.0 %opening.1.first_ref = bf16[1024,256]{1,0:T(8,128)(2,1)S(1)} custom-call(s32[2,32]{1,0:T(2,128)} %bitcast.3, bf16[1024,2048]{1,0:T(8,128)(2,1)} %refs_2_.11), custom_call_target="tpu_custom_call" | custom-call | tf_op jit(solution)/shard_map/opening/pallas_call | solution.py:260
  2.0 3.2 %collective-permute-start = (bf16[1024,256]{1,0:T(8,128)(2,1)S(1)}, bf16[1024,256]{1,0:T(8,128)(2,1)S(1)}, u32[]{:S(2)}, u32[]{:S(2)}) collective-permute-start(bf16[1024,256]{1,0:T(8,128)(2,1)S(1)} %opening.1.first_ref), channel_id=1, source_target_pairs={{0,8},{4,12},{8,0},{12,4},{1,9},{5,13},{9,1},{13,5},{2,10},{6,14},... | collective-permute-start | bytes 1572872 | tf_op jit(solution)/shard_map/ppermute | solution.py:283
  5.2 3.2 %planning.1 = (s32[2,9]{1,0:T(2,128)S(1)}, f32[1,9]{1,0:T(1,128)S(1)}, bf16[1024,256]{1,0:T(8,128)(2,1)S(1)}) custom-call(s32[2,32]{1,0:T(2,128)S(1)} %bitcast.4, f32[32]{0:T(128)S(1)} %copy-done.1, bf16[1024,2048]{1,0:T(8,128)(2,1)} %refs_2_.11, bf16[1024,256]{1,0:T(8,128)(2,1)S(1)} %opening.1.first_ref), custom_call_target="tpu_custom_call" | custom-call | tf_op jit(solution)/shard_map/planning/pallas_call | solution.py:269
  8.5 31.9 %collective-permute-done.refs_3_.refs_4_ = bf16[1024,256]{1,0:T(8,128)(2,1)S(1)} collective-permute-done((bf16[1024,256]{1,0:T(8,128)(2,1)S(1)}, bf16[1024,256]{1,0:T(8,128)(2,1)S(1)}, u32[]{:S(2)}, u32[]{:S(2)}) %collective-permute-start) | collective-permute-done | bytes 524320 | tf_op jit(solution)/shard_map/ppermute | solution.py:283
  40.4 2.6 %step.7 = (f32[2,2,128,128]{3,2,1,0:T(8,128)S(1)}, bf16[1024,256]{1,0:T(8,128)(2,1)S(1)}) custom-call(s32[2,9]{1,0:T(2,128)S(1)} %get-tuple-element.24.refs_0_, f32[1,9]{1,0:T(1,128)S(1)} %get-tuple-element.25.refs_1_, bf16[1024,2048]{1,0:T(8,128)(2,1)} %refs_2_.11, bf16[1024,256]{1,0:T(8,128)(2,1)S(1)} %collective-permute-done.refs_3_.refs_4_), custom_call_target="tpu_custom_call" | custom-call | tf_op jit(solution)/shard_map/step/pallas_call | solution.py:330
  43.2 2.8 %collective-permute-start.3 = (f32[2,2,128,128]{3,2,1,0:T(8,128)S(1)}, f32[2,2,128,128]{3,2,1,0:T(8,128)S(1)}, u32[]{:S(2)}, u32[]{:S(2)}) collective-permute-start(f32[2,2,128,128]{3,2,1,0:T(8,128)S(1)} %get-tuple-element.27.refs_4_.refs_5_), channel_id=1, source_target_pairs={{0,2},{1,3},{2,0},{3,1},{4,6},{5,7},{6,4},{7,5},{8,10},{9,11},{10,... | collective-permute-start | bytes 786440 | tf_op jit(solution)/shard_map/ppermute | solution.py:353
  46.1 16.8 %collective-permute-done.5.refs_3_.refs_4_ = bf16[1024,256]{1,0:T(8,128)(2,1)S(1)} collective-permute-done((bf16[1024,256]{1,0:T(8,128)(2,1)S(1)}, bf16[1024,256]{1,0:T(8,128)(2,1)S(1)}, u32[]{:S(2)}, u32[]{:S(2)}) %collective-permute-start.5) | collective-permute-done | bytes 524320 | tf_op jit(solution)/shard_map/ppermute | solution.py:283
  62.9 2.6 %step.8 = (f32[2,2,128,128]{3,2,1,0:T(8,128)S(1)}, bf16[1024,256]{1,0:T(8,128)(2,1)S(1)}) custom-call(s32[2,9]{1,0:T(2,128)S(1)} %get-tuple-element.24.refs_0_, f32[1,9]{1,0:T(1,128)S(1)} %get-tuple-element.25.refs_1_, bf16[1024,2048]{1,0:T(8,128)(2,1)} %refs_2_.11, bf16[1024,256]{1,0:T(8,128)(2,1)S(1)} %collective-permute-done.5.refs_3_.refs_4_, ...), custom_call_target="tpu_custom_call" | custom-call | tf_op jit(solution)/shard_map/step/pallas_call | solution.py:330
  65.7 2.8 %collective-permute-start.12 = (f32[2,2,128,128]{3,2,1,0:T(8,128)S(1)}, f32[2,2,128,128]{3,2,1,0:T(8,128)S(1)}, u32[]{:S(2)}, u32[]{:S(2)}) collective-permute-start(f32[2,2,128,128]{3,2,1,0:T(8,128)S(1)} %get-tuple-element.29.refs_9_.refs_5_), channel_id=1, source_target_pairs={{0,2},{1,3},{2,0},{3,1},{4,6},{5,7},{6,4},{7,5},{8,10},{9,11},{10,... | collective-permute-start | bytes 786440 | tf_op jit(solution)/shard_map/ppermute | solution.py:353
  68.5 0.1 collective-permute-start.13
  68.6 16.7 %collective-permute-done.1.refs_3_ = bf16[1024,256]{1,0:T(8,128)(2,1)S(1)} collective-permute-done((bf16[1024,256]{1,0:T(8,128)(2,1)S(1)}, bf16[1024,256]{1,0:T(8,128)(2,1)S(1)}, u32[]{:S(2)}, u32[]{:S(2)}) %collective-permute-start.1) | collective-permute-done | bytes 524320 | tf_op jit(solution)/shard_map/ppermute | solution.py:356
  85.3 4.5 %step.9 = (f32[2,2,128,128]{3,2,1,0:T(8,128)S(1)}, bf16[1024,256]{1,0:T(8,128)(2,1)S(1)}, bf16[1024,2048]{1,0:T(8,128)(2,1)}) custom-call(s32[2,9]{1,0:T(2,128)S(1)} %get-tuple-element.24.refs_0_, f32[1,9]{1,0:T(1,128)S(1)} %get-tuple-element.25.refs_1_, bf16[1024,2048]{1,0:T(8,128)(2,1)} %refs_2_.11, bf16[1024,256]{1,0:T(8,128)(2,1)S(1)} %collective-permute-done.1.refs_3_, ...), custom_call_target="tpu_custom_call" | custom-call | tf_op jit(solution)/shard_map/step/pallas_call | solution.py:330
  90.0 2.8 %collective-permute-start.7 = (f32[2,2,128,128]{3,2,1,0:T(8,128)S(1)}, f32[2,2,128,128]{3,2,1,0:T(8,128)S(1)}, u32[]{:S(2)}, u32[]{:S(2)}) collective-permute-start(f32[2,2,128,128]{3,2,1,0:T(8,128)S(1)} %get-tuple-element.30.refs_4_), channel_id=1, source_target_pairs={{0,2},{1,3},{2,0},{3,1},{4,6},{5,7},{6,4},{7,5},{8,10},{9,11},{10,... | collective-permute-start | bytes 786440 | tf_op jit(solution)/shard_map/ppermute | solution.py:353
  92.8 0.1 collective-permute-start.8
  93.0 14.8 %collective-permute-done.10.refs_3_ = bf16[1024,256]{1,0:T(8,128)(2,1)S(1)} collective-permute-done((bf16[1024,256]{1,0:T(8,128)(2,1)S(1)}, bf16[1024,256]{1,0:T(8,128)(2,1)S(1)}, u32[]{:S(2)}, u32[]{:S(2)}) %collective-permute-start.10) | collective-permute-done | bytes 524320 | tf_op jit(solution)/shard_map/ppermute | solution.py:356
  107.8 4.5 %step.10 = (f32[2,2,128,128]{3,2,1,0:T(8,128)S(1)}, bf16[1024,256]{1,0:T(8,128)(2,1)S(1)}, bf16[1024,2048]{1,0:T(8,128)(2,1)}) custom-call(s32[2,9]{1,0:T(2,128)S(1)} %get-tuple-element.24.refs_0_, f32[1,9]{1,0:T(1,128)S(1)} %get-tuple-element.25.refs_1_, bf16[1024,2048]{1,0:T(8,128)(2,1)} %refs_2_.11, ...), custom_call_target="tpu_custom_call", output_to_operand_aliasing={{2}: (9, {})} | custom-call | tf_op jit(solution)/shard_map/step/pallas_call | solution.py:330
  112.5 2.8 %collective-permute-start.16 = (f32[2,2,128,128]{3,2,1,0:T(8,128)S(1)}, f32[2,2,128,128]{3,2,1,0:T(8,128)S(1)}, u32[]{:S(2)}, u32[]{:S(2)}) collective-permute-start(f32[2,2,128,128]{3,2,1,0:T(8,128)S(1)} %get-tuple-element.36.refs_4_), channel_id=1, source_target_pairs={{0,2},{1,3},{2,0},{3,1},{4,6},{5,7},{6,4},{7,5},{8,10},{9,11},{10,... | collective-permute-start | bytes 786440 | tf_op jit(solution)/shard_map/ppermute | solution.py:353
  115.3 0.1 collective-permute-start.17
  115.4 14.8 %collective-permute-done.9.refs_8_ = bf16[1024,256]{1,0:T(8,128)(2,1)S(1)} collective-permute-done((bf16[1024,256]{1,0:T(8,128)(2,1)S(1)}, bf16[1024,256]{1,0:T(8,128)(2,1)S(1)}, u32[]{:S(2)}, u32[]{:S(2)}) %collective-permute-start.9) | collective-permute-done | bytes 524320 | tf_op jit(solution)/shard_map/ppermute | solution.py:356
  130.3 3.6 %step.11 = (bf16[1024,256]{1,0:T(8,128)(2,1)S(1)}, bf16[1024,2048]{1,0:T(8,128)(2,1)}) custom-call(s32[2,9]{1,0:T(2,128)S(1)} %get-tuple-element.24.refs_0_, f32[1,9]{1,0:T(1,128)S(1)} %get-tuple-element.25.refs_1_, bf16[1024,2048]{1,0:T(8,128)(2,1)} %refs_2_.11, ...), custom_call_target="tpu_custom_call", output_to_operand_aliasing={{1}: (9, {})} | custom-call | tf_op jit(solution)/shard_map/step/pallas_call | solution.py:330
  134.0 18.7 %collective-permute-done.18.refs_8_ = bf16[1024,256]{1,0:T(8,128)(2,1)S(1)} collective-permute-done((bf16[1024,256]{1,0:T(8,128)(2,1)S(1)}, bf16[1024,256]{1,0:T(8,128)(2,1)S(1)}, u32[]{:S(2)}, u32[]{:S(2)}) %collective-permute-start.18) | collective-permute-done | bytes 524320 | tf_op jit(solution)/shard_map/ppermute | solution.py:356
  152.8 3.6 %step.12 = (bf16[1024,128]{1,0:T(8,128)(2,1)S(1)}, bf16[768,128]{1,0:T(8,128)(2,1)S(1)}, bf16[256,128]{1,0:T(8,128)(2,1)S(1)}, bf16[1024,2048]{1,0:T(8,128)(2,1)}) custom-call(s32[2,9]{1,0:T(2,128)S(1)} %get-tuple-element.24.refs_0_, f32[1,9]{1,0:T(1,128)S(1)} %get-tuple-element.25.refs_1_, ...), custom_call_target="tpu_custom_call", output_to_operand_aliasing={{3}: (9, {})} | custom-call | tf_op jit(solution)/shard_map/step/pallas_call | solution.py:330
  156.4 2.9 %collective-permute-start.20 = (bf16[768,128]{1,0:T(8,128)(2,1)S(1)}, bf16[768,128]{1,0:T(8,128)(2,1)S(1)}, u32[]{:S(2)}, u32[]{:S(2)}) collective-permute-start(bf16[768,128]{1,0:T(8,128)(2,1)S(1)} %get-tuple-element.41), channel_id=1, source_target_pairs={{0,8},{4,12},{8,0},{12,4},{1,9},{5,13},{9,1},{13,5},{2,10},{6,14},... | collective-permute-start | bytes 589832 | tf_op jit(solution)/shard_map/ppermute | solution.py:356
  159.4 0.7 fusion
  161.4 0.1 collective-permute-start.21
  161.5 13.7 %collective-permute-done.14.refs_1_ = bf16[1024,256]{1,0:T(8,128)(2,1)S(1)} collective-permute-done((bf16[1024,256]{1,0:T(8,128)(2,1)S(1)}, bf16[1024,256]{1,0:T(8,128)(2,1)S(1)}, u32[]{:S(2)}, u32[]{:S(2)}) %collective-permute-start.14) | collective-permute-done | bytes 524320 | tf_op jit(solution)/shard_map/ppermute | solution.py:356
  175.2 1.4 step.13
  176.6 4.2 %collective-permute-done.19 = bf16[1024,128]{1,0:T(8,128)(2,1)S(1)} collective-permute-done((bf16[1024,128]{1,0:T(8,128)(2,1)S(1)}, bf16[1024,128]{1,0:T(8,128)(2,1)S(1)}, u32[]{:S(2)}, u32[]{:S(2)}) %collective-permute-start.19) | collective-permute-done | bytes 262176 | tf_op jit(solution)/shard_map/ppermute | solution.py:356
  180.8 0.7 constant_dynamic-update-slice_fusion.2
  181.6 3.5 %collective-permute-done.20 = bf16[768,128]{1,0:T(8,128)(2,1)S(1)} collective-permute-done((bf16[768,128]{1,0:T(8,128)(2,1)S(1)}, bf16[768,128]{1,0:T(8,128)(2,1)S(1)}, u32[]{:S(2)}, u32[]{:S(2)}) %collective-permute-start.20) | collective-permute-done | bytes 196640 | tf_op jit(solution)/shard_map/ppermute | solution.py:356
  185.1 0.7 constant_dynamic-update-slice_fusion.1
  185.8 0.6 constant_dynamic-update-slice_fusion
  (29 shorter events, 0.9 us)
Async XLA Ops:
  0.0 5.2 %copy-start = (s32[32,2]{0,1:T(2,128)S(1)}, s32[32,2]{0,1:T(2,128)}, u32[]{:S(2)}) copy-start(s32[32,2]{0,1:T(2,128)} %param.4) | copy-start | bytes 772
  0.0 5.2 %copy-start.1 = (f32[32]{0:T(128)S(1)}, f32[32]{0:T(128)}, u32[]{:S(2)}) copy-start(f32[32]{0:T(128)} %weight_ref.1) | copy-start | bytes 388
  2.0 38.4 %collective-permute-start = (bf16[1024,256]{1,0:T(8,128)(2,1)S(1)}, bf16[1024,256]{1,0:T(8,128)(2,1)S(1)}, u32[]{:S(2)}, u32[]{:S(2)}) collective-permute-start(bf16[1024,256]{1,0:T(8,128)(2,1)S(1)} %opening.1.first_ref), channel_id=1, source_target_pairs={{0,8},{4,12},{8,0},{12,4},{1,9},{5,13},{9,1},{13,5},{2,10},{6,14},... | collective-permute-start | bytes 1572872 | tf_op jit(solution)/shard_map/ppermute | solution.py:283
  8.4 54.5 %collective-permute-start.5 = (bf16[1024,256]{1,0:T(8,128)(2,1)S(1)}, bf16[1024,256]{1,0:T(8,128)(2,1)S(1)}, u32[]{:S(2)}, u32[]{:S(2)}) collective-permute-start(bf16[1024,256]{1,0:T(8,128)(2,1)S(1)} %get-tuple-element.28), channel_id=1, source_target_pairs={{0,8},{4,12},{8,0},{12,4},{1,9},{5,13},{9,1},{13,5},{2,10},{6,14},... | collective-permute-start | bytes 1572872 | tf_op jit(solution)/shard_map/ppermute | solution.py:283
  43.0 42.3 %collective-permute-start.1 = (bf16[1024,256]{1,0:T(8,128)(2,1)S(1)}, bf16[1024,256]{1,0:T(8,128)(2,1)S(1)}, u32[]{:S(2)}, u32[]{:S(2)}) collective-permute-start(bf16[1024,256]{1,0:T(8,128)(2,1)S(1)} %get-tuple-element.26), channel_id=1, source_target_pairs={{0,8},{4,12},{8,0},{12,4},{1,9},{5,13},{9,1},{13,5},{2,10},{6,14},... | collective-permute-start | bytes 1572872 | tf_op jit(solution)/shard_map/ppermute | solution.py:356
  43.1 22.5 %collective-permute-start.2 = (f32[2,2,128,128]{3,2,1,0:T(8,128)S(1)}, f32[2,2,128,128]{3,2,1,0:T(8,128)S(1)}, u32[]{:S(2)}, u32[]{:S(2)}) collective-permute-start(f32[2,2,128,128]{3,2,1,0:T(8,128)S(1)} %get-tuple-element.27.refs_4_.refs_5_), channel_id=1, source_target_pairs={{0,1},{1,0},{2,3},{3,2},{4,5},{5,4},{6,7},{7,6},{8,9},{9,8},{10,11... | collective-permute-start | bytes 786440 | tf_op jit(solution)/shard_map/ppermute | solution.py:353
  43.2 22.5 %collective-permute-start.3 = (f32[2,2,128,128]{3,2,1,0:T(8,128)S(1)}, f32[2,2,128,128]{3,2,1,0:T(8,128)S(1)}, u32[]{:S(2)}, u32[]{:S(2)}) collective-permute-start(f32[2,2,128,128]{3,2,1,0:T(8,128)S(1)} %get-tuple-element.27.refs_4_.refs_5_), channel_id=1, source_target_pairs={{0,2},{1,3},{2,0},{3,1},{4,6},{5,7},{6,4},{7,5},{8,10},{9,11},{10,... | collective-permute-start | bytes 786440 | tf_op jit(solution)/shard_map/ppermute | solution.py:353
  46.0 22.5 %collective-permute-start.4 = (f32[2,2,128,128]{3,2,1,0:T(8,128)S(1)}, f32[2,2,128,128]{3,2,1,0:T(8,128)S(1)}, u32[]{:S(2)}, u32[]{:S(2)}) collective-permute-start(f32[2,2,128,128]{3,2,1,0:T(8,128)S(1)} %get-tuple-element.27.refs_4_.refs_5_), channel_id=1, source_target_pairs={{0,3},{1,2},{2,1},{3,0},{4,7},{5,6},{6,5},{7,4},{8,11},{9,10},{10,... | collective-permute-start | bytes 786440 | tf_op jit(solution)/shard_map/ppermute | solution.py:353
  65.5 42.3 %collective-permute-start.10 = (bf16[1024,256]{1,0:T(8,128)(2,1)S(1)}, bf16[1024,256]{1,0:T(8,128)(2,1)S(1)}, u32[]{:S(2)}, u32[]{:S(2)}) collective-permute-start(bf16[1024,256]{1,0:T(8,128)(2,1)S(1)} %get-tuple-element.32), channel_id=1, source_target_pairs={{0,8},{4,12},{8,0},{12,4},{1,9},{5,13},{9,1},{13,5},{2,10},{6,14},... | collective-permute-start | bytes 1572872 | tf_op jit(solution)/shard_map/ppermute | solution.py:356
  65.6 24.3 %collective-permute-start.11 = (f32[2,2,128,128]{3,2,1,0:T(8,128)S(1)}, f32[2,2,128,128]{3,2,1,0:T(8,128)S(1)}, u32[]{:S(2)}, u32[]{:S(2)}) collective-permute-start(f32[2,2,128,128]{3,2,1,0:T(8,128)S(1)} %get-tuple-element.29.refs_9_.refs_5_), channel_id=1, source_target_pairs={{0,1},{1,0},{2,3},{3,2},{4,5},{5,4},{6,7},{7,6},{8,9},{9,8},{10,11... | collective-permute-start | bytes 786440 | tf_op jit(solution)/shard_map/ppermute | solution.py:353
  65.7 24.3 %collective-permute-start.12 = (f32[2,2,128,128]{3,2,1,0:T(8,128)S(1)}, f32[2,2,128,128]{3,2,1,0:T(8,128)S(1)}, u32[]{:S(2)}, u32[]{:S(2)}) collective-permute-start(f32[2,2,128,128]{3,2,1,0:T(8,128)S(1)} %get-tuple-element.29.refs_9_.refs_5_), channel_id=1, source_target_pairs={{0,2},{1,3},{2,0},{3,1},{4,6},{5,7},{6,4},{7,5},{8,10},{9,11},{10,... | collective-permute-start | bytes 786440 | tf_op jit(solution)/shard_map/ppermute | solution.py:353
  68.5 24.3 %collective-permute-start.13 = (f32[2,2,128,128]{3,2,1,0:T(8,128)S(1)}, f32[2,2,128,128]{3,2,1,0:T(8,128)S(1)}, u32[]{:S(2)}, u32[]{:S(2)}) collective-permute-start(f32[2,2,128,128]{3,2,1,0:T(8,128)S(1)} %get-tuple-element.29.refs_9_.refs_5_), channel_id=1, source_target_pairs={{0,3},{1,2},{2,1},{3,0},{4,7},{5,6},{6,5},{7,4},{8,11},{9,10},{10,... | collective-permute-start | bytes 786440 | tf_op jit(solution)/shard_map/ppermute | solution.py:353
  89.9 40.4 %collective-permute-start.9 = (bf16[1024,256]{1,0:T(8,128)(2,1)S(1)}, bf16[1024,256]{1,0:T(8,128)(2,1)S(1)}, u32[]{:S(2)}, u32[]{:S(2)}) collective-permute-start(bf16[1024,256]{1,0:T(8,128)(2,1)S(1)} %get-tuple-element.31), channel_id=1, source_target_pairs={{0,8},{4,12},{8,0},{12,4},{1,9},{5,13},{9,1},{13,5},{2,10},{6,14},... | collective-permute-start | bytes 1572872 | tf_op jit(solution)/shard_map/ppermute | solution.py:356
  90.0 22.5 %collective-permute-start.6 = (f32[2,2,128,128]{3,2,1,0:T(8,128)S(1)}, f32[2,2,128,128]{3,2,1,0:T(8,128)S(1)}, u32[]{:S(2)}, u32[]{:S(2)}) collective-permute-start(f32[2,2,128,128]{3,2,1,0:T(8,128)S(1)} %get-tuple-element.30.refs_4_), channel_id=1, source_target_pairs={{0,1},{1,0},{2,3},{3,2},{4,5},{5,4},{6,7},{7,6},{8,9},{9,8},{10,11... | collective-permute-start | bytes 786440 | tf_op jit(solution)/shard_map/ppermute | solution.py:353
  90.0 22.5 %collective-permute-start.7 = (f32[2,2,128,128]{3,2,1,0:T(8,128)S(1)}, f32[2,2,128,128]{3,2,1,0:T(8,128)S(1)}, u32[]{:S(2)}, u32[]{:S(2)}) collective-permute-start(f32[2,2,128,128]{3,2,1,0:T(8,128)S(1)} %get-tuple-element.30.refs_4_), channel_id=1, source_target_pairs={{0,2},{1,3},{2,0},{3,1},{4,6},{5,7},{6,4},{7,5},{8,10},{9,11},{10,... | collective-permute-start | bytes 786440 | tf_op jit(solution)/shard_map/ppermute | solution.py:353
  92.8 22.5 %collective-permute-start.8 = (f32[2,2,128,128]{3,2,1,0:T(8,128)S(1)}, f32[2,2,128,128]{3,2,1,0:T(8,128)S(1)}, u32[]{:S(2)}, u32[]{:S(2)}) collective-permute-start(f32[2,2,128,128]{3,2,1,0:T(8,128)S(1)} %get-tuple-element.30.refs_4_), channel_id=1, source_target_pairs={{0,3},{1,2},{2,1},{3,0},{4,7},{5,6},{6,5},{7,4},{8,11},{9,10},{10,... | collective-permute-start | bytes 786440 | tf_op jit(solution)/shard_map/ppermute | solution.py:353
  112.3 40.4 %collective-permute-start.18 = (bf16[1024,256]{1,0:T(8,128)(2,1)S(1)}, bf16[1024,256]{1,0:T(8,128)(2,1)S(1)}, u32[]{:S(2)}, u32[]{:S(2)}) collective-permute-start(bf16[1024,256]{1,0:T(8,128)(2,1)S(1)} %get-tuple-element.37), channel_id=1, source_target_pairs={{0,8},{4,12},{8,0},{12,4},{1,9},{5,13},{9,1},{13,5},{2,10},{6,14},... | collective-permute-start | bytes 1572872 | tf_op jit(solution)/shard_map/ppermute | solution.py:356
  112.4 21.6 %collective-permute-start.15 = (f32[2,2,128,128]{3,2,1,0:T(8,128)S(1)}, f32[2,2,128,128]{3,2,1,0:T(8,128)S(1)}, u32[]{:S(2)}, u32[]{:S(2)}) collective-permute-start(f32[2,2,128,128]{3,2,1,0:T(8,128)S(1)} %get-tuple-element.36.refs_4_), channel_id=1, source_target_pairs={{0,1},{1,0},{2,3},{3,2},{4,5},{5,4},{6,7},{7,6},{8,9},{9,8},{10,11... | collective-permute-start | bytes 786440 | tf_op jit(solution)/shard_map/ppermute | solution.py:353
  112.5 21.5 %collective-permute-start.16 = (f32[2,2,128,128]{3,2,1,0:T(8,128)S(1)}, f32[2,2,128,128]{3,2,1,0:T(8,128)S(1)}, u32[]{:S(2)}, u32[]{:S(2)}) collective-permute-start(f32[2,2,128,128]{3,2,1,0:T(8,128)S(1)} %get-tuple-element.36.refs_4_), channel_id=1, source_target_pairs={{0,2},{1,3},{2,0},{3,1},{4,6},{5,7},{6,4},{7,5},{8,10},{9,11},{10,... | collective-permute-start | bytes 786440 | tf_op jit(solution)/shard_map/ppermute | solution.py:353
  115.3 18.7 %collective-permute-start.17 = (f32[2,2,128,128]{3,2,1,0:T(8,128)S(1)}, f32[2,2,128,128]{3,2,1,0:T(8,128)S(1)}, u32[]{:S(2)}, u32[]{:S(2)}) collective-permute-start(f32[2,2,128,128]{3,2,1,0:T(8,128)S(1)} %get-tuple-element.36.refs_4_), channel_id=1, source_target_pairs={{0,3},{1,2},{2,1},{3,0},{4,7},{5,6},{6,5},{7,4},{8,11},{9,10},{10,... | collective-permute-start | bytes 786440 | tf_op jit(solution)/shard_map/ppermute | solution.py:353
  133.9 41.3 %collective-permute-start.14 = (bf16[1024,256]{1,0:T(8,128)(2,1)S(1)}, bf16[1024,256]{1,0:T(8,128)(2,1)S(1)}, u32[]{:S(2)}, u32[]{:S(2)}) collective-permute-start(bf16[1024,256]{1,0:T(8,128)(2,1)S(1)} %get-tuple-element.35), channel_id=1, source_target_pairs={{0,8},{4,12},{8,0},{12,4},{1,9},{5,13},{9,1},{13,5},{2,10},{6,14},... | collective-permute-start | bytes 1572872 | tf_op jit(solution)/shard_map/ppermute | solution.py:356
  156.4 24.5 %collective-permute-start.19 = (bf16[1024,128]{1,0:T(8,128)(2,1)S(1)}, bf16[1024,128]{1,0:T(8,128)(2,1)S(1)}, u32[]{:S(2)}, u32[]{:S(2)}) collective-permute-start(bf16[1024,128]{1,0:T(8,128)(2,1)S(1)} %get-tuple-element.40), channel_id=1, source_target_pairs={{0,8},{4,12},{8,0},{12,4},{1,9},{5,13},{9,1},{13,5},{2,10},{6,14},... | collective-permute-start | bytes 786440 | tf_op jit(solution)/shard_map/ppermute | solution.py:356
  156.4 28.6 %collective-permute-start.20 = (bf16[768,128]{1,0:T(8,128)(2,1)S(1)}, bf16[768,128]{1,0:T(8,128)(2,1)S(1)}, u32[]{:S(2)}, u32[]{:S(2)}) collective-permute-start(bf16[768,128]{1,0:T(8,128)(2,1)S(1)} %get-tuple-element.41), channel_id=1, source_target_pairs={{0,8},{4,12},{8,0},{12,4},{1,9},{5,13},{9,1},{13,5},{2,10},{6,14},... | collective-permute-start | bytes 589832 | tf_op jit(solution)/shard_map/ppermute | solution.py:356
  161.4 24.4 %collective-permute-start.21 = (bf16[256,128]{1,0:T(8,128)(2,1)S(1)}, bf16[256,128]{1,0:T(8,128)(2,1)S(1)}, u32[]{:S(2)}, u32[]{:S(2)}) collective-permute-start(bf16[256,128]{1,0:T(8,128)(2,1)S(1)} %get-tuple-element.42), channel_id=1, source_target_pairs={{0,8},{4,12},{8,0},{12,4},{1,9},{5,13},{9,1},{13,5},{2,10},{6,14},... | collective-permute-start | bytes 196616 | tf_op jit(solution)/shard_map/ppermute | solution.py:356

commit v7 on v6

--- a/solution.py
+++ b/solution.py
@@ -278,7 +278,7 @@
         scratch_shapes=[pltpu.SemaphoreType.DMA((per_dev,))],
         compiler_params=pltpu.CompilerParams(vmem_limit_bytes=8 * 2**20),
         name="planning",
-    )(stretch_blocks.T, stretch_weight, decoder, first)
+    )(pairs, stay(stretch_weight), decoder, first)
 
     sends = [lax.ppermute(part, "outer", to_first) for part in [first] + raw]
     last = width // LAST

time: 187 us -> 187 us (level)
  no operation moved by 1% of the time
where the time goes in v7:
time: 187 us; the launch traced here: 186 us
  waiting for transfers between devices  136 us (73%)
  Pallas kernels  28 us (15%)
  starting transfers between devices  18.3 us (10%)
  local copies, waits for them, and re-layouts  2.71 us (1%)
    ppermute x8, waiting for transfers between devices, shards(): lax.ppermute(results.pop(0), 'outer', to_second if final else to_first)  86.8 us
    ppermute x2, waiting for transfers between devices, shards(): sends = [lax.ppermute(part, 'outer', to_first) for part in [first] + raw]  48.8 us
    pallas_call x7, Pallas kernels, shards(): pl.pallas_call(functools.partial(step_kernel, spec), out_shape=shapes, in...  22.9 us
    ppermute x12, starting transfers between devices, shards(): lax.ppermute(mine, 'inner', [(i, i ^ hop) for i in range(ranks)])  11.4 us
  transfers between devices with their start and end apart: 22, of which 9 were waited for; matrix products, arithmetic and copies ran while one was open for 1% of the time, Pallas kernels for 14%

profile of v7, /device:TPU:0, one launch (start us, length us, event | category | flops | bytes accessed | tf_op | source)
XLA Modules:
  0.0 186.3 jit_solution(16820673078431700913)
XLA Ops:
  0.0 1.8 opening.1.first_ref
  1.8 3.3 %collective-permute-start = (bf16[1024,256]{1,0:T(8,128)(2,1)S(1)}, bf16[1024,256]{1,0:T(8,128)(2,1)S(1)}, u32[]{:S(2)}, u32[]{:S(2)}) collective-permute-start(bf16[1024,256]{1,0:T(8,128)(2,1)S(1)} %opening.1.first_ref), channel_id=1, source_target_pairs={{0,8},{4,12},{8,0},{12,4},{1,9},{5,13},{9,1},{13,5},{2,10},{6,14},... | collective-permute-start | bytes 1572872 | tf_op jit(solution)/shard_map/ppermute | solution.py:283
  5.2 3.3 %planning.1 = (s32[2,9]{1,0:T(2,128)S(1)}, f32[1,9]{1,0:T(1,128)S(1)}, bf16[1024,256]{1,0:T(8,128)(2,1)S(1)}) custom-call(s32[2,32]{1,0:T(2,128)} %bitcast.4, f32[32]{0:T(128)} %weight_ref.1, bf16[1024,2048]{1,0:T(8,128)(2,1)} %refs_2_.11, bf16[1024,256]{1,0:T(8,128)(2,1)S(1)} %opening.1.first_ref), custom_call_target="tpu_custom_call" | custom-call | tf_op jit(solution)/shard_map/planning/pallas_call | solution.py:269
  8.6 31.8 %collective-permute-done.refs_3_.refs_4_ = bf16[1024,256]{1,0:T(8,128)(2,1)S(1)} collective-permute-done((bf16[1024,256]{1,0:T(8,128)(2,1)S(1)}, bf16[1024,256]{1,0:T(8,128)(2,1)S(1)}, u32[]{:S(2)}, u32[]{:S(2)}) %collective-permute-start) | collective-permute-done | bytes 524320 | tf_op jit(solution)/shard_map/ppermute | solution.py:283
  40.4 2.6 %step.7 = (f32[2,2,128,128]{3,2,1,0:T(8,128)S(1)}, bf16[1024,256]{1,0:T(8,128)(2,1)S(1)}) custom-call(s32[2,9]{1,0:T(2,128)S(1)} %get-tuple-element.24.refs_0_, f32[1,9]{1,0:T(1,128)S(1)} %get-tuple-element.25.refs_1_, bf16[1024,2048]{1,0:T(8,128)(2,1)} %refs_2_.11, bf16[1024,256]{1,0:T(8,128)(2,1)S(1)} %collective-permute-done.refs_3_.refs_4_), custom_call_target="tpu_custom_call" | custom-call | tf_op jit(solution)/shard_map/step/pallas_call | solution.py:330
  43.2 2.7 %collective-permute-start.3 = (f32[2,2,128,128]{3,2,1,0:T(8,128)S(1)}, f32[2,2,128,128]{3,2,1,0:T(8,128)S(1)}, u32[]{:S(2)}, u32[]{:S(2)}) collective-permute-start(f32[2,2,128,128]{3,2,1,0:T(8,128)S(1)} %get-tuple-element.27.refs_4_.refs_5_), channel_id=1, source_target_pairs={{0,2},{1,3},{2,0},{3,1},{4,6},{5,7},{6,4},{7,5},{8,10},{9,11},{10,... | collective-permute-start | bytes 786440 | tf_op jit(solution)/shard_map/ppermute | solution.py:353
  45.9 16.9 %collective-permute-done.5.refs_3_.refs_4_ = bf16[1024,256]{1,0:T(8,128)(2,1)S(1)} collective-permute-done((bf16[1024,256]{1,0:T(8,128)(2,1)S(1)}, bf16[1024,256]{1,0:T(8,128)(2,1)S(1)}, u32[]{:S(2)}, u32[]{:S(2)}) %collective-permute-start.5) | collective-permute-done | bytes 524320 | tf_op jit(solution)/shard_map/ppermute | solution.py:283
  62.9 2.6 %step.8 = (f32[2,2,128,128]{3,2,1,0:T(8,128)S(1)}, bf16[1024,256]{1,0:T(8,128)(2,1)S(1)}) custom-call(s32[2,9]{1,0:T(2,128)S(1)} %get-tuple-element.24.refs_0_, f32[1,9]{1,0:T(1,128)S(1)} %get-tuple-element.25.refs_1_, bf16[1024,2048]{1,0:T(8,128)(2,1)} %refs_2_.11, bf16[1024,256]{1,0:T(8,128)(2,1)S(1)} %collective-permute-done.5.refs_3_.refs_4_, ...), custom_call_target="tpu_custom_call" | custom-call | tf_op jit(solution)/shard_map/step/pallas_call | solution.py:330
  65.7 2.7 %collective-permute-start.12 = (f32[2,2,128,128]{3,2,1,0:T(8,128)S(1)}, f32[2,2,128,128]{3,2,1,0:T(8,128)S(1)}, u32[]{:S(2)}, u32[]{:S(2)}) collective-permute-start(f32[2,2,128,128]{3,2,1,0:T(8,128)S(1)} %get-tuple-element.29.refs_9_.refs_5_), channel_id=1, source_target_pairs={{0,2},{1,3},{2,0},{3,1},{4,6},{5,7},{6,4},{7,5},{8,10},{9,11},{10,... | collective-permute-start | bytes 786440 | tf_op jit(solution)/shard_map/ppermute | solution.py:353
  68.4 0.1 collective-permute-start.13
  68.5 16.8 %collective-permute-done.1.refs_3_ = bf16[1024,256]{1,0:T(8,128)(2,1)S(1)} collective-permute-done((bf16[1024,256]{1,0:T(8,128)(2,1)S(1)}, bf16[1024,256]{1,0:T(8,128)(2,1)S(1)}, u32[]{:S(2)}, u32[]{:S(2)}) %collective-permute-start.1) | collective-permute-done | bytes 524320 | tf_op jit(solution)/shard_map/ppermute | solution.py:356
  85.3 4.5 %step.9 = (f32[2,2,128,128]{3,2,1,0:T(8,128)S(1)}, bf16[1024,256]{1,0:T(8,128)(2,1)S(1)}, bf16[1024,2048]{1,0:T(8,128)(2,1)}) custom-call(s32[2,9]{1,0:T(2,128)S(1)} %get-tuple-element.24.refs_0_, f32[1,9]{1,0:T(1,128)S(1)} %get-tuple-element.25.refs_1_, bf16[1024,2048]{1,0:T(8,128)(2,1)} %refs_2_.11, bf16[1024,256]{1,0:T(8,128)(2,1)S(1)} %collective-permute-done.1.refs_3_, ...), custom_call_target="tpu_custom_call" | custom-call | tf_op jit(solution)/shard_map/step/pallas_call | solution.py:330
  90.0 2.7 %collective-permute-start.7 = (f32[2,2,128,128]{3,2,1,0:T(8,128)S(1)}, f32[2,2,128,128]{3,2,1,0:T(8,128)S(1)}, u32[]{:S(2)}, u32[]{:S(2)}) collective-permute-start(f32[2,2,128,128]{3,2,1,0:T(8,128)S(1)} %get-tuple-element.30.refs_4_), channel_id=1, source_target_pairs={{0,2},{1,3},{2,0},{3,1},{4,6},{5,7},{6,4},{7,5},{8,10},{9,11},{10,... | collective-permute-start | bytes 786440 | tf_op jit(solution)/shard_map/ppermute | solution.py:353
  92.7 0.1 collective-permute-start.8
  92.8 15.0 %collective-permute-done.10.refs_3_ = bf16[1024,256]{1,0:T(8,128)(2,1)S(1)} collective-permute-done((bf16[1024,256]{1,0:T(8,128)(2,1)S(1)}, bf16[1024,256]{1,0:T(8,128)(2,1)S(1)}, u32[]{:S(2)}, u32[]{:S(2)}) %collective-permute-start.10) | collective-permute-done | bytes 524320 | tf_op jit(solution)/shard_map/ppermute | solution.py:356
  107.8 4.5 %step.10 = (f32[2,2,128,128]{3,2,1,0:T(8,128)S(1)}, bf16[1024,256]{1,0:T(8,128)(2,1)S(1)}, bf16[1024,2048]{1,0:T(8,128)(2,1)}) custom-call(s32[2,9]{1,0:T(2,128)S(1)} %get-tuple-element.24.refs_0_, f32[1,9]{1,0:T(1,128)S(1)} %get-tuple-element.25.refs_1_, bf16[1024,2048]{1,0:T(8,128)(2,1)} %refs_2_.11, ...), custom_call_target="tpu_custom_call", output_to_operand_aliasing={{2}: (9, {})} | custom-call | tf_op jit(solution)/shard_map/step/pallas_call | solution.py:330
  112.5 2.7 %collective-permute-start.16 = (f32[2,2,128,128]{3,2,1,0:T(8,128)S(1)}, f32[2,2,128,128]{3,2,1,0:T(8,128)S(1)}, u32[]{:S(2)}, u32[]{:S(2)}) collective-permute-start(f32[2,2,128,128]{3,2,1,0:T(8,128)S(1)} %get-tuple-element.36.refs_4_), channel_id=1, source_target_pairs={{0,2},{1,3},{2,0},{3,1},{4,6},{5,7},{6,4},{7,5},{8,10},{9,11},{10,... | collective-permute-start | bytes 786440 | tf_op jit(solution)/shard_map/ppermute | solution.py:353
  115.2 0.1 collective-permute-start.17
  115.3 15.0 %collective-permute-done.9.refs_8_ = bf16[1024,256]{1,0:T(8,128)(2,1)S(1)} collective-permute-done((bf16[1024,256]{1,0:T(8,128)(2,1)S(1)}, bf16[1024,256]{1,0:T(8,128)(2,1)S(1)}, u32[]{:S(2)}, u32[]{:S(2)}) %collective-permute-start.9) | collective-permute-done | bytes 524320 | tf_op jit(solution)/shard_map/ppermute | solution.py:356
  130.3 3.6 %step.11 = (bf16[1024,256]{1,0:T(8,128)(2,1)S(1)}, bf16[1024,2048]{1,0:T(8,128)(2,1)}) custom-call(s32[2,9]{1,0:T(2,128)S(1)} %get-tuple-element.24.refs_0_, f32[1,9]{1,0:T(1,128)S(1)} %get-tuple-element.25.refs_1_, bf16[1024,2048]{1,0:T(8,128)(2,1)} %refs_2_.11, ...), custom_call_target="tpu_custom_call", output_to_operand_aliasing={{1}: (9, {})} | custom-call | tf_op jit(solution)/shard_map/step/pallas_call | solution.py:330
  134.0 18.7 %collective-permute-done.18.refs_8_ = bf16[1024,256]{1,0:T(8,128)(2,1)S(1)} collective-permute-done((bf16[1024,256]{1,0:T(8,128)(2,1)S(1)}, bf16[1024,256]{1,0:T(8,128)(2,1)S(1)}, u32[]{:S(2)}, u32[]{:S(2)}) %collective-permute-start.18) | collective-permute-done | bytes 524320 | tf_op jit(solution)/shard_map/ppermute | solution.py:356
  152.7 3.6 %step.12 = (bf16[1024,128]{1,0:T(8,128)(2,1)S(1)}, bf16[768,128]{1,0:T(8,128)(2,1)S(1)}, bf16[256,128]{1,0:T(8,128)(2,1)S(1)}, bf16[1024,2048]{1,0:T(8,128)(2,1)}) custom-call(s32[2,9]{1,0:T(2,128)S(1)} %get-tuple-element.24.refs_0_, f32[1,9]{1,0:T(1,128)S(1)} %get-tuple-element.25.refs_1_, ...), custom_call_target="tpu_custom_call", output_to_operand_aliasing={{3}: (9, {})} | custom-call | tf_op jit(solution)/shard_map/step/pallas_call | solution.py:330
  156.4 2.9 %collective-permute-start.20 = (bf16[768,128]{1,0:T(8,128)(2,1)S(1)}, bf16[768,128]{1,0:T(8,128)(2,1)S(1)}, u32[]{:S(2)}, u32[]{:S(2)}) collective-permute-start(bf16[768,128]{1,0:T(8,128)(2,1)S(1)} %get-tuple-element.41), channel_id=1, source_target_pairs={{0,8},{4,12},{8,0},{12,4},{1,9},{5,13},{9,1},{13,5},{2,10},{6,14},... | collective-permute-start | bytes 589832 | tf_op jit(solution)/shard_map/ppermute | solution.py:356
  159.3 0.7 fusion
  161.4 0.1 collective-permute-start.21
  161.5 13.7 %collective-permute-done.14.refs_1_ = bf16[1024,256]{1,0:T(8,128)(2,1)S(1)} collective-permute-done((bf16[1024,256]{1,0:T(8,128)(2,1)S(1)}, bf16[1024,256]{1,0:T(8,128)(2,1)S(1)}, u32[]{:S(2)}, u32[]{:S(2)}) %collective-permute-start.14) | collective-permute-done | bytes 524320 | tf_op jit(solution)/shard_map/ppermute | solution.py:356
  175.2 1.4 step.13
  176.6 4.2 %collective-permute-done.19 = bf16[1024,128]{1,0:T(8,128)(2,1)S(1)} collective-permute-done((bf16[1024,128]{1,0:T(8,128)(2,1)S(1)}, bf16[1024,128]{1,0:T(8,128)(2,1)S(1)}, u32[]{:S(2)}, u32[]{:S(2)}) %collective-permute-start.19) | collective-permute-done | bytes 262176 | tf_op jit(solution)/shard_map/ppermute | solution.py:356
  180.8 0.7 constant_dynamic-update-slice_fusion.2
  181.6 3.4 %collective-permute-done.20 = bf16[768,128]{1,0:T(8,128)(2,1)S(1)} collective-permute-done((bf16[768,128]{1,0:T(8,128)(2,1)S(1)}, bf16[768,128]{1,0:T(8,128)(2,1)S(1)}, u32[]{:S(2)}, u32[]{:S(2)}) %collective-permute-start.20) | collective-permute-done | bytes 196640 | tf_op jit(solution)/shard_map/ppermute | solution.py:356
  184.9 0.7 constant_dynamic-update-slice_fusion.1
  185.6 0.6 constant_dynamic-update-slice_fusion
  (25 shorter events, 0.9 us)
Async XLA Ops:
  1.8 38.5 %collective-permute-start = (bf16[1024,256]{1,0:T(8,128)(2,1)S(1)}, bf16[1024,256]{1,0:T(8,128)(2,1)S(1)}, u32[]{:S(2)}, u32[]{:S(2)}) collective-permute-start(bf16[1024,256]{1,0:T(8,128)(2,1)S(1)} %opening.1.first_ref), channel_id=1, source_target_pairs={{0,8},{4,12},{8,0},{12,4},{1,9},{5,13},{9,1},{13,5},{2,10},{6,14},... | collective-permute-start | bytes 1572872 | tf_op jit(solution)/shard_map/ppermute | solution.py:283
  8.5 54.4 %collective-permute-start.5 = (bf16[1024,256]{1,0:T(8,128)(2,1)S(1)}, bf16[1024,256]{1,0:T(8,128)(2,1)S(1)}, u32[]{:S(2)}, u32[]{:S(2)}) collective-permute-start(bf16[1024,256]{1,0:T(8,128)(2,1)S(1)} %get-tuple-element.28), channel_id=1, source_target_pairs={{0,8},{4,12},{8,0},{12,4},{1,9},{5,13},{9,1},{13,5},{2,10},{6,14},... | collective-permute-start | bytes 1572872 | tf_op jit(solution)/shard_map/ppermute | solution.py:283
  43.0 42.3 %collective-permute-start.1 = (bf16[1024,256]{1,0:T(8,128)(2,1)S(1)}, bf16[1024,256]{1,0:T(8,128)(2,1)S(1)}, u32[]{:S(2)}, u32[]{:S(2)}) collective-permute-start(bf16[1024,256]{1,0:T(8,128)(2,1)S(1)} %get-tuple-element.26), channel_id=1, source_target_pairs={{0,8},{4,12},{8,0},{12,4},{1,9},{5,13},{9,1},{13,5},{2,10},{6,14},... | collective-permute-start | bytes 1572872 | tf_op jit(solution)/shard_map/ppermute | solution.py:356
  43.1 22.5 %collective-permute-start.2 = (f32[2,2,128,128]{3,2,1,0:T(8,128)S(1)}, f32[2,2,128,128]{3,2,1,0:T(8,128)S(1)}, u32[]{:S(2)}, u32[]{:S(2)}) collective-permute-start(f32[2,2,128,128]{3,2,1,0:T(8,128)S(1)} %get-tuple-element.27.refs_4_.refs_5_), channel_id=1, source_target_pairs={{0,1},{1,0},{2,3},{3,2},{4,5},{5,4},{6,7},{7,6},{8,9},{9,8},{10,11... | collective-permute-start | bytes 786440 | tf_op jit(solution)/shard_map/ppermute | solution.py:353
  43.2 22.5 %collective-permute-start.3 = (f32[2,2,128,128]{3,2,1,0:T(8,128)S(1)}, f32[2,2,128,128]{3,2,1,0:T(8,128)S(1)}, u32[]{:S(2)}, u32[]{:S(2)}) collective-permute-start(f32[2,2,128,128]{3,2,1,0:T(8,128)S(1)} %get-tuple-element.27.refs_4_.refs_5_), channel_id=1, source_target_pairs={{0,2},{1,3},{2,0},{3,1},{4,6},{5,7},{6,4},{7,5},{8,10},{9,11},{10,... | collective-permute-start | bytes 786440 | tf_op jit(solution)/shard_map/ppermute | solution.py:353
  45.9 22.5 %collective-permute-start.4 = (f32[2,2,128,128]{3,2,1,0:T(8,128)S(1)}, f32[2,2,128,128]{3,2,1,0:T(8,128)S(1)}, u32[]{:S(2)}, u32[]{:S(2)}) collective-permute-start(f32[2,2,128,128]{3,2,1,0:T(8,128)S(1)} %get-tuple-element.27.refs_4_.refs_5_), channel_id=1, source_target_pairs={{0,3},{1,2},{2,1},{3,0},{4,7},{5,6},{6,5},{7,4},{8,11},{9,10},{10,... | collective-permute-start | bytes 786440 | tf_op jit(solution)/shard_map/ppermute | solution.py:353
  65.5 42.3 %collective-permute-start.10 = (bf16[1024,256]{1,0:T(8,128)(2,1)S(1)}, bf16[1024,256]{1,0:T(8,128)(2,1)S(1)}, u32[]{:S(2)}, u32[]{:S(2)}) collective-permute-start(bf16[1024,256]{1,0:T(8,128)(2,1)S(1)} %get-tuple-element.32), channel_id=1, source_target_pairs={{0,8},{4,12},{8,0},{12,4},{1,9},{5,13},{9,1},{13,5},{2,10},{6,14},... | collective-permute-start | bytes 1572872 | tf_op jit(solution)/shard_map/ppermute | solution.py:356
  65.6 24.3 %collective-permute-start.11 = (f32[2,2,128,128]{3,2,1,0:T(8,128)S(1)}, f32[2,2,128,128]{3,2,1,0:T(8,128)S(1)}, u32[]{:S(2)}, u32[]{:S(2)}) collective-permute-start(f32[2,2,128,128]{3,2,1,0:T(8,128)S(1)} %get-tuple-element.29.refs_9_.refs_5_), channel_id=1, source_target_pairs={{0,1},{1,0},{2,3},{3,2},{4,5},{5,4},{6,7},{7,6},{8,9},{9,8},{10,11... | collective-permute-start | bytes 786440 | tf_op jit(solution)/shard_map/ppermute | solution.py:353
  65.7 24.3 %collective-permute-start.12 = (f32[2,2,128,128]{3,2,1,0:T(8,128)S(1)}, f32[2,2,128,128]{3,2,1,0:T(8,128)S(1)}, u32[]{:S(2)}, u32[]{:S(2)}) collective-permute-start(f32[2,2,128,128]{3,2,1,0:T(8,128)S(1)} %get-tuple-element.29.refs_9_.refs_5_), channel_id=1, source_target_pairs={{0,2},{1,3},{2,0},{3,1},{4,6},{5,7},{6,4},{7,5},{8,10},{9,11},{10,... | collective-permute-start | bytes 786440 | tf_op jit(solution)/shard_map/ppermute | solution.py:353
  68.4 24.4 %collective-permute-start.13 = (f32[2,2,128,128]{3,2,1,0:T(8,128)S(1)}, f32[2,2,128,128]{3,2,1,0:T(8,128)S(1)}, u32[]{:S(2)}, u32[]{:S(2)}) collective-permute-start(f32[2,2,128,128]{3,2,1,0:T(8,128)S(1)} %get-tuple-element.29.refs_9_.refs_5_), channel_id=1, source_target_pairs={{0,3},{1,2},{2,1},{3,0},{4,7},{5,6},{6,5},{7,4},{8,11},{9,10},{10,... | collective-permute-start | bytes 786440 | tf_op jit(solution)/shard_map/ppermute | solution.py:353
  89.8 40.4 %collective-permute-start.9 = (bf16[1024,256]{1,0:T(8,128)(2,1)S(1)}, bf16[1024,256]{1,0:T(8,128)(2,1)S(1)}, u32[]{:S(2)}, u32[]{:S(2)}) collective-permute-start(bf16[1024,256]{1,0:T(8,128)(2,1)S(1)} %get-tuple-element.31), channel_id=1, source_target_pairs={{0,8},{4,12},{8,0},{12,4},{1,9},{5,13},{9,1},{13,5},{2,10},{6,14},... | collective-permute-start | bytes 1572872 | tf_op jit(solution)/shard_map/ppermute | solution.py:356
  89.9 22.5 %collective-permute-start.6 = (f32[2,2,128,128]{3,2,1,0:T(8,128)S(1)}, f32[2,2,128,128]{3,2,1,0:T(8,128)S(1)}, u32[]{:S(2)}, u32[]{:S(2)}) collective-permute-start(f32[2,2,128,128]{3,2,1,0:T(8,128)S(1)} %get-tuple-element.30.refs_4_), channel_id=1, source_target_pairs={{0,1},{1,0},{2,3},{3,2},{4,5},{5,4},{6,7},{7,6},{8,9},{9,8},{10,11... | collective-permute-start | bytes 786440 | tf_op jit(solution)/shard_map/ppermute | solution.py:353
  90.0 22.5 %collective-permute-start.7 = (f32[2,2,128,128]{3,2,1,0:T(8,128)S(1)}, f32[2,2,128,128]{3,2,1,0:T(8,128)S(1)}, u32[]{:S(2)}, u32[]{:S(2)}) collective-permute-start(f32[2,2,128,128]{3,2,1,0:T(8,128)S(1)} %get-tuple-element.30.refs_4_), channel_id=1, source_target_pairs={{0,2},{1,3},{2,0},{3,1},{4,6},{5,7},{6,4},{7,5},{8,10},{9,11},{10,... | collective-permute-start | bytes 786440 | tf_op jit(solution)/shard_map/ppermute | solution.py:353
  92.7 22.5 %collective-permute-start.8 = (f32[2,2,128,128]{3,2,1,0:T(8,128)S(1)}, f32[2,2,128,128]{3,2,1,0:T(8,128)S(1)}, u32[]{:S(2)}, u32[]{:S(2)}) collective-permute-start(f32[2,2,128,128]{3,2,1,0:T(8,128)S(1)} %get-tuple-element.30.refs_4_), channel_id=1, source_target_pairs={{0,3},{1,2},{2,1},{3,0},{4,7},{5,6},{6,5},{7,4},{8,11},{9,10},{10,... | collective-permute-start | bytes 786440 | tf_op jit(solution)/shard_map/ppermute | solution.py:353
  112.3 40.4 %collective-permute-start.18 = (bf16[1024,256]{1,0:T(8,128)(2,1)S(1)}, bf16[1024,256]{1,0:T(8,128)(2,1)S(1)}, u32[]{:S(2)}, u32[]{:S(2)}) collective-permute-start(bf16[1024,256]{1,0:T(8,128)(2,1)S(1)} %get-tuple-element.37), channel_id=1, source_target_pairs={{0,8},{4,12},{8,0},{12,4},{1,9},{5,13},{9,1},{13,5},{2,10},{6,14},... | collective-permute-start | bytes 1572872 | tf_op jit(solution)/shard_map/ppermute | solution.py:356
  112.4 21.6 %collective-permute-start.15 = (f32[2,2,128,128]{3,2,1,0:T(8,128)S(1)}, f32[2,2,128,128]{3,2,1,0:T(8,128)S(1)}, u32[]{:S(2)}, u32[]{:S(2)}) collective-permute-start(f32[2,2,128,128]{3,2,1,0:T(8,128)S(1)} %get-tuple-element.36.refs_4_), channel_id=1, source_target_pairs={{0,1},{1,0},{2,3},{3,2},{4,5},{5,4},{6,7},{7,6},{8,9},{9,8},{10,11... | collective-permute-start | bytes 786440 | tf_op jit(solution)/shard_map/ppermute | solution.py:353
  112.5 21.5 %collective-permute-start.16 = (f32[2,2,128,128]{3,2,1,0:T(8,128)S(1)}, f32[2,2,128,128]{3,2,1,0:T(8,128)S(1)}, u32[]{:S(2)}, u32[]{:S(2)}) collective-permute-start(f32[2,2,128,128]{3,2,1,0:T(8,128)S(1)} %get-tuple-element.36.refs_4_), channel_id=1, source_target_pairs={{0,2},{1,3},{2,0},{3,1},{4,6},{5,7},{6,4},{7,5},{8,10},{9,11},{10,... | collective-permute-start | bytes 786440 | tf_op jit(solution)/shard_map/ppermute | solution.py:353
  115.2 18.8 %collective-permute-start.17 = (f32[2,2,128,128]{3,2,1,0:T(8,128)S(1)}, f32[2,2,128,128]{3,2,1,0:T(8,128)S(1)}, u32[]{:S(2)}, u32[]{:S(2)}) collective-permute-start(f32[2,2,128,128]{3,2,1,0:T(8,128)S(1)} %get-tuple-element.36.refs_4_), channel_id=1, source_target_pairs={{0,3},{1,2},{2,1},{3,0},{4,7},{5,6},{6,5},{7,4},{8,11},{9,10},{10,... | collective-permute-start | bytes 786440 | tf_op jit(solution)/shard_map/ppermute | solution.py:353
  133.9 41.3 %collective-permute-start.14 = (bf16[1024,256]{1,0:T(8,128)(2,1)S(1)}, bf16[1024,256]{1,0:T(8,128)(2,1)S(1)}, u32[]{:S(2)}, u32[]{:S(2)}) collective-permute-start(bf16[1024,256]{1,0:T(8,128)(2,1)S(1)} %get-tuple-element.35), channel_id=1, source_target_pairs={{0,8},{4,12},{8,0},{12,4},{1,9},{5,13},{9,1},{13,5},{2,10},{6,14},... | collective-permute-start | bytes 1572872 | tf_op jit(solution)/shard_map/ppermute | solution.py:356
  156.4 24.5 %collective-permute-start.19 = (bf16[1024,128]{1,0:T(8,128)(2,1)S(1)}, bf16[1024,128]{1,0:T(8,128)(2,1)S(1)}, u32[]{:S(2)}, u32[]{:S(2)}) collective-permute-start(bf16[1024,128]{1,0:T(8,128)(2,1)S(1)} %get-tuple-element.40), channel_id=1, source_target_pairs={{0,8},{4,12},{8,0},{12,4},{1,9},{5,13},{9,1},{13,5},{2,10},{6,14},... | collective-permute-start | bytes 786440 | tf_op jit(solution)/shard_map/ppermute | solution.py:356
  156.4 28.5 %collective-permute-start.20 = (bf16[768,128]{1,0:T(8,128)(2,1)S(1)}, bf16[768,128]{1,0:T(8,128)(2,1)S(1)}, u32[]{:S(2)}, u32[]{:S(2)}) collective-permute-start(bf16[768,128]{1,0:T(8,128)(2,1)S(1)} %get-tuple-element.41), channel_id=1, source_target_pairs={{0,8},{4,12},{8,0},{12,4},{1,9},{5,13},{9,1},{13,5},{2,10},{6,14},... | collective-permute-start | bytes 589832 | tf_op jit(solution)/shard_map/ppermute | solution.py:356
  161.4 24.3 %collective-permute-start.21 = (bf16[256,128]{1,0:T(8,128)(2,1)S(1)}, bf16[256,128]{1,0:T(8,128)(2,1)S(1)}, u32[]{:S(2)}, u32[]{:S(2)}) collective-permute-start(bf16[256,128]{1,0:T(8,128)(2,1)S(1)} %get-tuple-element.42), channel_id=1, source_target_pairs={{0,8},{4,12},{8,0},{12,4},{1,9},{5,13},{9,1},{13,5},{2,10},{6,14},... | collective-permute-start | bytes 196616 | tf_op jit(solution)/shard_map/ppermute | solution.py:356

commit v8 on v7

--- a/solution.py
+++ b/solution.py
@@ -9,7 +9,7 @@
 
 BLOCK = 128
 STRETCH = 256
-CHUNKS = (2, 2, 2, 2)
+CHUNKS = (2, 3, 3)
 LAST = 4
 LAG = 2
 

time: 187 us -> 187 us (level)
  Pallas kernels: 28 us -> 24.2 us
  waiting for transfers between devices: 136 us -> 139 us
    ppermute x8 -> x7, waiting for transfers between devices: 86.8 us -> 55.4 us  [shards(): lax.ppermute(results.pop(0), 'outer', to_second if final else to_first)]
    ppermute x12 -> x9, waiting for transfers between devices: 0.03 us -> 30 us  [shards(): lax.ppermute(mine, 'inner', [(i, i ^ hop) for i in range(ranks)])]
    ppermute x2, waiting for transfers between devices: 48.8 us -> 53.2 us  [shards(): sends = [lax.ppermute(part, 'outer', to_first) for part in [first] + raw]]
    pallas_call x7 -> x5, Pallas kernels: 22.9 us -> 19 us  [shards(): pl.pallas_call(functools.partial(step_kernel, spec), out_shape=shapes, in...]
    ppermute x12 -> x9, starting transfers between devices: 11.4 us -> 8.47 us  [shards(): lax.ppermute(mine, 'inner', [(i, i ^ hop) for i in range(ranks)])]
    ppermute x8 -> x7, starting transfers between devices: 3.48 us -> 6.12 us  [shards(): lax.ppermute(results.pop(0), 'outer', to_second if final else to_first)]
  transfers between devices with their start and end apart: 22 -> 18, of which waited for: 9 -> 12; matrix products, arithmetic and copies ran while one was open for 1% -> 1% of each run, Pallas kernels for 14% -> 12%
where the time goes in v8:
time: 187 us; the launch traced here: 186 us
  waiting for transfers between devices  139 us (74%)
  Pallas kernels  24.2 us (13%)
  starting transfers between devices  18 us (10%)
  local copies, waits for them, and re-layouts  3.43 us (2%)
  between operations  2.02 us (1%)
    ppermute x7, waiting for transfers between devices, shards(): lax.ppermute(results.pop(0), 'outer', to_second if final else to_first)  55.4 us
    ppermute x2, waiting for transfers between devices, shards(): sends = [lax.ppermute(part, 'outer', to_first) for part in [first] + raw]  53.2 us
    ppermute x9, waiting for transfers between devices, shards(): lax.ppermute(mine, 'inner', [(i, i ^ hop) for i in range(ranks)])  30 us
    pallas_call x5, Pallas kernels, shards(): pl.pallas_call(functools.partial(step_kernel, spec), out_shape=shapes, in...  19 us
    ppermute x9, starting transfers between devices, shards(): lax.ppermute(mine, 'inner', [(i, i ^ hop) for i in range(ranks)])  8.47 us
    ppermute x7, starting transfers between devices, shards(): lax.ppermute(results.pop(0), 'outer', to_second if final else to_first)  6.12 us
  transfers between devices with their start and end apart: 18, of which 12 were waited for; matrix products, arithmetic and copies ran while one was open for 1% of the time, Pallas kernels for 12%

profile of v8, /device:TPU:0, one launch (start us, length us, event | category | flops | bytes accessed | tf_op | source)
XLA Modules:
  0.0 186.3 jit_solution(6378837388728805662)
XLA Ops:
  0.0 1.8 opening.1.first_ref
  1.8 3.3 %collective-permute-start = (bf16[1024,256]{1,0:T(8,128)(2,1)S(1)}, bf16[1024,256]{1,0:T(8,128)(2,1)S(1)}, u32[]{:S(2)}, u32[]{:S(2)}) collective-permute-start(bf16[1024,256]{1,0:T(8,128)(2,1)S(1)} %opening.1.first_ref), channel_id=1, source_target_pairs={{0,8},{4,12},{8,0},{12,4},{1,9},{5,13},{9,1},{13,5},{2,10},{6,14},... | collective-permute-start | bytes 1572872 | tf_op jit(solution)/shard_map/ppermute | solution.py:283
  5.2 3.4 %planning.1 = (s32[2,9]{1,0:T(2,128)S(1)}, f32[1,9]{1,0:T(1,128)S(1)}, bf16[1024,384]{1,0:T(8,128)(2,1)S(1)}) custom-call(s32[2,32]{1,0:T(2,128)} %bitcast.5, f32[32]{0:T(128)} %weight_ref.1, bf16[1024,2048]{1,0:T(8,128)(2,1)} %refs_2_.7, bf16[1024,256]{1,0:T(8,128)(2,1)S(1)} %opening.1.first_ref), custom_call_target="tpu_custom_call" | custom-call | tf_op jit(solution)/shard_map/planning/pallas_call | solution.py:269
  8.6 37.4 %collective-permute-done.refs_3_.refs_4_ = bf16[1024,256]{1,0:T(8,128)(2,1)S(1)} collective-permute-done((bf16[1024,256]{1,0:T(8,128)(2,1)S(1)}, bf16[1024,256]{1,0:T(8,128)(2,1)S(1)}, u32[]{:S(2)}, u32[]{:S(2)}) %collective-permute-start) | collective-permute-done | bytes 524320 | tf_op jit(solution)/shard_map/ppermute | solution.py:283
  46.0 2.8 %step.5 = (f32[2,2,128,128]{3,2,1,0:T(8,128)S(1)}, bf16[1024,384]{1,0:T(8,128)(2,1)S(1)}) custom-call(s32[2,9]{1,0:T(2,128)S(1)} %get-tuple-element.21.refs_0_, f32[1,9]{1,0:T(1,128)S(1)} %get-tuple-element.22.refs_1_, bf16[1024,2048]{1,0:T(8,128)(2,1)} %refs_2_.7, bf16[1024,256]{1,0:T(8,128)(2,1)S(1)} %collective-permute-done.refs_3_.refs_4_), custom_call_target="tpu_custom_call" | custom-call | tf_op jit(solution)/shard_map/step/pallas_call | solution.py:330
  49.0 2.7 %collective-permute-start.4 = (f32[2,2,128,128]{3,2,1,0:T(8,128)S(1)}, f32[2,2,128,128]{3,2,1,0:T(8,128)S(1)}, u32[]{:S(2)}, u32[]{:S(2)}) collective-permute-start(f32[2,2,128,128]{3,2,1,0:T(8,128)S(1)} %get-tuple-element.25.refs_5_.refs_9_), channel_id=1, source_target_pairs={{0,2},{1,3},{2,0},{3,1},{4,6},{5,7},{6,4},{7,5},{8,10},{9,11},{10,... | collective-permute-start | bytes 786440 | tf_op jit(solution)/shard_map/ppermute | solution.py:353
  51.7 7.1 %collective-permute-done.4.refs_7_ = f32[2,2,128,128]{3,2,1,0:T(8,128)S(1)} collective-permute-done((f32[2,2,128,128]{3,2,1,0:T(8,128)S(1)}, f32[2,2,128,128]{3,2,1,0:T(8,128)S(1)}, u32[]{:S(2)}, u32[]{:S(2)}) %collective-permute-start.4) | collective-permute-done | bytes 262176 | tf_op jit(solution)/shard_map/ppermute | solution.py:353
  58.8 5.1 %collective-permute-done.5.refs_8_ = f32[2,2,128,128]{3,2,1,0:T(8,128)S(1)} collective-permute-done((f32[2,2,128,128]{3,2,1,0:T(8,128)S(1)}, f32[2,2,128,128]{3,2,1,0:T(8,128)S(1)}, u32[]{:S(2)}, u32[]{:S(2)}) %collective-permute-start.5) | collective-permute-done | bytes 262176 | tf_op jit(solution)/shard_map/ppermute | solution.py:353
  63.9 15.8 %collective-permute-done.2.refs_3_.refs_4_ = bf16[1024,384]{1,0:T(8,128)(2,1)S(1)} collective-permute-done((bf16[1024,384]{1,0:T(8,128)(2,1)S(1)}, bf16[1024,384]{1,0:T(8,128)(2,1)S(1)}, u32[]{:S(2)}, u32[]{:S(2)}) %collective-permute-start.2) | collective-permute-done | bytes 786464 | tf_op jit(solution)/shard_map/ppermute | solution.py:283
  79.7 4.9 %step.6 = (f32[3,2,128,128]{3,2,1,0:T(8,128)S(1)}, bf16[1024,256]{1,0:T(8,128)(2,1)S(1)}, bf16[1024,2048]{1,0:T(8,128)(2,1)}) custom-call(s32[2,9]{1,0:T(2,128)S(1)} %get-tuple-element.21.refs_0_, f32[1,9]{1,0:T(1,128)S(1)} %get-tuple-element.22.refs_1_, bf16[1024,2048]{1,0:T(8,128)(2,1)} %refs_2_.7, ...), custom_call_target="tpu_custom_call" | custom-call | tf_op jit(solution)/shard_map/step/pallas_call | solution.py:330
  84.7 2.7 %collective-permute-start.7 = (f32[3,2,128,128]{3,2,1,0:T(8,128)S(1)}, f32[3,2,128,128]{3,2,1,0:T(8,128)S(1)}, u32[]{:S(2)}, u32[]{:S(2)}) collective-permute-start(f32[3,2,128,128]{3,2,1,0:T(8,128)S(1)} %get-tuple-element.26.refs_5_), channel_id=1, source_target_pairs={{0,2},{1,3},{2,0},{3,1},{4,6},{5,7},{6,4},{7,5},{8,10},{9,11},{10,... | collective-permute-start | bytes 1179656 | tf_op jit(solution)/shard_map/ppermute | solution.py:353
  87.5 9.9 %collective-permute-done.7.refs_7_ = f32[3,2,128,128]{3,2,1,0:T(8,128)S(1)} collective-permute-done((f32[3,2,128,128]{3,2,1,0:T(8,128)S(1)}, f32[3,2,128,128]{3,2,1,0:T(8,128)S(1)}, u32[]{:S(2)}, u32[]{:S(2)}) %collective-permute-start.7) | collective-permute-done | bytes 393248 | tf_op jit(solution)/shard_map/ppermute | solution.py:353
  97.3 7.9 %collective-permute-done.8.refs_8_ = f32[3,2,128,128]{3,2,1,0:T(8,128)S(1)} collective-permute-done((f32[3,2,128,128]{3,2,1,0:T(8,128)S(1)}, f32[3,2,128,128]{3,2,1,0:T(8,128)S(1)}, u32[]{:S(2)}, u32[]{:S(2)}) %collective-permute-start.8) | collective-permute-done | bytes 393248 | tf_op jit(solution)/shard_map/ppermute | solution.py:353
  105.3 2.6 %collective-permute-done.1.refs_3_ = bf16[1024,384]{1,0:T(8,128)(2,1)S(1)} collective-permute-done((bf16[1024,384]{1,0:T(8,128)(2,1)S(1)}, bf16[1024,384]{1,0:T(8,128)(2,1)S(1)}, u32[]{:S(2)}, u32[]{:S(2)}) %collective-permute-start.1) | collective-permute-done | bytes 786464 | tf_op jit(solution)/shard_map/ppermute | solution.py:356
  107.8 5.7 %step.7 = (f32[3,2,128,128]{3,2,1,0:T(8,128)S(1)}, bf16[1024,384]{1,0:T(8,128)(2,1)S(1)}, bf16[1024,2048]{1,0:T(8,128)(2,1)}) custom-call(s32[2,9]{1,0:T(2,128)S(1)} %get-tuple-element.21.refs_0_, f32[1,9]{1,0:T(1,128)S(1)} %get-tuple-element.22.refs_1_, bf16[1024,2048]{1,0:T(8,128)(2,1)} %refs_2_.7, ...), custom_call_target="tpu_custom_call", output_to_operand_aliasing={{2}: (9, {})} | custom-call | tf_op jit(solution)/shard_map/step/pallas_call | solution.py:330
  113.6 2.7 %collective-permute-start.11 = (f32[3,2,128,128]{3,2,1,0:T(8,128)S(1)}, f32[3,2,128,128]{3,2,1,0:T(8,128)S(1)}, u32[]{:S(2)}, u32[]{:S(2)}) collective-permute-start(f32[3,2,128,128]{3,2,1,0:T(8,128)S(1)} %get-tuple-element.29.refs_4_), channel_id=1, source_target_pairs={{0,2},{1,3},{2,0},{3,1},{4,6},{5,7},{6,4},{7,5},{8,10},{9,11},{10,... | collective-permute-start | bytes 1179656 | tf_op jit(solution)/shard_map/ppermute | solution.py:353
  116.4 19.5 %collective-permute-done.13.refs_8_ = bf16[1024,256]{1,0:T(8,128)(2,1)S(1)} collective-permute-done((bf16[1024,256]{1,0:T(8,128)(2,1)S(1)}, bf16[1024,256]{1,0:T(8,128)(2,1)S(1)}, u32[]{:S(2)}, u32[]{:S(2)}) %collective-permute-start.13) | collective-permute-done | bytes 524320 | tf_op jit(solution)/shard_map/ppermute | solution.py:356
  135.9 4.2 %step.8 = (bf16[1024,128]{1,0:T(8,128)(2,1)S(1)}, bf16[1024,128]{1,0:T(8,128)(2,1)S(1)}, bf16[768,128]{1,0:T(8,128)(2,1)S(1)}, bf16[256,128]{1,0:T(8,128)(2,1)S(1)}, bf16[1024,2048]{1,0:T(8,128)(2,1)}) custom-call(s32[2,9]{1,0:T(2,128)S(1)} %get-tuple-element.21.refs_0_, f32[1,9]{1,0:T(1,128)S(1)} %get-tuple-element.22.refs_1_, ...), custom_call_target="tpu_custom_call", output_to_operand_aliasing={{4}: (9, {})} | custom-call | tf_op jit(solution)/shard_map/step/pallas_call | solution.py:330
  140.1 1.3 collective-permute-start.14
  141.4 1.7 collective-permute-start.15
  143.1 0.7 fusion
  145.7 1.3 collective-permute-start.16
  146.9 1.7 collective-permute-start.17
  148.7 20.9 %collective-permute-done.9.refs_1_ = bf16[1024,384]{1,0:T(8,128)(2,1)S(1)} collective-permute-done((bf16[1024,384]{1,0:T(8,128)(2,1)S(1)}, bf16[1024,384]{1,0:T(8,128)(2,1)S(1)}, u32[]{:S(2)}, u32[]{:S(2)}) %collective-permute-start.9) | collective-permute-done | bytes 786464 | tf_op jit(solution)/shard_map/ppermute | solution.py:356
  169.6 1.5 step.9
  171.1 4.1 %collective-permute-done.14 = bf16[1024,128]{1,0:T(8,128)(2,1)S(1)} collective-permute-done((bf16[1024,128]{1,0:T(8,128)(2,1)S(1)}, bf16[1024,128]{1,0:T(8,128)(2,1)S(1)}, u32[]{:S(2)}, u32[]{:S(2)}) %collective-permute-start.14) | collective-permute-done | bytes 262176 | tf_op jit(solution)/shard_map/ppermute | solution.py:356
  175.2 0.7 constant_dynamic-update-slice_fusion.2
  175.9 4.9 %collective-permute-done.15 = bf16[1024,128]{1,0:T(8,128)(2,1)S(1)} collective-permute-done((bf16[1024,128]{1,0:T(8,128)(2,1)S(1)}, bf16[1024,128]{1,0:T(8,128)(2,1)S(1)}, u32[]{:S(2)}, u32[]{:S(2)}) %collective-permute-start.15) | collective-permute-done | bytes 262176 | tf_op jit(solution)/shard_map/ppermute | solution.py:356
  180.8 0.7 constant_dynamic-update-slice_fusion.1
  181.6 3.4 %collective-permute-done.16 = bf16[768,128]{1,0:T(8,128)(2,1)S(1)} collective-permute-done((bf16[768,128]{1,0:T(8,128)(2,1)S(1)}, bf16[768,128]{1,0:T(8,128)(2,1)S(1)}, u32[]{:S(2)}, u32[]{:S(2)}) %collective-permute-start.16) | collective-permute-done | bytes 196640 | tf_op jit(solution)/shard_map/ppermute | solution.py:356
  184.9 0.7 constant_dynamic-update-slice_fusion
  185.6 0.6 constant_dynamic-update-slice_fusion.3
  (16 shorter events, 0.7 us)
Async XLA Ops:
  1.8 44.2 %collective-permute-start = (bf16[1024,256]{1,0:T(8,128)(2,1)S(1)}, bf16[1024,256]{1,0:T(8,128)(2,1)S(1)}, u32[]{:S(2)}, u32[]{:S(2)}) collective-permute-start(bf16[1024,256]{1,0:T(8,128)(2,1)S(1)} %opening.1.first_ref), channel_id=1, source_target_pairs={{0,8},{4,12},{8,0},{12,4},{1,9},{5,13},{9,1},{13,5},{2,10},{6,14},... | collective-permute-start | bytes 1572872 | tf_op jit(solution)/shard_map/ppermute | solution.py:283
  8.6 71.2 %collective-permute-start.2 = (bf16[1024,384]{1,0:T(8,128)(2,1)S(1)}, bf16[1024,384]{1,0:T(8,128)(2,1)S(1)}, u32[]{:S(2)}, u32[]{:S(2)}) collective-permute-start(bf16[1024,384]{1,0:T(8,128)(2,1)S(1)} %get-tuple-element.24), channel_id=1, source_target_pairs={{0,8},{4,12},{8,0},{12,4},{1,9},{5,13},{9,1},{13,5},{2,10},{6,14},... | collective-permute-start | bytes 2359304 | tf_op jit(solution)/shard_map/ppermute | solution.py:283
  48.8 59.0 %collective-permute-start.1 = (bf16[1024,384]{1,0:T(8,128)(2,1)S(1)}, bf16[1024,384]{1,0:T(8,128)(2,1)S(1)}, u32[]{:S(2)}, u32[]{:S(2)}) collective-permute-start(bf16[1024,384]{1,0:T(8,128)(2,1)S(1)} %get-tuple-element.23), channel_id=1, source_target_pairs={{0,8},{4,12},{8,0},{12,4},{1,9},{5,13},{9,1},{13,5},{2,10},{6,14},... | collective-permute-start | bytes 2359304 | tf_op jit(solution)/shard_map/ppermute | solution.py:356
  48.9 2.8 %collective-permute-start.3 = (f32[2,2,128,128]{3,2,1,0:T(8,128)S(1)}, f32[2,2,128,128]{3,2,1,0:T(8,128)S(1)}, u32[]{:S(2)}, u32[]{:S(2)}) collective-permute-start(f32[2,2,128,128]{3,2,1,0:T(8,128)S(1)} %get-tuple-element.25.refs_5_.refs_9_), channel_id=1, source_target_pairs={{0,1},{1,0},{2,3},{3,2},{4,5},{5,4},{6,7},{7,6},{8,9},{9,8},{10,11... | collective-permute-start | bytes 786440 | tf_op jit(solution)/shard_map/ppermute | solution.py:353
  49.0 9.8 %collective-permute-start.4 = (f32[2,2,128,128]{3,2,1,0:T(8,128)S(1)}, f32[2,2,128,128]{3,2,1,0:T(8,128)S(1)}, u32[]{:S(2)}, u32[]{:S(2)}) collective-permute-start(f32[2,2,128,128]{3,2,1,0:T(8,128)S(1)} %get-tuple-element.25.refs_5_.refs_9_), channel_id=1, source_target_pairs={{0,2},{1,3},{2,0},{3,1},{4,6},{5,7},{6,4},{7,5},{8,10},{9,11},{10,... | collective-permute-start | bytes 786440 | tf_op jit(solution)/shard_map/ppermute | solution.py:353
  51.6 12.3 %collective-permute-start.5 = (f32[2,2,128,128]{3,2,1,0:T(8,128)S(1)}, f32[2,2,128,128]{3,2,1,0:T(8,128)S(1)}, u32[]{:S(2)}, u32[]{:S(2)}) collective-permute-start(f32[2,2,128,128]{3,2,1,0:T(8,128)S(1)} %get-tuple-element.25.refs_5_.refs_9_), channel_id=1, source_target_pairs={{0,3},{1,2},{2,1},{3,0},{4,7},{5,6},{6,5},{7,4},{8,11},{9,10},{10,... | collective-permute-start | bytes 786440 | tf_op jit(solution)/shard_map/ppermute | solution.py:353
  84.6 2.8 %collective-permute-start.6 = (f32[3,2,128,128]{3,2,1,0:T(8,128)S(1)}, f32[3,2,128,128]{3,2,1,0:T(8,128)S(1)}, u32[]{:S(2)}, u32[]{:S(2)}) collective-permute-start(f32[3,2,128,128]{3,2,1,0:T(8,128)S(1)} %get-tuple-element.26.refs_5_), channel_id=1, source_target_pairs={{0,1},{1,0},{2,3},{3,2},{4,5},{5,4},{6,7},{7,6},{8,9},{9,8},{10,11... | collective-permute-start | bytes 1179656 | tf_op jit(solution)/shard_map/ppermute | solution.py:353
  84.7 12.6 %collective-permute-start.7 = (f32[3,2,128,128]{3,2,1,0:T(8,128)S(1)}, f32[3,2,128,128]{3,2,1,0:T(8,128)S(1)}, u32[]{:S(2)}, u32[]{:S(2)}) collective-permute-start(f32[3,2,128,128]{3,2,1,0:T(8,128)S(1)} %get-tuple-element.26.refs_5_), channel_id=1, source_target_pairs={{0,2},{1,3},{2,0},{3,1},{4,6},{5,7},{6,4},{7,5},{8,10},{9,11},{10,... | collective-permute-start | bytes 1179656 | tf_op jit(solution)/shard_map/ppermute | solution.py:353
  87.4 17.9 %collective-permute-start.8 = (f32[3,2,128,128]{3,2,1,0:T(8,128)S(1)}, f32[3,2,128,128]{3,2,1,0:T(8,128)S(1)}, u32[]{:S(2)}, u32[]{:S(2)}) collective-permute-start(f32[3,2,128,128]{3,2,1,0:T(8,128)S(1)} %get-tuple-element.26.refs_5_), channel_id=1, source_target_pairs={{0,3},{1,2},{2,1},{3,0},{4,7},{5,6},{6,5},{7,4},{8,11},{9,10},{10,... | collective-permute-start | bytes 1179656 | tf_op jit(solution)/shard_map/ppermute | solution.py:353
  87.5 48.4 %collective-permute-start.13 = (bf16[1024,256]{1,0:T(8,128)(2,1)S(1)}, bf16[1024,256]{1,0:T(8,128)(2,1)S(1)}, u32[]{:S(2)}, u32[]{:S(2)}) collective-permute-start(bf16[1024,256]{1,0:T(8,128)(2,1)S(1)} %get-tuple-element.30), channel_id=1, source_target_pairs={{0,8},{4,12},{8,0},{12,4},{1,9},{5,13},{9,1},{13,5},{2,10},{6,14},... | collective-permute-start | bytes 1572872 | tf_op jit(solution)/shard_map/ppermute | solution.py:356
  113.5 56.1 %collective-permute-start.9 = (bf16[1024,384]{1,0:T(8,128)(2,1)S(1)}, bf16[1024,384]{1,0:T(8,128)(2,1)S(1)}, u32[]{:S(2)}, u32[]{:S(2)}) collective-permute-start(bf16[1024,384]{1,0:T(8,128)(2,1)S(1)} %get-tuple-element.28), channel_id=1, source_target_pairs={{0,8},{4,12},{8,0},{12,4},{1,9},{5,13},{9,1},{13,5},{2,10},{6,14},... | collective-permute-start | bytes 2359304 | tf_op jit(solution)/shard_map/ppermute | solution.py:356
  113.6 22.3 %collective-permute-start.10 = (f32[3,2,128,128]{3,2,1,0:T(8,128)S(1)}, f32[3,2,128,128]{3,2,1,0:T(8,128)S(1)}, u32[]{:S(2)}, u32[]{:S(2)}) collective-permute-start(f32[3,2,128,128]{3,2,1,0:T(8,128)S(1)} %get-tuple-element.29.refs_4_), channel_id=1, source_target_pairs={{0,1},{1,0},{2,3},{3,2},{4,5},{5,4},{6,7},{7,6},{8,9},{9,8},{10,11... | collective-permute-start | bytes 1179656 | tf_op jit(solution)/shard_map/ppermute | solution.py:353
  113.6 22.3 %collective-permute-start.11 = (f32[3,2,128,128]{3,2,1,0:T(8,128)S(1)}, f32[3,2,128,128]{3,2,1,0:T(8,128)S(1)}, u32[]{:S(2)}, u32[]{:S(2)}) collective-permute-start(f32[3,2,128,128]{3,2,1,0:T(8,128)S(1)} %get-tuple-element.29.refs_4_), channel_id=1, source_target_pairs={{0,2},{1,3},{2,0},{3,1},{4,6},{5,7},{6,4},{7,5},{8,10},{9,11},{10,... | collective-permute-start | bytes 1179656 | tf_op jit(solution)/shard_map/ppermute | solution.py:353
  116.3 19.6 %collective-permute-start.12 = (f32[3,2,128,128]{3,2,1,0:T(8,128)S(1)}, f32[3,2,128,128]{3,2,1,0:T(8,128)S(1)}, u32[]{:S(2)}, u32[]{:S(2)}) collective-permute-start(f32[3,2,128,128]{3,2,1,0:T(8,128)S(1)} %get-tuple-element.29.refs_4_), channel_id=1, source_target_pairs={{0,3},{1,2},{2,1},{3,0},{4,7},{5,6},{6,5},{7,4},{8,11},{9,10},{10,... | collective-permute-start | bytes 1179656 | tf_op jit(solution)/shard_map/ppermute | solution.py:353
  140.1 35.1 %collective-permute-start.14 = (bf16[1024,128]{1,0:T(8,128)(2,1)S(1)}, bf16[1024,128]{1,0:T(8,128)(2,1)S(1)}, u32[]{:S(2)}, u32[]{:S(2)}) collective-permute-start(bf16[1024,128]{1,0:T(8,128)(2,1)S(1)} %get-tuple-element.33), channel_id=1, source_target_pairs={{0,8},{4,12},{8,0},{12,4},{1,9},{5,13},{9,1},{13,5},{2,10},{6,14},... | collective-permute-start | bytes 786440 | tf_op jit(solution)/shard_map/ppermute | solution.py:356
  141.4 39.5 %collective-permute-start.15 = (bf16[1024,128]{1,0:T(8,128)(2,1)S(1)}, bf16[1024,128]{1,0:T(8,128)(2,1)S(1)}, u32[]{:S(2)}, u32[]{:S(2)}) collective-permute-start(bf16[1024,128]{1,0:T(8,128)(2,1)S(1)} %get-tuple-element.34), channel_id=1, source_target_pairs={{0,8},{4,12},{8,0},{12,4},{1,9},{5,13},{9,1},{13,5},{2,10},{6,14},... | collective-permute-start | bytes 786440 | tf_op jit(solution)/shard_map/ppermute | solution.py:356
  145.7 39.3 %collective-permute-start.16 = (bf16[768,128]{1,0:T(8,128)(2,1)S(1)}, bf16[768,128]{1,0:T(8,128)(2,1)S(1)}, u32[]{:S(2)}, u32[]{:S(2)}) collective-permute-start(bf16[768,128]{1,0:T(8,128)(2,1)S(1)} %get-tuple-element.35), channel_id=1, source_target_pairs={{0,8},{4,12},{8,0},{12,4},{1,9},{5,13},{9,1},{13,5},{2,10},{6,14},... | collective-permute-start | bytes 589832 | tf_op jit(solution)/shard_map/ppermute | solution.py:356
  146.9 38.7 %collective-permute-start.17 = (bf16[256,128]{1,0:T(8,128)(2,1)S(1)}, bf16[256,128]{1,0:T(8,128)(2,1)S(1)}, u32[]{:S(2)}, u32[]{:S(2)}) collective-permute-start(bf16[256,128]{1,0:T(8,128)(2,1)S(1)} %get-tuple-element.36), channel_id=1, source_target_pairs={{0,8},{4,12},{8,0},{12,4},{1,9},{5,13},{9,1},{13,5},{2,10},{6,14},... | collective-permute-start | bytes 196616 | tf_op jit(solution)/shard_map/ppermute | solution.py:356

commit v9 on v7

--- a/solution.py
+++ b/solution.py
@@ -10,7 +10,7 @@
 BLOCK = 128
 STRETCH = 256
 CHUNKS = (2, 2, 2, 2)
-LAST = 4
+LAST = 2
 LAG = 2
 
 ANY = pl.BlockSpec(memory_space=pl.ANY)

time: 187 us -> 187 us (level)
  transfers between devices with their start and end apart: 22 -> 22, of which waited for: 9 -> 10; matrix products, arithmetic and copies ran while one was open for 1% -> 1% of each run, Pallas kernels for 14% -> 14%
where the time goes in v9:
time: 187 us; the launch traced here: 186 us
  waiting for transfers between devices  136 us (73%)
  Pallas kernels  28 us (15%)
  starting transfers between devices  18.3 us (10%)
  local copies, waits for them, and re-layouts  2.71 us (1%)
    ppermute x8, waiting for transfers between devices, shards(): lax.ppermute(results.pop(0), 'outer', to_second if final else to_first)  86.9 us
    ppermute x2, waiting for transfers between devices, shards(): sends = [lax.ppermute(part, 'outer', to_first) for part in [first] + raw]  48.8 us
    pallas_call x7, Pallas kernels, shards(): pl.pallas_call(functools.partial(step_kernel, spec), out_shape=shapes, in...  22.9 us
    ppermute x12, starting transfers between devices, shards(): lax.ppermute(mine, 'inner', [(i, i ^ hop) for i in range(ranks)])  11.4 us
  transfers between devices with their start and end apart: 22, of which 10 were waited for; matrix products, arithmetic and copies ran while one was open for 1% of the time, Pallas kernels for 14%

profile of v9, /device:TPU:0, one launch (start us, length us, event | category | flops | bytes accessed | tf_op | source)
XLA Modules:
  0.0 186.3 jit_solution(6635976330588578437)
XLA Ops:
  0.0 1.8 opening.1.first_ref
  1.8 3.3 %collective-permute-start = (bf16[1024,256]{1,0:T(8,128)(2,1)S(1)}, bf16[1024,256]{1,0:T(8,128)(2,1)S(1)}, u32[]{:S(2)}, u32[]{:S(2)}) collective-permute-start(bf16[1024,256]{1,0:T(8,128)(2,1)S(1)} %opening.1.first_ref), channel_id=1, source_target_pairs={{0,8},{4,12},{8,0},{12,4},{1,9},{5,13},{9,1},{13,5},{2,10},{6,14},... | collective-permute-start | bytes 1572872 | tf_op jit(solution)/shard_map/ppermute | solution.py:283
  5.2 3.3 %planning.1 = (s32[2,9]{1,0:T(2,128)S(1)}, f32[1,9]{1,0:T(1,128)S(1)}, bf16[1024,256]{1,0:T(8,128)(2,1)S(1)}) custom-call(s32[2,32]{1,0:T(2,128)} %bitcast.4, f32[32]{0:T(128)} %weight_ref.1, bf16[1024,2048]{1,0:T(8,128)(2,1)} %refs_2_.11, bf16[1024,256]{1,0:T(8,128)(2,1)S(1)} %opening.1.first_ref), custom_call_target="tpu_custom_call" | custom-call | tf_op jit(solution)/shard_map/planning/pallas_call | solution.py:269
  8.6 31.8 %collective-permute-done.refs_3_.refs_4_ = bf16[1024,256]{1,0:T(8,128)(2,1)S(1)} collective-permute-done((bf16[1024,256]{1,0:T(8,128)(2,1)S(1)}, bf16[1024,256]{1,0:T(8,128)(2,1)S(1)}, u32[]{:S(2)}, u32[]{:S(2)}) %collective-permute-start) | collective-permute-done | bytes 524320 | tf_op jit(solution)/shard_map/ppermute | solution.py:283
  40.4 2.6 %step.7 = (f32[2,2,128,128]{3,2,1,0:T(8,128)S(1)}, bf16[1024,256]{1,0:T(8,128)(2,1)S(1)}) custom-call(s32[2,9]{1,0:T(2,128)S(1)} %get-tuple-element.24.refs_0_, f32[1,9]{1,0:T(1,128)S(1)} %get-tuple-element.25.refs_1_, bf16[1024,2048]{1,0:T(8,128)(2,1)} %refs_2_.11, bf16[1024,256]{1,0:T(8,128)(2,1)S(1)} %collective-permute-done.refs_3_.refs_4_), custom_call_target="tpu_custom_call" | custom-call | tf_op jit(solution)/shard_map/step/pallas_call | solution.py:330
  43.2 2.7 %collective-permute-start.3 = (f32[2,2,128,128]{3,2,1,0:T(8,128)S(1)}, f32[2,2,128,128]{3,2,1,0:T(8,128)S(1)}, u32[]{:S(2)}, u32[]{:S(2)}) collective-permute-start(f32[2,2,128,128]{3,2,1,0:T(8,128)S(1)} %get-tuple-element.27.refs_4_.refs_5_), channel_id=1, source_target_pairs={{0,2},{1,3},{2,0},{3,1},{4,6},{5,7},{6,4},{7,5},{8,10},{9,11},{10,... | collective-permute-start | bytes 786440 | tf_op jit(solution)/shard_map/ppermute | solution.py:353
  45.9 16.9 %collective-permute-done.5.refs_3_.refs_4_ = bf16[1024,256]{1,0:T(8,128)(2,1)S(1)} collective-permute-done((bf16[1024,256]{1,0:T(8,128)(2,1)S(1)}, bf16[1024,256]{1,0:T(8,128)(2,1)S(1)}, u32[]{:S(2)}, u32[]{:S(2)}) %collective-permute-start.5) | collective-permute-done | bytes 524320 | tf_op jit(solution)/shard_map/ppermute | solution.py:283
  62.9 2.6 %step.8 = (f32[2,2,128,128]{3,2,1,0:T(8,128)S(1)}, bf16[1024,256]{1,0:T(8,128)(2,1)S(1)}) custom-call(s32[2,9]{1,0:T(2,128)S(1)} %get-tuple-element.24.refs_0_, f32[1,9]{1,0:T(1,128)S(1)} %get-tuple-element.25.refs_1_, bf16[1024,2048]{1,0:T(8,128)(2,1)} %refs_2_.11, bf16[1024,256]{1,0:T(8,128)(2,1)S(1)} %collective-permute-done.5.refs_3_.refs_4_, ...), custom_call_target="tpu_custom_call" | custom-call | tf_op jit(solution)/shard_map/step/pallas_call | solution.py:330
  65.7 2.7 %collective-permute-start.12 = (f32[2,2,128,128]{3,2,1,0:T(8,128)S(1)}, f32[2,2,128,128]{3,2,1,0:T(8,128)S(1)}, u32[]{:S(2)}, u32[]{:S(2)}) collective-permute-start(f32[2,2,128,128]{3,2,1,0:T(8,128)S(1)} %get-tuple-element.29.refs_9_.refs_5_), channel_id=1, source_target_pairs={{0,2},{1,3},{2,0},{3,1},{4,6},{5,7},{6,4},{7,5},{8,10},{9,11},{10,... | collective-permute-start | bytes 786440 | tf_op jit(solution)/shard_map/ppermute | solution.py:353
  68.4 0.1 collective-permute-start.13
  68.5 16.8 %collective-permute-done.1.refs_3_ = bf16[1024,256]{1,0:T(8,128)(2,1)S(1)} collective-permute-done((bf16[1024,256]{1,0:T(8,128)(2,1)S(1)}, bf16[1024,256]{1,0:T(8,128)(2,1)S(1)}, u32[]{:S(2)}, u32[]{:S(2)}) %collective-permute-start.1) | collective-permute-done | bytes 524320 | tf_op jit(solution)/shard_map/ppermute | solution.py:356
  85.3 4.5 %step.9 = (f32[2,2,128,128]{3,2,1,0:T(8,128)S(1)}, bf16[1024,256]{1,0:T(8,128)(2,1)S(1)}, bf16[1024,2048]{1,0:T(8,128)(2,1)}) custom-call(s32[2,9]{1,0:T(2,128)S(1)} %get-tuple-element.24.refs_0_, f32[1,9]{1,0:T(1,128)S(1)} %get-tuple-element.25.refs_1_, bf16[1024,2048]{1,0:T(8,128)(2,1)} %refs_2_.11, bf16[1024,256]{1,0:T(8,128)(2,1)S(1)} %collective-permute-done.1.refs_3_, ...), custom_call_target="tpu_custom_call" | custom-call | tf_op jit(solution)/shard_map/step/pallas_call | solution.py:330
  90.0 2.7 %collective-permute-start.7 = (f32[2,2,128,128]{3,2,1,0:T(8,128)S(1)}, f32[2,2,128,128]{3,2,1,0:T(8,128)S(1)}, u32[]{:S(2)}, u32[]{:S(2)}) collective-permute-start(f32[2,2,128,128]{3,2,1,0:T(8,128)S(1)} %get-tuple-element.30.refs_4_), channel_id=1, source_target_pairs={{0,2},{1,3},{2,0},{3,1},{4,6},{5,7},{6,4},{7,5},{8,10},{9,11},{10,... | collective-permute-start | bytes 786440 | tf_op jit(solution)/shard_map/ppermute | solution.py:353
  92.7 0.1 collective-permute-start.8
  92.8 15.0 %collective-permute-done.10.refs_3_ = bf16[1024,256]{1,0:T(8,128)(2,1)S(1)} collective-permute-done((bf16[1024,256]{1,0:T(8,128)(2,1)S(1)}, bf16[1024,256]{1,0:T(8,128)(2,1)S(1)}, u32[]{:S(2)}, u32[]{:S(2)}) %collective-permute-start.10) | collective-permute-done | bytes 524320 | tf_op jit(solution)/shard_map/ppermute | solution.py:356
  107.8 4.5 %step.10 = (f32[2,2,128,128]{3,2,1,0:T(8,128)S(1)}, bf16[1024,256]{1,0:T(8,128)(2,1)S(1)}, bf16[1024,2048]{1,0:T(8,128)(2,1)}) custom-call(s32[2,9]{1,0:T(2,128)S(1)} %get-tuple-element.24.refs_0_, f32[1,9]{1,0:T(1,128)S(1)} %get-tuple-element.25.refs_1_, bf16[1024,2048]{1,0:T(8,128)(2,1)} %refs_2_.11, ...), custom_call_target="tpu_custom_call", output_to_operand_aliasing={{2}: (9, {})} | custom-call | tf_op jit(solution)/shard_map/step/pallas_call | solution.py:330
  112.5 2.7 %collective-permute-start.16 = (f32[2,2,128,128]{3,2,1,0:T(8,128)S(1)}, f32[2,2,128,128]{3,2,1,0:T(8,128)S(1)}, u32[]{:S(2)}, u32[]{:S(2)}) collective-permute-start(f32[2,2,128,128]{3,2,1,0:T(8,128)S(1)} %get-tuple-element.36.refs_4_), channel_id=1, source_target_pairs={{0,2},{1,3},{2,0},{3,1},{4,6},{5,7},{6,4},{7,5},{8,10},{9,11},{10,... | collective-permute-start | bytes 786440 | tf_op jit(solution)/shard_map/ppermute | solution.py:353
  115.3 15.0 %collective-permute-done.9.refs_8_ = bf16[1024,256]{1,0:T(8,128)(2,1)S(1)} collective-permute-done((bf16[1024,256]{1,0:T(8,128)(2,1)S(1)}, bf16[1024,256]{1,0:T(8,128)(2,1)S(1)}, u32[]{:S(2)}, u32[]{:S(2)}) %collective-permute-start.9) | collective-permute-done | bytes 524320 | tf_op jit(solution)/shard_map/ppermute | solution.py:356
  130.3 3.6 %step.11 = (bf16[1024,256]{1,0:T(8,128)(2,1)S(1)}, bf16[1024,2048]{1,0:T(8,128)(2,1)}) custom-call(s32[2,9]{1,0:T(2,128)S(1)} %get-tuple-element.24.refs_0_, f32[1,9]{1,0:T(1,128)S(1)} %get-tuple-element.25.refs_1_, bf16[1024,2048]{1,0:T(8,128)(2,1)} %refs_2_.11, ...), custom_call_target="tpu_custom_call", output_to_operand_aliasing={{1}: (9, {})} | custom-call | tf_op jit(solution)/shard_map/step/pallas_call | solution.py:330
  134.0 18.7 %collective-permute-done.18.refs_8_ = bf16[1024,256]{1,0:T(8,128)(2,1)S(1)} collective-permute-done((bf16[1024,256]{1,0:T(8,128)(2,1)S(1)}, bf16[1024,256]{1,0:T(8,128)(2,1)S(1)}, u32[]{:S(2)}, u32[]{:S(2)}) %collective-permute-start.18) | collective-permute-done | bytes 524320 | tf_op jit(solution)/shard_map/ppermute | solution.py:356
  152.7 3.6 %step.12 = (bf16[1024,128]{1,0:T(8,128)(2,1)S(1)}, bf16[512,128]{1,0:T(8,128)(2,1)S(1)}, bf16[512,128]{1,0:T(8,128)(2,1)S(1)}, bf16[1024,2048]{1,0:T(8,128)(2,1)}) custom-call(s32[2,9]{1,0:T(2,128)S(1)} %get-tuple-element.24.refs_0_, f32[1,9]{1,0:T(1,128)S(1)} %get-tuple-element.25.refs_1_, ...), custom_call_target="tpu_custom_call", output_to_operand_aliasing={{3}: (9, {})} | custom-call | tf_op jit(solution)/shard_map/step/pallas_call | solution.py:330
  156.4 2.9 %collective-permute-start.20 = (bf16[512,128]{1,0:T(8,128)(2,1)S(1)}, bf16[512,128]{1,0:T(8,128)(2,1)S(1)}, u32[]{:S(2)}, u32[]{:S(2)}) collective-permute-start(bf16[512,128]{1,0:T(8,128)(2,1)S(1)} %get-tuple-element.41), channel_id=1, source_target_pairs={{0,8},{4,12},{8,0},{12,4},{1,9},{5,13},{9,1},{13,5},{2,10},{6,14},... | collective-permute-start | bytes 393224 | tf_op jit(solution)/shard_map/ppermute | solution.py:356
  159.3 0.7 fusion
  161.3 0.1 collective-permute-start.21
  161.5 13.7 %collective-permute-done.14.refs_1_ = bf16[1024,256]{1,0:T(8,128)(2,1)S(1)} collective-permute-done((bf16[1024,256]{1,0:T(8,128)(2,1)S(1)}, bf16[1024,256]{1,0:T(8,128)(2,1)S(1)}, u32[]{:S(2)}, u32[]{:S(2)}) %collective-permute-start.14) | collective-permute-done | bytes 524320 | tf_op jit(solution)/shard_map/ppermute | solution.py:356
  175.2 1.4 step.13
  176.6 4.2 %collective-permute-done.19 = bf16[1024,128]{1,0:T(8,128)(2,1)S(1)} collective-permute-done((bf16[1024,128]{1,0:T(8,128)(2,1)S(1)}, bf16[1024,128]{1,0:T(8,128)(2,1)S(1)}, u32[]{:S(2)}, u32[]{:S(2)}) %collective-permute-start.19) | collective-permute-done | bytes 262176 | tf_op jit(solution)/shard_map/ppermute | solution.py:356
  180.8 0.7 constant_dynamic-update-slice_fusion.2
  181.6 2.1 %collective-permute-done.20 = bf16[512,128]{1,0:T(8,128)(2,1)S(1)} collective-permute-done((bf16[512,128]{1,0:T(8,128)(2,1)S(1)}, bf16[512,128]{1,0:T(8,128)(2,1)S(1)}, u32[]{:S(2)}, u32[]{:S(2)}) %collective-permute-start.20) | collective-permute-done | bytes 131104 | tf_op jit(solution)/shard_map/ppermute | solution.py:356
  183.6 0.7 constant_dynamic-update-slice_fusion.1
  184.3 1.3 collective-permute-done.21
  185.6 0.7 constant_dynamic-update-slice_fusion
  (25 shorter events, 1.0 us)
Async XLA Ops:
  1.8 38.5 %collective-permute-start = (bf16[1024,256]{1,0:T(8,128)(2,1)S(1)}, bf16[1024,256]{1,0:T(8,128)(2,1)S(1)}, u32[]{:S(2)}, u32[]{:S(2)}) collective-permute-start(bf16[1024,256]{1,0:T(8,128)(2,1)S(1)} %opening.1.first_ref), channel_id=1, source_target_pairs={{0,8},{4,12},{8,0},{12,4},{1,9},{5,13},{9,1},{13,5},{2,10},{6,14},... | collective-permute-start | bytes 1572872 | tf_op jit(solution)/shard_map/ppermute | solution.py:283
  8.5 54.4 %collective-permute-start.5 = (bf16[1024,256]{1,0:T(8,128)(2,1)S(1)}, bf16[1024,256]{1,0:T(8,128)(2,1)S(1)}, u32[]{:S(2)}, u32[]{:S(2)}) collective-permute-start(bf16[1024,256]{1,0:T(8,128)(2,1)S(1)} %get-tuple-element.28), channel_id=1, source_target_pairs={{0,8},{4,12},{8,0},{12,4},{1,9},{5,13},{9,1},{13,5},{2,10},{6,14},... | collective-permute-start | bytes 1572872 | tf_op jit(solution)/shard_map/ppermute | solution.py:283
  43.0 42.3 %collective-permute-start.1 = (bf16[1024,256]{1,0:T(8,128)(2,1)S(1)}, bf16[1024,256]{1,0:T(8,128)(2,1)S(1)}, u32[]{:S(2)}, u32[]{:S(2)}) collective-permute-start(bf16[1024,256]{1,0:T(8,128)(2,1)S(1)} %get-tuple-element.26), channel_id=1, source_target_pairs={{0,8},{4,12},{8,0},{12,4},{1,9},{5,13},{9,1},{13,5},{2,10},{6,14},... | collective-permute-start | bytes 1572872 | tf_op jit(solution)/shard_map/ppermute | solution.py:356
  43.1 22.5 %collective-permute-start.2 = (f32[2,2,128,128]{3,2,1,0:T(8,128)S(1)}, f32[2,2,128,128]{3,2,1,0:T(8,128)S(1)}, u32[]{:S(2)}, u32[]{:S(2)}) collective-permute-start(f32[2,2,128,128]{3,2,1,0:T(8,128)S(1)} %get-tuple-element.27.refs_4_.refs_5_), channel_id=1, source_target_pairs={{0,1},{1,0},{2,3},{3,2},{4,5},{5,4},{6,7},{7,6},{8,9},{9,8},{10,11... | collective-permute-start | bytes 786440 | tf_op jit(solution)/shard_map/ppermute | solution.py:353
  43.2 22.5 %collective-permute-start.3 = (f32[2,2,128,128]{3,2,1,0:T(8,128)S(1)}, f32[2,2,128,128]{3,2,1,0:T(8,128)S(1)}, u32[]{:S(2)}, u32[]{:S(2)}) collective-permute-start(f32[2,2,128,128]{3,2,1,0:T(8,128)S(1)} %get-tuple-element.27.refs_4_.refs_5_), channel_id=1, source_target_pairs={{0,2},{1,3},{2,0},{3,1},{4,6},{5,7},{6,4},{7,5},{8,10},{9,11},{10,... | collective-permute-start | bytes 786440 | tf_op jit(solution)/shard_map/ppermute | solution.py:353
  45.9 22.5 %collective-permute-start.4 = (f32[2,2,128,128]{3,2,1,0:T(8,128)S(1)}, f32[2,2,128,128]{3,2,1,0:T(8,128)S(1)}, u32[]{:S(2)}, u32[]{:S(2)}) collective-permute-start(f32[2,2,128,128]{3,2,1,0:T(8,128)S(1)} %get-tuple-element.27.refs_4_.refs_5_), channel_id=1, source_target_pairs={{0,3},{1,2},{2,1},{3,0},{4,7},{5,6},{6,5},{7,4},{8,11},{9,10},{10,... | collective-permute-start | bytes 786440 | tf_op jit(solution)/shard_map/ppermute | solution.py:353
  65.5 42.3 %collective-permute-start.10 = (bf16[1024,256]{1,0:T(8,128)(2,1)S(1)}, bf16[1024,256]{1,0:T(8,128)(2,1)S(1)}, u32[]{:S(2)}, u32[]{:S(2)}) collective-permute-start(bf16[1024,256]{1,0:T(8,128)(2,1)S(1)} %get-tuple-element.32), channel_id=1, source_target_pairs={{0,8},{4,12},{8,0},{12,4},{1,9},{5,13},{9,1},{13,5},{2,10},{6,14},... | collective-permute-start | bytes 1572872 | tf_op jit(solution)/shard_map/ppermute | solution.py:356
  65.6 24.3 %collective-permute-start.11 = (f32[2,2,128,128]{3,2,1,0:T(8,128)S(1)}, f32[2,2,128,128]{3,2,1,0:T(8,128)S(1)}, u32[]{:S(2)}, u32[]{:S(2)}) collective-permute-start(f32[2,2,128,128]{3,2,1,0:T(8,128)S(1)} %get-tuple-element.29.refs_9_.refs_5_), channel_id=1, source_target_pairs={{0,1},{1,0},{2,3},{3,2},{4,5},{5,4},{6,7},{7,6},{8,9},{9,8},{10,11... | collective-permute-start | bytes 786440 | tf_op jit(solution)/shard_map/ppermute | solution.py:353
  65.7 24.3 %collective-permute-start.12 = (f32[2,2,128,128]{3,2,1,0:T(8,128)S(1)}, f32[2,2,128,128]{3,2,1,0:T(8,128)S(1)}, u32[]{:S(2)}, u32[]{:S(2)}) collective-permute-start(f32[2,2,128,128]{3,2,1,0:T(8,128)S(1)} %get-tuple-element.29.refs_9_.refs_5_), channel_id=1, source_target_pairs={{0,2},{1,3},{2,0},{3,1},{4,6},{5,7},{6,4},{7,5},{8,10},{9,11},{10,... | collective-permute-start | bytes 786440 | tf_op jit(solution)/shard_map/ppermute | solution.py:353
  68.4 24.4 %collective-permute-start.13 = (f32[2,2,128,128]{3,2,1,0:T(8,128)S(1)}, f32[2,2,128,128]{3,2,1,0:T(8,128)S(1)}, u32[]{:S(2)}, u32[]{:S(2)}) collective-permute-start(f32[2,2,128,128]{3,2,1,0:T(8,128)S(1)} %get-tuple-element.29.refs_9_.refs_5_), channel_id=1, source_target_pairs={{0,3},{1,2},{2,1},{3,0},{4,7},{5,6},{6,5},{7,4},{8,11},{9,10},{10,... | collective-permute-start | bytes 786440 | tf_op jit(solution)/shard_map/ppermute | solution.py:353
  89.8 40.4 %collective-permute-start.9 = (bf16[1024,256]{1,0:T(8,128)(2,1)S(1)}, bf16[1024,256]{1,0:T(8,128)(2,1)S(1)}, u32[]{:S(2)}, u32[]{:S(2)}) collective-permute-start(bf16[1024,256]{1,0:T(8,128)(2,1)S(1)} %get-tuple-element.31), channel_id=1, source_target_pairs={{0,8},{4,12},{8,0},{12,4},{1,9},{5,13},{9,1},{13,5},{2,10},{6,14},... | collective-permute-start | bytes 1572872 | tf_op jit(solution)/shard_map/ppermute | solution.py:356
  89.9 22.5 %collective-permute-start.6 = (f32[2,2,128,128]{3,2,1,0:T(8,128)S(1)}, f32[2,2,128,128]{3,2,1,0:T(8,128)S(1)}, u32[]{:S(2)}, u32[]{:S(2)}) collective-permute-start(f32[2,2,128,128]{3,2,1,0:T(8,128)S(1)} %get-tuple-element.30.refs_4_), channel_id=1, source_target_pairs={{0,1},{1,0},{2,3},{3,2},{4,5},{5,4},{6,7},{7,6},{8,9},{9,8},{10,11... | collective-permute-start | bytes 786440 | tf_op jit(solution)/shard_map/ppermute | solution.py:353
  90.0 22.5 %collective-permute-start.7 = (f32[2,2,128,128]{3,2,1,0:T(8,128)S(1)}, f32[2,2,128,128]{3,2,1,0:T(8,128)S(1)}, u32[]{:S(2)}, u32[]{:S(2)}) collective-permute-start(f32[2,2,128,128]{3,2,1,0:T(8,128)S(1)} %get-tuple-element.30.refs_4_), channel_id=1, source_target_pairs={{0,2},{1,3},{2,0},{3,1},{4,6},{5,7},{6,4},{7,5},{8,10},{9,11},{10,... | collective-permute-start | bytes 786440 | tf_op jit(solution)/shard_map/ppermute | solution.py:353
  92.7 22.5 %collective-permute-start.8 = (f32[2,2,128,128]{3,2,1,0:T(8,128)S(1)}, f32[2,2,128,128]{3,2,1,0:T(8,128)S(1)}, u32[]{:S(2)}, u32[]{:S(2)}) collective-permute-start(f32[2,2,128,128]{3,2,1,0:T(8,128)S(1)} %get-tuple-element.30.refs_4_), channel_id=1, source_target_pairs={{0,3},{1,2},{2,1},{3,0},{4,7},{5,6},{6,5},{7,4},{8,11},{9,10},{10,... | collective-permute-start | bytes 786440 | tf_op jit(solution)/shard_map/ppermute | solution.py:353
  112.3 40.4 %collective-permute-start.18 = (bf16[1024,256]{1,0:T(8,128)(2,1)S(1)}, bf16[1024,256]{1,0:T(8,128)(2,1)S(1)}, u32[]{:S(2)}, u32[]{:S(2)}) collective-permute-start(bf16[1024,256]{1,0:T(8,128)(2,1)S(1)} %get-tuple-element.37), channel_id=1, source_target_pairs={{0,8},{4,12},{8,0},{12,4},{1,9},{5,13},{9,1},{13,5},{2,10},{6,14},... | collective-permute-start | bytes 1572872 | tf_op jit(solution)/shard_map/ppermute | solution.py:356
  112.4 21.6 %collective-permute-start.15 = (f32[2,2,128,128]{3,2,1,0:T(8,128)S(1)}, f32[2,2,128,128]{3,2,1,0:T(8,128)S(1)}, u32[]{:S(2)}, u32[]{:S(2)}) collective-permute-start(f32[2,2,128,128]{3,2,1,0:T(8,128)S(1)} %get-tuple-element.36.refs_4_), channel_id=1, source_target_pairs={{0,1},{1,0},{2,3},{3,2},{4,5},{5,4},{6,7},{7,6},{8,9},{9,8},{10,11... | collective-permute-start | bytes 786440 | tf_op jit(solution)/shard_map/ppermute | solution.py:353
  112.5 21.5 %collective-permute-start.16 = (f32[2,2,128,128]{3,2,1,0:T(8,128)S(1)}, f32[2,2,128,128]{3,2,1,0:T(8,128)S(1)}, u32[]{:S(2)}, u32[]{:S(2)}) collective-permute-start(f32[2,2,128,128]{3,2,1,0:T(8,128)S(1)} %get-tuple-element.36.refs_4_), channel_id=1, source_target_pairs={{0,2},{1,3},{2,0},{3,1},{4,6},{5,7},{6,4},{7,5},{8,10},{9,11},{10,... | collective-permute-start | bytes 786440 | tf_op jit(solution)/shard_map/ppermute | solution.py:353
  115.2 18.8 %collective-permute-start.17 = (f32[2,2,128,128]{3,2,1,0:T(8,128)S(1)}, f32[2,2,128,128]{3,2,1,0:T(8,128)S(1)}, u32[]{:S(2)}, u32[]{:S(2)}) collective-permute-start(f32[2,2,128,128]{3,2,1,0:T(8,128)S(1)} %get-tuple-element.36.refs_4_), channel_id=1, source_target_pairs={{0,3},{1,2},{2,1},{3,0},{4,7},{5,6},{6,5},{7,4},{8,11},{9,10},{10,... | collective-permute-start | bytes 786440 | tf_op jit(solution)/shard_map/ppermute | solution.py:353
  133.9 41.3 %collective-permute-start.14 = (bf16[1024,256]{1,0:T(8,128)(2,1)S(1)}, bf16[1024,256]{1,0:T(8,128)(2,1)S(1)}, u32[]{:S(2)}, u32[]{:S(2)}) collective-permute-start(bf16[1024,256]{1,0:T(8,128)(2,1)S(1)} %get-tuple-element.35), channel_id=1, source_target_pairs={{0,8},{4,12},{8,0},{12,4},{1,9},{5,13},{9,1},{13,5},{2,10},{6,14},... | collective-permute-start | bytes 1572872 | tf_op jit(solution)/shard_map/ppermute | solution.py:356
  156.3 24.5 %collective-permute-start.19 = (bf16[1024,128]{1,0:T(8,128)(2,1)S(1)}, bf16[1024,128]{1,0:T(8,128)(2,1)S(1)}, u32[]{:S(2)}, u32[]{:S(2)}) collective-permute-start(bf16[1024,128]{1,0:T(8,128)(2,1)S(1)} %get-tuple-element.40), channel_id=1, source_target_pairs={{0,8},{4,12},{8,0},{12,4},{1,9},{5,13},{9,1},{13,5},{2,10},{6,14},... | collective-permute-start | bytes 786440 | tf_op jit(solution)/shard_map/ppermute | solution.py:356
  156.4 27.2 %collective-permute-start.20 = (bf16[512,128]{1,0:T(8,128)(2,1)S(1)}, bf16[512,128]{1,0:T(8,128)(2,1)S(1)}, u32[]{:S(2)}, u32[]{:S(2)}) collective-permute-start(bf16[512,128]{1,0:T(8,128)(2,1)S(1)} %get-tuple-element.41), channel_id=1, source_target_pairs={{0,8},{4,12},{8,0},{12,4},{1,9},{5,13},{9,1},{13,5},{2,10},{6,14},... | collective-permute-start | bytes 393224 | tf_op jit(solution)/shard_map/ppermute | solution.py:356
  161.3 24.3 %collective-permute-start.21 = (bf16[512,128]{1,0:T(8,128)(2,1)S(1)}, bf16[512,128]{1,0:T(8,128)(2,1)S(1)}, u32[]{:S(2)}, u32[]{:S(2)}) collective-permute-start(bf16[512,128]{1,0:T(8,128)(2,1)S(1)} %get-tuple-element.42), channel_id=1, source_target_pairs={{0,8},{4,12},{8,0},{12,4},{1,9},{5,13},{9,1},{13,5},{2,10},{6,14},... | collective-permute-start | bytes 393224 | tf_op jit(solution)/shard_map/ppermute | solution.py:356

commit v10 on v7

--- a/solution.py
+++ b/solution.py
@@ -90,9 +90,7 @@
 
         @pl.when(me >= stride)
         def _():
-            copy = pltpu.make_async_copy(decoder_ref.at[:, pl.ds(0, sizes[0] * BLOCK)], out_ref, sem.at[0])
-            copy.start()
-            copy.wait()
+            gather(decoder_ref, range(sizes[0]), [out_ref], sizes, sem)
 
         @pl.when(me < stride)
         def _():

time: 187 us -> 187 us (level)
  no operation moved by 1% of the time
where the time goes in v10:
time: 187 us; the launch traced here: 186 us
  waiting for transfers between devices  136 us (73%)
  Pallas kernels  28 us (15%)
  starting transfers between devices  18.3 us (10%)
  local copies, waits for them, and re-layouts  2.71 us (1%)
    ppermute x8, waiting for transfers between devices, shards(): lax.ppermute(results.pop(0), 'outer', to_second if final else to_first)  86.8 us
    ppermute x2, waiting for transfers between devices, shards(): sends = [lax.ppermute(part, 'outer', to_first) for part in [first] + raw]  48.8 us
    pallas_call x7, Pallas kernels, shards(): pl.pallas_call(functools.partial(step_kernel, spec), out_shape=shapes, in...  22.9 us
    ppermute x12, starting transfers between devices, shards(): lax.ppermute(mine, 'inner', [(i, i ^ hop) for i in range(ranks)])  11.4 us
  transfers between devices with their start and end apart: 22, of which 9 were waited for; matrix products, arithmetic and copies ran while one was open for 1% of the time, Pallas kernels for 14%

profile of v10, /device:TPU:0, one launch (start us, length us, event | category | flops | bytes accessed | tf_op | source)
XLA Modules:
  0.0 186.3 jit_solution(4485754585348330801)
XLA Ops:
  0.0 1.8 opening.1.first_ref
  1.8 3.3 %collective-permute-start = (bf16[1024,256]{1,0:T(8,128)(2,1)S(1)}, bf16[1024,256]{1,0:T(8,128)(2,1)S(1)}, u32[]{:S(2)}, u32[]{:S(2)}) collective-permute-start(bf16[1024,256]{1,0:T(8,128)(2,1)S(1)} %opening.1.first_ref), channel_id=1, source_target_pairs={{0,8},{4,12},{8,0},{12,4},{1,9},{5,13},{9,1},{13,5},{2,10},{6,14},... | collective-permute-start | bytes 1572872 | tf_op jit(solution)/shard_map/ppermute | solution.py:281
  5.2 3.3 %planning.1 = (s32[2,9]{1,0:T(2,128)S(1)}, f32[1,9]{1,0:T(1,128)S(1)}, bf16[1024,256]{1,0:T(8,128)(2,1)S(1)}) custom-call(s32[2,32]{1,0:T(2,128)} %bitcast.4, f32[32]{0:T(128)} %weight_ref.1, bf16[1024,2048]{1,0:T(8,128)(2,1)} %refs_2_.11, bf16[1024,256]{1,0:T(8,128)(2,1)S(1)} %opening.1.first_ref), custom_call_target="tpu_custom_call" | custom-call | tf_op jit(solution)/shard_map/planning/pallas_call | solution.py:267
  8.6 31.8 %collective-permute-done.refs_3_.refs_4_ = bf16[1024,256]{1,0:T(8,128)(2,1)S(1)} collective-permute-done((bf16[1024,256]{1,0:T(8,128)(2,1)S(1)}, bf16[1024,256]{1,0:T(8,128)(2,1)S(1)}, u32[]{:S(2)}, u32[]{:S(2)}) %collective-permute-start) | collective-permute-done | bytes 524320 | tf_op jit(solution)/shard_map/ppermute | solution.py:281
  40.4 2.6 %step.7 = (f32[2,2,128,128]{3,2,1,0:T(8,128)S(1)}, bf16[1024,256]{1,0:T(8,128)(2,1)S(1)}) custom-call(s32[2,9]{1,0:T(2,128)S(1)} %get-tuple-element.24.refs_0_, f32[1,9]{1,0:T(1,128)S(1)} %get-tuple-element.25.refs_1_, bf16[1024,2048]{1,0:T(8,128)(2,1)} %refs_2_.11, bf16[1024,256]{1,0:T(8,128)(2,1)S(1)} %collective-permute-done.refs_3_.refs_4_), custom_call_target="tpu_custom_call" | custom-call | tf_op jit(solution)/shard_map/step/pallas_call | solution.py:328
  43.2 2.7 %collective-permute-start.3 = (f32[2,2,128,128]{3,2,1,0:T(8,128)S(1)}, f32[2,2,128,128]{3,2,1,0:T(8,128)S(1)}, u32[]{:S(2)}, u32[]{:S(2)}) collective-permute-start(f32[2,2,128,128]{3,2,1,0:T(8,128)S(1)} %get-tuple-element.27.refs_4_.refs_5_), channel_id=1, source_target_pairs={{0,2},{1,3},{2,0},{3,1},{4,6},{5,7},{6,4},{7,5},{8,10},{9,11},{10,... | collective-permute-start | bytes 786440 | tf_op jit(solution)/shard_map/ppermute | solution.py:351
  45.9 16.9 %collective-permute-done.5.refs_3_.refs_4_ = bf16[1024,256]{1,0:T(8,128)(2,1)S(1)} collective-permute-done((bf16[1024,256]{1,0:T(8,128)(2,1)S(1)}, bf16[1024,256]{1,0:T(8,128)(2,1)S(1)}, u32[]{:S(2)}, u32[]{:S(2)}) %collective-permute-start.5) | collective-permute-done | bytes 524320 | tf_op jit(solution)/shard_map/ppermute | solution.py:281
  62.9 2.6 %step.8 = (f32[2,2,128,128]{3,2,1,0:T(8,128)S(1)}, bf16[1024,256]{1,0:T(8,128)(2,1)S(1)}) custom-call(s32[2,9]{1,0:T(2,128)S(1)} %get-tuple-element.24.refs_0_, f32[1,9]{1,0:T(1,128)S(1)} %get-tuple-element.25.refs_1_, bf16[1024,2048]{1,0:T(8,128)(2,1)} %refs_2_.11, bf16[1024,256]{1,0:T(8,128)(2,1)S(1)} %collective-permute-done.5.refs_3_.refs_4_, ...), custom_call_target="tpu_custom_call" | custom-call | tf_op jit(solution)/shard_map/step/pallas_call | solution.py:328
  65.7 2.7 %collective-permute-start.12 = (f32[2,2,128,128]{3,2,1,0:T(8,128)S(1)}, f32[2,2,128,128]{3,2,1,0:T(8,128)S(1)}, u32[]{:S(2)}, u32[]{:S(2)}) collective-permute-start(f32[2,2,128,128]{3,2,1,0:T(8,128)S(1)} %get-tuple-element.29.refs_9_.refs_5_), channel_id=1, source_target_pairs={{0,2},{1,3},{2,0},{3,1},{4,6},{5,7},{6,4},{7,5},{8,10},{9,11},{10,... | collective-permute-start | bytes 786440 | tf_op jit(solution)/shard_map/ppermute | solution.py:351
  68.4 0.1 collective-permute-start.13
  68.5 16.8 %collective-permute-done.1.refs_3_ = bf16[1024,256]{1,0:T(8,128)(2,1)S(1)} collective-permute-done((bf16[1024,256]{1,0:T(8,128)(2,1)S(1)}, bf16[1024,256]{1,0:T(8,128)(2,1)S(1)}, u32[]{:S(2)}, u32[]{:S(2)}) %collective-permute-start.1) | collective-permute-done | bytes 524320 | tf_op jit(solution)/shard_map/ppermute | solution.py:354
  85.3 4.5 %step.9 = (f32[2,2,128,128]{3,2,1,0:T(8,128)S(1)}, bf16[1024,256]{1,0:T(8,128)(2,1)S(1)}, bf16[1024,2048]{1,0:T(8,128)(2,1)}) custom-call(s32[2,9]{1,0:T(2,128)S(1)} %get-tuple-element.24.refs_0_, f32[1,9]{1,0:T(1,128)S(1)} %get-tuple-element.25.refs_1_, bf16[1024,2048]{1,0:T(8,128)(2,1)} %refs_2_.11, bf16[1024,256]{1,0:T(8,128)(2,1)S(1)} %collective-permute-done.1.refs_3_, ...), custom_call_target="tpu_custom_call" | custom-call | tf_op jit(solution)/shard_map/step/pallas_call | solution.py:328
  90.0 2.7 %collective-permute-start.7 = (f32[2,2,128,128]{3,2,1,0:T(8,128)S(1)}, f32[2,2,128,128]{3,2,1,0:T(8,128)S(1)}, u32[]{:S(2)}, u32[]{:S(2)}) collective-permute-start(f32[2,2,128,128]{3,2,1,0:T(8,128)S(1)} %get-tuple-element.30.refs_4_), channel_id=1, source_target_pairs={{0,2},{1,3},{2,0},{3,1},{4,6},{5,7},{6,4},{7,5},{8,10},{9,11},{10,... | collective-permute-start | bytes 786440 | tf_op jit(solution)/shard_map/ppermute | solution.py:351
  92.7 0.1 collective-permute-start.8
  92.8 15.0 %collective-permute-done.10.refs_3_ = bf16[1024,256]{1,0:T(8,128)(2,1)S(1)} collective-permute-done((bf16[1024,256]{1,0:T(8,128)(2,1)S(1)}, bf16[1024,256]{1,0:T(8,128)(2,1)S(1)}, u32[]{:S(2)}, u32[]{:S(2)}) %collective-permute-start.10) | collective-permute-done | bytes 524320 | tf_op jit(solution)/shard_map/ppermute | solution.py:354
  107.8 4.5 %step.10 = (f32[2,2,128,128]{3,2,1,0:T(8,128)S(1)}, bf16[1024,256]{1,0:T(8,128)(2,1)S(1)}, bf16[1024,2048]{1,0:T(8,128)(2,1)}) custom-call(s32[2,9]{1,0:T(2,128)S(1)} %get-tuple-element.24.refs_0_, f32[1,9]{1,0:T(1,128)S(1)} %get-tuple-element.25.refs_1_, bf16[1024,2048]{1,0:T(8,128)(2,1)} %refs_2_.11, ...), custom_call_target="tpu_custom_call", output_to_operand_aliasing={{2}: (9, {})} | custom-call | tf_op jit(solution)/shard_map/step/pallas_call | solution.py:328
  112.5 2.7 %collective-permute-start.16 = (f32[2,2,128,128]{3,2,1,0:T(8,128)S(1)}, f32[2,2,128,128]{3,2,1,0:T(8,128)S(1)}, u32[]{:S(2)}, u32[]{:S(2)}) collective-permute-start(f32[2,2,128,128]{3,2,1,0:T(8,128)S(1)} %get-tuple-element.36.refs_4_), channel_id=1, source_target_pairs={{0,2},{1,3},{2,0},{3,1},{4,6},{5,7},{6,4},{7,5},{8,10},{9,11},{10,... | collective-permute-start | bytes 786440 | tf_op jit(solution)/shard_map/ppermute | solution.py:351
  115.2 0.1 collective-permute-start.17
  115.3 15.0 %collective-permute-done.9.refs_8_ = bf16[1024,256]{1,0:T(8,128)(2,1)S(1)} collective-permute-done((bf16[1024,256]{1,0:T(8,128)(2,1)S(1)}, bf16[1024,256]{1,0:T(8,128)(2,1)S(1)}, u32[]{:S(2)}, u32[]{:S(2)}) %collective-permute-start.9) | collective-permute-done | bytes 524320 | tf_op jit(solution)/shard_map/ppermute | solution.py:354
  130.3 3.6 %step.11 = (bf16[1024,256]{1,0:T(8,128)(2,1)S(1)}, bf16[1024,2048]{1,0:T(8,128)(2,1)}) custom-call(s32[2,9]{1,0:T(2,128)S(1)} %get-tuple-element.24.refs_0_, f32[1,9]{1,0:T(1,128)S(1)} %get-tuple-element.25.refs_1_, bf16[1024,2048]{1,0:T(8,128)(2,1)} %refs_2_.11, ...), custom_call_target="tpu_custom_call", output_to_operand_aliasing={{1}: (9, {})} | custom-call | tf_op jit(solution)/shard_map/step/pallas_call | solution.py:328
  134.0 18.7 %collective-permute-done.18.refs_8_ = bf16[1024,256]{1,0:T(8,128)(2,1)S(1)} collective-permute-done((bf16[1024,256]{1,0:T(8,128)(2,1)S(1)}, bf16[1024,256]{1,0:T(8,128)(2,1)S(1)}, u32[]{:S(2)}, u32[]{:S(2)}) %collective-permute-start.18) | collective-permute-done | bytes 524320 | tf_op jit(solution)/shard_map/ppermute | solution.py:354
  152.7 3.6 %step.12 = (bf16[1024,128]{1,0:T(8,128)(2,1)S(1)}, bf16[768,128]{1,0:T(8,128)(2,1)S(1)}, bf16[256,128]{1,0:T(8,128)(2,1)S(1)}, bf16[1024,2048]{1,0:T(8,128)(2,1)}) custom-call(s32[2,9]{1,0:T(2,128)S(1)} %get-tuple-element.24.refs_0_, f32[1,9]{1,0:T(1,128)S(1)} %get-tuple-element.25.refs_1_, ...), custom_call_target="tpu_custom_call", output_to_operand_aliasing={{3}: (9, {})} | custom-call | tf_op jit(solution)/shard_map/step/pallas_call | solution.py:328
  156.4 2.9 %collective-permute-start.20 = (bf16[768,128]{1,0:T(8,128)(2,1)S(1)}, bf16[768,128]{1,0:T(8,128)(2,1)S(1)}, u32[]{:S(2)}, u32[]{:S(2)}) collective-permute-start(bf16[768,128]{1,0:T(8,128)(2,1)S(1)} %get-tuple-element.41), channel_id=1, source_target_pairs={{0,8},{4,12},{8,0},{12,4},{1,9},{5,13},{9,1},{13,5},{2,10},{6,14},... | collective-permute-start | bytes 589832 | tf_op jit(solution)/shard_map/ppermute | solution.py:354
  159.3 0.7 fusion
  161.4 0.1 collective-permute-start.21
  161.5 13.7 %collective-permute-done.14.refs_1_ = bf16[1024,256]{1,0:T(8,128)(2,1)S(1)} collective-permute-done((bf16[1024,256]{1,0:T(8,128)(2,1)S(1)}, bf16[1024,256]{1,0:T(8,128)(2,1)S(1)}, u32[]{:S(2)}, u32[]{:S(2)}) %collective-permute-start.14) | collective-permute-done | bytes 524320 | tf_op jit(solution)/shard_map/ppermute | solution.py:354
  175.2 1.4 step.13
  176.6 4.2 %collective-permute-done.19 = bf16[1024,128]{1,0:T(8,128)(2,1)S(1)} collective-permute-done((bf16[1024,128]{1,0:T(8,128)(2,1)S(1)}, bf16[1024,128]{1,0:T(8,128)(2,1)S(1)}, u32[]{:S(2)}, u32[]{:S(2)}) %collective-permute-start.19) | collective-permute-done | bytes 262176 | tf_op jit(solution)/shard_map/ppermute | solution.py:354
  180.8 0.7 constant_dynamic-update-slice_fusion.2
  181.6 3.4 %collective-permute-done.20 = bf16[768,128]{1,0:T(8,128)(2,1)S(1)} collective-permute-done((bf16[768,128]{1,0:T(8,128)(2,1)S(1)}, bf16[768,128]{1,0:T(8,128)(2,1)S(1)}, u32[]{:S(2)}, u32[]{:S(2)}) %collective-permute-start.20) | collective-permute-done | bytes 196640 | tf_op jit(solution)/shard_map/ppermute | solution.py:354
  184.9 0.7 constant_dynamic-update-slice_fusion.1
  185.6 0.6 constant_dynamic-update-slice_fusion
  (25 shorter events, 0.9 us)
Async XLA Ops:
  1.8 38.5 %collective-permute-start = (bf16[1024,256]{1,0:T(8,128)(2,1)S(1)}, bf16[1024,256]{1,0:T(8,128)(2,1)S(1)}, u32[]{:S(2)}, u32[]{:S(2)}) collective-permute-start(bf16[1024,256]{1,0:T(8,128)(2,1)S(1)} %opening.1.first_ref), channel_id=1, source_target_pairs={{0,8},{4,12},{8,0},{12,4},{1,9},{5,13},{9,1},{13,5},{2,10},{6,14},... | collective-permute-start | bytes 1572872 | tf_op jit(solution)/shard_map/ppermute | solution.py:281
  8.5 54.4 %collective-permute-start.5 = (bf16[1024,256]{1,0:T(8,128)(2,1)S(1)}, bf16[1024,256]{1,0:T(8,128)(2,1)S(1)}, u32[]{:S(2)}, u32[]{:S(2)}) collective-permute-start(bf16[1024,256]{1,0:T(8,128)(2,1)S(1)} %get-tuple-element.28), channel_id=1, source_target_pairs={{0,8},{4,12},{8,0},{12,4},{1,9},{5,13},{9,1},{13,5},{2,10},{6,14},... | collective-permute-start | bytes 1572872 | tf_op jit(solution)/shard_map/ppermute | solution.py:281
  43.0 42.3 %collective-permute-start.1 = (bf16[1024,256]{1,0:T(8,128)(2,1)S(1)}, bf16[1024,256]{1,0:T(8,128)(2,1)S(1)}, u32[]{:S(2)}, u32[]{:S(2)}) collective-permute-start(bf16[1024,256]{1,0:T(8,128)(2,1)S(1)} %get-tuple-element.26), channel_id=1, source_target_pairs={{0,8},{4,12},{8,0},{12,4},{1,9},{5,13},{9,1},{13,5},{2,10},{6,14},... | collective-permute-start | bytes 1572872 | tf_op jit(solution)/shard_map/ppermute | solution.py:354
  43.1 22.5 %collective-permute-start.2 = (f32[2,2,128,128]{3,2,1,0:T(8,128)S(1)}, f32[2,2,128,128]{3,2,1,0:T(8,128)S(1)}, u32[]{:S(2)}, u32[]{:S(2)}) collective-permute-start(f32[2,2,128,128]{3,2,1,0:T(8,128)S(1)} %get-tuple-element.27.refs_4_.refs_5_), channel_id=1, source_target_pairs={{0,1},{1,0},{2,3},{3,2},{4,5},{5,4},{6,7},{7,6},{8,9},{9,8},{10,11... | collective-permute-start | bytes 786440 | tf_op jit(solution)/shard_map/ppermute | solution.py:351
  43.2 22.5 %collective-permute-start.3 = (f32[2,2,128,128]{3,2,1,0:T(8,128)S(1)}, f32[2,2,128,128]{3,2,1,0:T(8,128)S(1)}, u32[]{:S(2)}, u32[]{:S(2)}) collective-permute-start(f32[2,2,128,128]{3,2,1,0:T(8,128)S(1)} %get-tuple-element.27.refs_4_.refs_5_), channel_id=1, source_target_pairs={{0,2},{1,3},{2,0},{3,1},{4,6},{5,7},{6,4},{7,5},{8,10},{9,11},{10,... | collective-permute-start | bytes 786440 | tf_op jit(solution)/shard_map/ppermute | solution.py:351
  45.9 22.5 %collective-permute-start.4 = (f32[2,2,128,128]{3,2,1,0:T(8,128)S(1)}, f32[2,2,128,128]{3,2,1,0:T(8,128)S(1)}, u32[]{:S(2)}, u32[]{:S(2)}) collective-permute-start(f32[2,2,128,128]{3,2,1,0:T(8,128)S(1)} %get-tuple-element.27.refs_4_.refs_5_), channel_id=1, source_target_pairs={{0,3},{1,2},{2,1},{3,0},{4,7},{5,6},{6,5},{7,4},{8,11},{9,10},{10,... | collective-permute-start | bytes 786440 | tf_op jit(solution)/shard_map/ppermute | solution.py:351
  65.5 42.3 %collective-permute-start.10 = (bf16[1024,256]{1,0:T(8,128)(2,1)S(1)}, bf16[1024,256]{1,0:T(8,128)(2,1)S(1)}, u32[]{:S(2)}, u32[]{:S(2)}) collective-permute-start(bf16[1024,256]{1,0:T(8,128)(2,1)S(1)} %get-tuple-element.32), channel_id=1, source_target_pairs={{0,8},{4,12},{8,0},{12,4},{1,9},{5,13},{9,1},{13,5},{2,10},{6,14},... | collective-permute-start | bytes 1572872 | tf_op jit(solution)/shard_map/ppermute | solution.py:354
  65.6 24.3 %collective-permute-start.11 = (f32[2,2,128,128]{3,2,1,0:T(8,128)S(1)}, f32[2,2,128,128]{3,2,1,0:T(8,128)S(1)}, u32[]{:S(2)}, u32[]{:S(2)}) collective-permute-start(f32[2,2,128,128]{3,2,1,0:T(8,128)S(1)} %get-tuple-element.29.refs_9_.refs_5_), channel_id=1, source_target_pairs={{0,1},{1,0},{2,3},{3,2},{4,5},{5,4},{6,7},{7,6},{8,9},{9,8},{10,11... | collective-permute-start | bytes 786440 | tf_op jit(solution)/shard_map/ppermute | solution.py:351
  65.7 24.3 %collective-permute-start.12 = (f32[2,2,128,128]{3,2,1,0:T(8,128)S(1)}, f32[2,2,128,128]{3,2,1,0:T(8,128)S(1)}, u32[]{:S(2)}, u32[]{:S(2)}) collective-permute-start(f32[2,2,128,128]{3,2,1,0:T(8,128)S(1)} %get-tuple-element.29.refs_9_.refs_5_), channel_id=1, source_target_pairs={{0,2},{1,3},{2,0},{3,1},{4,6},{5,7},{6,4},{7,5},{8,10},{9,11},{10,... | collective-permute-start | bytes 786440 | tf_op jit(solution)/shard_map/ppermute | solution.py:351
  68.4 24.4 %collective-permute-start.13 = (f32[2,2,128,128]{3,2,1,0:T(8,128)S(1)}, f32[2,2,128,128]{3,2,1,0:T(8,128)S(1)}, u32[]{:S(2)}, u32[]{:S(2)}) collective-permute-start(f32[2,2,128,128]{3,2,1,0:T(8,128)S(1)} %get-tuple-element.29.refs_9_.refs_5_), channel_id=1, source_target_pairs={{0,3},{1,2},{2,1},{3,0},{4,7},{5,6},{6,5},{7,4},{8,11},{9,10},{10,... | collective-permute-start | bytes 786440 | tf_op jit(solution)/shard_map/ppermute | solution.py:351
  89.8 40.4 %collective-permute-start.9 = (bf16[1024,256]{1,0:T(8,128)(2,1)S(1)}, bf16[1024,256]{1,0:T(8,128)(2,1)S(1)}, u32[]{:S(2)}, u32[]{:S(2)}) collective-permute-start(bf16[1024,256]{1,0:T(8,128)(2,1)S(1)} %get-tuple-element.31), channel_id=1, source_target_pairs={{0,8},{4,12},{8,0},{12,4},{1,9},{5,13},{9,1},{13,5},{2,10},{6,14},... | collective-permute-start | bytes 1572872 | tf_op jit(solution)/shard_map/ppermute | solution.py:354
  89.9 22.5 %collective-permute-start.6 = (f32[2,2,128,128]{3,2,1,0:T(8,128)S(1)}, f32[2,2,128,128]{3,2,1,0:T(8,128)S(1)}, u32[]{:S(2)}, u32[]{:S(2)}) collective-permute-start(f32[2,2,128,128]{3,2,1,0:T(8,128)S(1)} %get-tuple-element.30.refs_4_), channel_id=1, source_target_pairs={{0,1},{1,0},{2,3},{3,2},{4,5},{5,4},{6,7},{7,6},{8,9},{9,8},{10,11... | collective-permute-start | bytes 786440 | tf_op jit(solution)/shard_map/ppermute | solution.py:351
  90.0 22.5 %collective-permute-start.7 = (f32[2,2,128,128]{3,2,1,0:T(8,128)S(1)}, f32[2,2,128,128]{3,2,1,0:T(8,128)S(1)}, u32[]{:S(2)}, u32[]{:S(2)}) collective-permute-start(f32[2,2,128,128]{3,2,1,0:T(8,128)S(1)} %get-tuple-element.30.refs_4_), channel_id=1, source_target_pairs={{0,2},{1,3},{2,0},{3,1},{4,6},{5,7},{6,4},{7,5},{8,10},{9,11},{10,... | collective-permute-start | bytes 786440 | tf_op jit(solution)/shard_map/ppermute | solution.py:351
  92.7 22.5 %collective-permute-start.8 = (f32[2,2,128,128]{3,2,1,0:T(8,128)S(1)}, f32[2,2,128,128]{3,2,1,0:T(8,128)S(1)}, u32[]{:S(2)}, u32[]{:S(2)}) collective-permute-start(f32[2,2,128,128]{3,2,1,0:T(8,128)S(1)} %get-tuple-element.30.refs_4_), channel_id=1, source_target_pairs={{0,3},{1,2},{2,1},{3,0},{4,7},{5,6},{6,5},{7,4},{8,11},{9,10},{10,... | collective-permute-start | bytes 786440 | tf_op jit(solution)/shard_map/ppermute | solution.py:351
  112.3 40.4 %collective-permute-start.18 = (bf16[1024,256]{1,0:T(8,128)(2,1)S(1)}, bf16[1024,256]{1,0:T(8,128)(2,1)S(1)}, u32[]{:S(2)}, u32[]{:S(2)}) collective-permute-start(bf16[1024,256]{1,0:T(8,128)(2,1)S(1)} %get-tuple-element.37), channel_id=1, source_target_pairs={{0,8},{4,12},{8,0},{12,4},{1,9},{5,13},{9,1},{13,5},{2,10},{6,14},... | collective-permute-start | bytes 1572872 | tf_op jit(solution)/shard_map/ppermute | solution.py:354
  112.4 21.6 %collective-permute-start.15 = (f32[2,2,128,128]{3,2,1,0:T(8,128)S(1)}, f32[2,2,128,128]{3,2,1,0:T(8,128)S(1)}, u32[]{:S(2)}, u32[]{:S(2)}) collective-permute-start(f32[2,2,128,128]{3,2,1,0:T(8,128)S(1)} %get-tuple-element.36.refs_4_), channel_id=1, source_target_pairs={{0,1},{1,0},{2,3},{3,2},{4,5},{5,4},{6,7},{7,6},{8,9},{9,8},{10,11... | collective-permute-start | bytes 786440 | tf_op jit(solution)/shard_map/ppermute | solution.py:351
  112.5 21.5 %collective-permute-start.16 = (f32[2,2,128,128]{3,2,1,0:T(8,128)S(1)}, f32[2,2,128,128]{3,2,1,0:T(8,128)S(1)}, u32[]{:S(2)}, u32[]{:S(2)}) collective-permute-start(f32[2,2,128,128]{3,2,1,0:T(8,128)S(1)} %get-tuple-element.36.refs_4_), channel_id=1, source_target_pairs={{0,2},{1,3},{2,0},{3,1},{4,6},{5,7},{6,4},{7,5},{8,10},{9,11},{10,... | collective-permute-start | bytes 786440 | tf_op jit(solution)/shard_map/ppermute | solution.py:351
  115.2 18.8 %collective-permute-start.17 = (f32[2,2,128,128]{3,2,1,0:T(8,128)S(1)}, f32[2,2,128,128]{3,2,1,0:T(8,128)S(1)}, u32[]{:S(2)}, u32[]{:S(2)}) collective-permute-start(f32[2,2,128,128]{3,2,1,0:T(8,128)S(1)} %get-tuple-element.36.refs_4_), channel_id=1, source_target_pairs={{0,3},{1,2},{2,1},{3,0},{4,7},{5,6},{6,5},{7,4},{8,11},{9,10},{10,... | collective-permute-start | bytes 786440 | tf_op jit(solution)/shard_map/ppermute | solution.py:351
  133.9 41.3 %collective-permute-start.14 = (bf16[1024,256]{1,0:T(8,128)(2,1)S(1)}, bf16[1024,256]{1,0:T(8,128)(2,1)S(1)}, u32[]{:S(2)}, u32[]{:S(2)}) collective-permute-start(bf16[1024,256]{1,0:T(8,128)(2,1)S(1)} %get-tuple-element.35), channel_id=1, source_target_pairs={{0,8},{4,12},{8,0},{12,4},{1,9},{5,13},{9,1},{13,5},{2,10},{6,14},... | collective-permute-start | bytes 1572872 | tf_op jit(solution)/shard_map/ppermute | solution.py:354
  156.4 24.5 %collective-permute-start.19 = (bf16[1024,128]{1,0:T(8,128)(2,1)S(1)}, bf16[1024,128]{1,0:T(8,128)(2,1)S(1)}, u32[]{:S(2)}, u32[]{:S(2)}) collective-permute-start(bf16[1024,128]{1,0:T(8,128)(2,1)S(1)} %get-tuple-element.40), channel_id=1, source_target_pairs={{0,8},{4,12},{8,0},{12,4},{1,9},{5,13},{9,1},{13,5},{2,10},{6,14},... | collective-permute-start | bytes 786440 | tf_op jit(solution)/shard_map/ppermute | solution.py:354
  156.4 28.5 %collective-permute-start.20 = (bf16[768,128]{1,0:T(8,128)(2,1)S(1)}, bf16[768,128]{1,0:T(8,128)(2,1)S(1)}, u32[]{:S(2)}, u32[]{:S(2)}) collective-permute-start(bf16[768,128]{1,0:T(8,128)(2,1)S(1)} %get-tuple-element.41), channel_id=1, source_target_pairs={{0,8},{4,12},{8,0},{12,4},{1,9},{5,13},{9,1},{13,5},{2,10},{6,14},... | collective-permute-start | bytes 589832 | tf_op jit(solution)/shard_map/ppermute | solution.py:354
  161.4 24.3 %collective-permute-start.21 = (bf16[256,128]{1,0:T(8,128)(2,1)S(1)}, bf16[256,128]{1,0:T(8,128)(2,1)S(1)}, u32[]{:S(2)}, u32[]{:S(2)}) collective-permute-start(bf16[256,128]{1,0:T(8,128)(2,1)S(1)} %get-tuple-element.42), channel_id=1, source_target_pairs={{0,8},{4,12},{8,0},{12,4},{1,9},{5,13},{9,1},{13,5},{2,10},{6,14},... | collective-permute-start | bytes 196616 | tf_op jit(solution)/shard_map/ppermute | solution.py:354

commit v11 on v10

--- a/solution.py
+++ b/solution.py
@@ -10,7 +10,7 @@
 BLOCK = 128
 STRETCH = 256
 CHUNKS = (2, 2, 2, 2)
-LAST = 4
+LAST = 2
 LAG = 2
 
 ANY = pl.BlockSpec(memory_space=pl.ANY)

time: 187 us -> 187 us (level)
  transfers between devices with their start and end apart: 22 -> 22, of which waited for: 9 -> 10; matrix products, arithmetic and copies ran while one was open for 1% -> 1% of each run, Pallas kernels for 14% -> 14%
where the time goes in v11:
time: 187 us; the launch traced here: 186 us
  waiting for transfers between devices  136 us (73%)
  Pallas kernels  28 us (15%)
  starting transfers between devices  18.3 us (10%)
  local copies, waits for them, and re-layouts  2.71 us (1%)
    ppermute x8, waiting for transfers between devices, shards(): lax.ppermute(results.pop(0), 'outer', to_second if final else to_first)  86.9 us
    ppermute x2, waiting for transfers between devices, shards(): sends = [lax.ppermute(part, 'outer', to_first) for part in [first] + raw]  48.8 us
    pallas_call x7, Pallas kernels, shards(): pl.pallas_call(functools.partial(step_kernel, spec), out_shape=shapes, in...  22.9 us
    ppermute x12, starting transfers between devices, shards(): lax.ppermute(mine, 'inner', [(i, i ^ hop) for i in range(ranks)])  11.4 us
  transfers between devices with their start and end apart: 22, of which 10 were waited for; matrix products, arithmetic and copies ran while one was open for 1% of the time, Pallas kernels for 14%

profile of v11, /device:TPU:0, one launch (start us, length us, event | category | flops | bytes accessed | tf_op | source)
XLA Modules:
  0.0 186.3 jit_solution(3437565819143465356)
XLA Ops:
  0.0 1.8 opening.1.first_ref
  1.8 3.3 %collective-permute-start = (bf16[1024,256]{1,0:T(8,128)(2,1)S(1)}, bf16[1024,256]{1,0:T(8,128)(2,1)S(1)}, u32[]{:S(2)}, u32[]{:S(2)}) collective-permute-start(bf16[1024,256]{1,0:T(8,128)(2,1)S(1)} %opening.1.first_ref), channel_id=1, source_target_pairs={{0,8},{4,12},{8,0},{12,4},{1,9},{5,13},{9,1},{13,5},{2,10},{6,14},... | collective-permute-start | bytes 1572872 | tf_op jit(solution)/shard_map/ppermute | solution.py:281
  5.2 3.3 %planning.1 = (s32[2,9]{1,0:T(2,128)S(1)}, f32[1,9]{1,0:T(1,128)S(1)}, bf16[1024,256]{1,0:T(8,128)(2,1)S(1)}) custom-call(s32[2,32]{1,0:T(2,128)} %bitcast.4, f32[32]{0:T(128)} %weight_ref.1, bf16[1024,2048]{1,0:T(8,128)(2,1)} %refs_2_.11, bf16[1024,256]{1,0:T(8,128)(2,1)S(1)} %opening.1.first_ref), custom_call_target="tpu_custom_call" | custom-call | tf_op jit(solution)/shard_map/planning/pallas_call | solution.py:267
  8.6 31.8 %collective-permute-done.refs_3_.refs_4_ = bf16[1024,256]{1,0:T(8,128)(2,1)S(1)} collective-permute-done((bf16[1024,256]{1,0:T(8,128)(2,1)S(1)}, bf16[1024,256]{1,0:T(8,128)(2,1)S(1)}, u32[]{:S(2)}, u32[]{:S(2)}) %collective-permute-start) | collective-permute-done | bytes 524320 | tf_op jit(solution)/shard_map/ppermute | solution.py:281
  40.4 2.6 %step.7 = (f32[2,2,128,128]{3,2,1,0:T(8,128)S(1)}, bf16[1024,256]{1,0:T(8,128)(2,1)S(1)}) custom-call(s32[2,9]{1,0:T(2,128)S(1)} %get-tuple-element.24.refs_0_, f32[1,9]{1,0:T(1,128)S(1)} %get-tuple-element.25.refs_1_, bf16[1024,2048]{1,0:T(8,128)(2,1)} %refs_2_.11, bf16[1024,256]{1,0:T(8,128)(2,1)S(1)} %collective-permute-done.refs_3_.refs_4_), custom_call_target="tpu_custom_call" | custom-call | tf_op jit(solution)/shard_map/step/pallas_call | solution.py:328
  43.2 2.7 %collective-permute-start.3 = (f32[2,2,128,128]{3,2,1,0:T(8,128)S(1)}, f32[2,2,128,128]{3,2,1,0:T(8,128)S(1)}, u32[]{:S(2)}, u32[]{:S(2)}) collective-permute-start(f32[2,2,128,128]{3,2,1,0:T(8,128)S(1)} %get-tuple-element.27.refs_4_.refs_5_), channel_id=1, source_target_pairs={{0,2},{1,3},{2,0},{3,1},{4,6},{5,7},{6,4},{7,5},{8,10},{9,11},{10,... | collective-permute-start | bytes 786440 | tf_op jit(solution)/shard_map/ppermute | solution.py:351
  45.9 16.9 %collective-permute-done.5.refs_3_.refs_4_ = bf16[1024,256]{1,0:T(8,128)(2,1)S(1)} collective-permute-done((bf16[1024,256]{1,0:T(8,128)(2,1)S(1)}, bf16[1024,256]{1,0:T(8,128)(2,1)S(1)}, u32[]{:S(2)}, u32[]{:S(2)}) %collective-permute-start.5) | collective-permute-done | bytes 524320 | tf_op jit(solution)/shard_map/ppermute | solution.py:281
  62.9 2.6 %step.8 = (f32[2,2,128,128]{3,2,1,0:T(8,128)S(1)}, bf16[1024,256]{1,0:T(8,128)(2,1)S(1)}) custom-call(s32[2,9]{1,0:T(2,128)S(1)} %get-tuple-element.24.refs_0_, f32[1,9]{1,0:T(1,128)S(1)} %get-tuple-element.25.refs_1_, bf16[1024,2048]{1,0:T(8,128)(2,1)} %refs_2_.11, bf16[1024,256]{1,0:T(8,128)(2,1)S(1)} %collective-permute-done.5.refs_3_.refs_4_, ...), custom_call_target="tpu_custom_call" | custom-call | tf_op jit(solution)/shard_map/step/pallas_call | solution.py:328
  65.7 2.7 %collective-permute-start.12 = (f32[2,2,128,128]{3,2,1,0:T(8,128)S(1)}, f32[2,2,128,128]{3,2,1,0:T(8,128)S(1)}, u32[]{:S(2)}, u32[]{:S(2)}) collective-permute-start(f32[2,2,128,128]{3,2,1,0:T(8,128)S(1)} %get-tuple-element.29.refs_9_.refs_5_), channel_id=1, source_target_pairs={{0,2},{1,3},{2,0},{3,1},{4,6},{5,7},{6,4},{7,5},{8,10},{9,11},{10,... | collective-permute-start | bytes 786440 | tf_op jit(solution)/shard_map/ppermute | solution.py:351
  68.4 0.1 collective-permute-start.13
  68.5 16.8 %collective-permute-done.1.refs_3_ = bf16[1024,256]{1,0:T(8,128)(2,1)S(1)} collective-permute-done((bf16[1024,256]{1,0:T(8,128)(2,1)S(1)}, bf16[1024,256]{1,0:T(8,128)(2,1)S(1)}, u32[]{:S(2)}, u32[]{:S(2)}) %collective-permute-start.1) | collective-permute-done | bytes 524320 | tf_op jit(solution)/shard_map/ppermute | solution.py:354
  85.3 4.5 %step.9 = (f32[2,2,128,128]{3,2,1,0:T(8,128)S(1)}, bf16[1024,256]{1,0:T(8,128)(2,1)S(1)}, bf16[1024,2048]{1,0:T(8,128)(2,1)}) custom-call(s32[2,9]{1,0:T(2,128)S(1)} %get-tuple-element.24.refs_0_, f32[1,9]{1,0:T(1,128)S(1)} %get-tuple-element.25.refs_1_, bf16[1024,2048]{1,0:T(8,128)(2,1)} %refs_2_.11, bf16[1024,256]{1,0:T(8,128)(2,1)S(1)} %collective-permute-done.1.refs_3_, ...), custom_call_target="tpu_custom_call" | custom-call | tf_op jit(solution)/shard_map/step/pallas_call | solution.py:328
  90.0 2.7 %collective-permute-start.7 = (f32[2,2,128,128]{3,2,1,0:T(8,128)S(1)}, f32[2,2,128,128]{3,2,1,0:T(8,128)S(1)}, u32[]{:S(2)}, u32[]{:S(2)}) collective-permute-start(f32[2,2,128,128]{3,2,1,0:T(8,128)S(1)} %get-tuple-element.30.refs_4_), channel_id=1, source_target_pairs={{0,2},{1,3},{2,0},{3,1},{4,6},{5,7},{6,4},{7,5},{8,10},{9,11},{10,... | collective-permute-start | bytes 786440 | tf_op jit(solution)/shard_map/ppermute | solution.py:351
  92.7 0.1 collective-permute-start.8
  92.8 15.0 %collective-permute-done.10.refs_3_ = bf16[1024,256]{1,0:T(8,128)(2,1)S(1)} collective-permute-done((bf16[1024,256]{1,0:T(8,128)(2,1)S(1)}, bf16[1024,256]{1,0:T(8,128)(2,1)S(1)}, u32[]{:S(2)}, u32[]{:S(2)}) %collective-permute-start.10) | collective-permute-done | bytes 524320 | tf_op jit(solution)/shard_map/ppermute | solution.py:354
  107.8 4.5 %step.10 = (f32[2,2,128,128]{3,2,1,0:T(8,128)S(1)}, bf16[1024,256]{1,0:T(8,128)(2,1)S(1)}, bf16[1024,2048]{1,0:T(8,128)(2,1)}) custom-call(s32[2,9]{1,0:T(2,128)S(1)} %get-tuple-element.24.refs_0_, f32[1,9]{1,0:T(1,128)S(1)} %get-tuple-element.25.refs_1_, bf16[1024,2048]{1,0:T(8,128)(2,1)} %refs_2_.11, ...), custom_call_target="tpu_custom_call", output_to_operand_aliasing={{2}: (9, {})} | custom-call | tf_op jit(solution)/shard_map/step/pallas_call | solution.py:328
  112.5 2.7 %collective-permute-start.16 = (f32[2,2,128,128]{3,2,1,0:T(8,128)S(1)}, f32[2,2,128,128]{3,2,1,0:T(8,128)S(1)}, u32[]{:S(2)}, u32[]{:S(2)}) collective-permute-start(f32[2,2,128,128]{3,2,1,0:T(8,128)S(1)} %get-tuple-element.36.refs_4_), channel_id=1, source_target_pairs={{0,2},{1,3},{2,0},{3,1},{4,6},{5,7},{6,4},{7,5},{8,10},{9,11},{10,... | collective-permute-start | bytes 786440 | tf_op jit(solution)/shard_map/ppermute | solution.py:351
  115.3 15.0 %collective-permute-done.9.refs_8_ = bf16[1024,256]{1,0:T(8,128)(2,1)S(1)} collective-permute-done((bf16[1024,256]{1,0:T(8,128)(2,1)S(1)}, bf16[1024,256]{1,0:T(8,128)(2,1)S(1)}, u32[]{:S(2)}, u32[]{:S(2)}) %collective-permute-start.9) | collective-permute-done | bytes 524320 | tf_op jit(solution)/shard_map/ppermute | solution.py:354
  130.3 3.6 %step.11 = (bf16[1024,256]{1,0:T(8,128)(2,1)S(1)}, bf16[1024,2048]{1,0:T(8,128)(2,1)}) custom-call(s32[2,9]{1,0:T(2,128)S(1)} %get-tuple-element.24.refs_0_, f32[1,9]{1,0:T(1,128)S(1)} %get-tuple-element.25.refs_1_, bf16[1024,2048]{1,0:T(8,128)(2,1)} %refs_2_.11, ...), custom_call_target="tpu_custom_call", output_to_operand_aliasing={{1}: (9, {})} | custom-call | tf_op jit(solution)/shard_map/step/pallas_call | solution.py:328
  134.0 18.7 %collective-permute-done.18.refs_8_ = bf16[1024,256]{1,0:T(8,128)(2,1)S(1)} collective-permute-done((bf16[1024,256]{1,0:T(8,128)(2,1)S(1)}, bf16[1024,256]{1,0:T(8,128)(2,1)S(1)}, u32[]{:S(2)}, u32[]{:S(2)}) %collective-permute-start.18) | collective-permute-done | bytes 524320 | tf_op jit(solution)/shard_map/ppermute | solution.py:354
  152.7 3.6 %step.12 = (bf16[1024,128]{1,0:T(8,128)(2,1)S(1)}, bf16[512,128]{1,0:T(8,128)(2,1)S(1)}, bf16[512,128]{1,0:T(8,128)(2,1)S(1)}, bf16[1024,2048]{1,0:T(8,128)(2,1)}) custom-call(s32[2,9]{1,0:T(2,128)S(1)} %get-tuple-element.24.refs_0_, f32[1,9]{1,0:T(1,128)S(1)} %get-tuple-element.25.refs_1_, ...), custom_call_target="tpu_custom_call", output_to_operand_aliasing={{3}: (9, {})} | custom-call | tf_op jit(solution)/shard_map/step/pallas_call | solution.py:328
  156.4 2.9 %collective-permute-start.20 = (bf16[512,128]{1,0:T(8,128)(2,1)S(1)}, bf16[512,128]{1,0:T(8,128)(2,1)S(1)}, u32[]{:S(2)}, u32[]{:S(2)}) collective-permute-start(bf16[512,128]{1,0:T(8,128)(2,1)S(1)} %get-tuple-element.41), channel_id=1, source_target_pairs={{0,8},{4,12},{8,0},{12,4},{1,9},{5,13},{9,1},{13,5},{2,10},{6,14},... | collective-permute-start | bytes 393224 | tf_op jit(solution)/shard_map/ppermute | solution.py:354
  159.3 0.7 fusion
  161.3 0.1 collective-permute-start.21
  161.5 13.7 %collective-permute-done.14.refs_1_ = bf16[1024,256]{1,0:T(8,128)(2,1)S(1)} collective-permute-done((bf16[1024,256]{1,0:T(8,128)(2,1)S(1)}, bf16[1024,256]{1,0:T(8,128)(2,1)S(1)}, u32[]{:S(2)}, u32[]{:S(2)}) %collective-permute-start.14) | collective-permute-done | bytes 524320 | tf_op jit(solution)/shard_map/ppermute | solution.py:354
  175.2 1.4 step.13
  176.6 4.2 %collective-permute-done.19 = bf16[1024,128]{1,0:T(8,128)(2,1)S(1)} collective-permute-done((bf16[1024,128]{1,0:T(8,128)(2,1)S(1)}, bf16[1024,128]{1,0:T(8,128)(2,1)S(1)}, u32[]{:S(2)}, u32[]{:S(2)}) %collective-permute-start.19) | collective-permute-done | bytes 262176 | tf_op jit(solution)/shard_map/ppermute | solution.py:354
  180.8 0.7 constant_dynamic-update-slice_fusion.2
  181.6 2.1 %collective-permute-done.20 = bf16[512,128]{1,0:T(8,128)(2,1)S(1)} collective-permute-done((bf16[512,128]{1,0:T(8,128)(2,1)S(1)}, bf16[512,128]{1,0:T(8,128)(2,1)S(1)}, u32[]{:S(2)}, u32[]{:S(2)}) %collective-permute-start.20) | collective-permute-done | bytes 131104 | tf_op jit(solution)/shard_map/ppermute | solution.py:354
  183.6 0.7 constant_dynamic-update-slice_fusion.1
  184.3 1.3 collective-permute-done.21
  185.6 0.7 constant_dynamic-update-slice_fusion
  (25 shorter events, 1.0 us)
Async XLA Ops:
  1.8 38.5 %collective-permute-start = (bf16[1024,256]{1,0:T(8,128)(2,1)S(1)}, bf16[1024,256]{1,0:T(8,128)(2,1)S(1)}, u32[]{:S(2)}, u32[]{:S(2)}) collective-permute-start(bf16[1024,256]{1,0:T(8,128)(2,1)S(1)} %opening.1.first_ref), channel_id=1, source_target_pairs={{0,8},{4,12},{8,0},{12,4},{1,9},{5,13},{9,1},{13,5},{2,10},{6,14},... | collective-permute-start | bytes 1572872 | tf_op jit(solution)/shard_map/ppermute | solution.py:281
  8.5 54.4 %collective-permute-start.5 = (bf16[1024,256]{1,0:T(8,128)(2,1)S(1)}, bf16[1024,256]{1,0:T(8,128)(2,1)S(1)}, u32[]{:S(2)}, u32[]{:S(2)}) collective-permute-start(bf16[1024,256]{1,0:T(8,128)(2,1)S(1)} %get-tuple-element.28), channel_id=1, source_target_pairs={{0,8},{4,12},{8,0},{12,4},{1,9},{5,13},{9,1},{13,5},{2,10},{6,14},... | collective-permute-start | bytes 1572872 | tf_op jit(solution)/shard_map/ppermute | solution.py:281
  43.0 42.3 %collective-permute-start.1 = (bf16[1024,256]{1,0:T(8,128)(2,1)S(1)}, bf16[1024,256]{1,0:T(8,128)(2,1)S(1)}, u32[]{:S(2)}, u32[]{:S(2)}) collective-permute-start(bf16[1024,256]{1,0:T(8,128)(2,1)S(1)} %get-tuple-element.26), channel_id=1, source_target_pairs={{0,8},{4,12},{8,0},{12,4},{1,9},{5,13},{9,1},{13,5},{2,10},{6,14},... | collective-permute-start | bytes 1572872 | tf_op jit(solution)/shard_map/ppermute | solution.py:354
  43.1 22.5 %collective-permute-start.2 = (f32[2,2,128,128]{3,2,1,0:T(8,128)S(1)}, f32[2,2,128,128]{3,2,1,0:T(8,128)S(1)}, u32[]{:S(2)}, u32[]{:S(2)}) collective-permute-start(f32[2,2,128,128]{3,2,1,0:T(8,128)S(1)} %get-tuple-element.27.refs_4_.refs_5_), channel_id=1, source_target_pairs={{0,1},{1,0},{2,3},{3,2},{4,5},{5,4},{6,7},{7,6},{8,9},{9,8},{10,11... | collective-permute-start | bytes 786440 | tf_op jit(solution)/shard_map/ppermute | solution.py:351
  43.2 22.5 %collective-permute-start.3 = (f32[2,2,128,128]{3,2,1,0:T(8,128)S(1)}, f32[2,2,128,128]{3,2,1,0:T(8,128)S(1)}, u32[]{:S(2)}, u32[]{:S(2)}) collective-permute-start(f32[2,2,128,128]{3,2,1,0:T(8,128)S(1)} %get-tuple-element.27.refs_4_.refs_5_), channel_id=1, source_target_pairs={{0,2},{1,3},{2,0},{3,1},{4,6},{5,7},{6,4},{7,5},{8,10},{9,11},{10,... | collective-permute-start | bytes 786440 | tf_op jit(solution)/shard_map/ppermute | solution.py:351
  45.9 22.5 %collective-permute-start.4 = (f32[2,2,128,128]{3,2,1,0:T(8,128)S(1)}, f32[2,2,128,128]{3,2,1,0:T(8,128)S(1)}, u32[]{:S(2)}, u32[]{:S(2)}) collective-permute-start(f32[2,2,128,128]{3,2,1,0:T(8,128)S(1)} %get-tuple-element.27.refs_4_.refs_5_), channel_id=1, source_target_pairs={{0,3},{1,2},{2,1},{3,0},{4,7},{5,6},{6,5},{7,4},{8,11},{9,10},{10,... | collective-permute-start | bytes 786440 | tf_op jit(solution)/shard_map/ppermute | solution.py:351
  65.5 42.3 %collective-permute-start.10 = (bf16[1024,256]{1,0:T(8,128)(2,1)S(1)}, bf16[1024,256]{1,0:T(8,128)(2,1)S(1)}, u32[]{:S(2)}, u32[]{:S(2)}) collective-permute-start(bf16[1024,256]{1,0:T(8,128)(2,1)S(1)} %get-tuple-element.32), channel_id=1, source_target_pairs={{0,8},{4,12},{8,0},{12,4},{1,9},{5,13},{9,1},{13,5},{2,10},{6,14},... | collective-permute-start | bytes 1572872 | tf_op jit(solution)/shard_map/ppermute | solution.py:354
  65.6 24.3 %collective-permute-start.11 = (f32[2,2,128,128]{3,2,1,0:T(8,128)S(1)}, f32[2,2,128,128]{3,2,1,0:T(8,128)S(1)}, u32[]{:S(2)}, u32[]{:S(2)}) collective-permute-start(f32[2,2,128,128]{3,2,1,0:T(8,128)S(1)} %get-tuple-element.29.refs_9_.refs_5_), channel_id=1, source_target_pairs={{0,1},{1,0},{2,3},{3,2},{4,5},{5,4},{6,7},{7,6},{8,9},{9,8},{10,11... | collective-permute-start | bytes 786440 | tf_op jit(solution)/shard_map/ppermute | solution.py:351
  65.7 24.3 %collective-permute-start.12 = (f32[2,2,128,128]{3,2,1,0:T(8,128)S(1)}, f32[2,2,128,128]{3,2,1,0:T(8,128)S(1)}, u32[]{:S(2)}, u32[]{:S(2)}) collective-permute-start(f32[2,2,128,128]{3,2,1,0:T(8,128)S(1)} %get-tuple-element.29.refs_9_.refs_5_), channel_id=1, source_target_pairs={{0,2},{1,3},{2,0},{3,1},{4,6},{5,7},{6,4},{7,5},{8,10},{9,11},{10,... | collective-permute-start | bytes 786440 | tf_op jit(solution)/shard_map/ppermute | solution.py:351
  68.4 24.4 %collective-permute-start.13 = (f32[2,2,128,128]{3,2,1,0:T(8,128)S(1)}, f32[2,2,128,128]{3,2,1,0:T(8,128)S(1)}, u32[]{:S(2)}, u32[]{:S(2)}) collective-permute-start(f32[2,2,128,128]{3,2,1,0:T(8,128)S(1)} %get-tuple-element.29.refs_9_.refs_5_), channel_id=1, source_target_pairs={{0,3},{1,2},{2,1},{3,0},{4,7},{5,6},{6,5},{7,4},{8,11},{9,10},{10,... | collective-permute-start | bytes 786440 | tf_op jit(solution)/shard_map/ppermute | solution.py:351
  89.8 40.4 %collective-permute-start.9 = (bf16[1024,256]{1,0:T(8,128)(2,1)S(1)}, bf16[1024,256]{1,0:T(8,128)(2,1)S(1)}, u32[]{:S(2)}, u32[]{:S(2)}) collective-permute-start(bf16[1024,256]{1,0:T(8,128)(2,1)S(1)} %get-tuple-element.31), channel_id=1, source_target_pairs={{0,8},{4,12},{8,0},{12,4},{1,9},{5,13},{9,1},{13,5},{2,10},{6,14},... | collective-permute-start | bytes 1572872 | tf_op jit(solution)/shard_map/ppermute | solution.py:354
  89.9 22.5 %collective-permute-start.6 = (f32[2,2,128,128]{3,2,1,0:T(8,128)S(1)}, f32[2,2,128,128]{3,2,1,0:T(8,128)S(1)}, u32[]{:S(2)}, u32[]{:S(2)}) collective-permute-start(f32[2,2,128,128]{3,2,1,0:T(8,128)S(1)} %get-tuple-element.30.refs_4_), channel_id=1, source_target_pairs={{0,1},{1,0},{2,3},{3,2},{4,5},{5,4},{6,7},{7,6},{8,9},{9,8},{10,11... | collective-permute-start | bytes 786440 | tf_op jit(solution)/shard_map/ppermute | solution.py:351
  90.0 22.5 %collective-permute-start.7 = (f32[2,2,128,128]{3,2,1,0:T(8,128)S(1)}, f32[2,2,128,128]{3,2,1,0:T(8,128)S(1)}, u32[]{:S(2)}, u32[]{:S(2)}) collective-permute-start(f32[2,2,128,128]{3,2,1,0:T(8,128)S(1)} %get-tuple-element.30.refs_4_), channel_id=1, source_target_pairs={{0,2},{1,3},{2,0},{3,1},{4,6},{5,7},{6,4},{7,5},{8,10},{9,11},{10,... | collective-permute-start | bytes 786440 | tf_op jit(solution)/shard_map/ppermute | solution.py:351
  92.7 22.5 %collective-permute-start.8 = (f32[2,2,128,128]{3,2,1,0:T(8,128)S(1)}, f32[2,2,128,128]{3,2,1,0:T(8,128)S(1)}, u32[]{:S(2)}, u32[]{:S(2)}) collective-permute-start(f32[2,2,128,128]{3,2,1,0:T(8,128)S(1)} %get-tuple-element.30.refs_4_), channel_id=1, source_target_pairs={{0,3},{1,2},{2,1},{3,0},{4,7},{5,6},{6,5},{7,4},{8,11},{9,10},{10,... | collective-permute-start | bytes 786440 | tf_op jit(solution)/shard_map/ppermute | solution.py:351
  112.3 40.4 %collective-permute-start.18 = (bf16[1024,256]{1,0:T(8,128)(2,1)S(1)}, bf16[1024,256]{1,0:T(8,128)(2,1)S(1)}, u32[]{:S(2)}, u32[]{:S(2)}) collective-permute-start(bf16[1024,256]{1,0:T(8,128)(2,1)S(1)} %get-tuple-element.37), channel_id=1, source_target_pairs={{0,8},{4,12},{8,0},{12,4},{1,9},{5,13},{9,1},{13,5},{2,10},{6,14},... | collective-permute-start | bytes 1572872 | tf_op jit(solution)/shard_map/ppermute | solution.py:354
  112.4 21.6 %collective-permute-start.15 = (f32[2,2,128,128]{3,2,1,0:T(8,128)S(1)}, f32[2,2,128,128]{3,2,1,0:T(8,128)S(1)}, u32[]{:S(2)}, u32[]{:S(2)}) collective-permute-start(f32[2,2,128,128]{3,2,1,0:T(8,128)S(1)} %get-tuple-element.36.refs_4_), channel_id=1, source_target_pairs={{0,1},{1,0},{2,3},{3,2},{4,5},{5,4},{6,7},{7,6},{8,9},{9,8},{10,11... | collective-permute-start | bytes 786440 | tf_op jit(solution)/shard_map/ppermute | solution.py:351
  112.5 21.5 %collective-permute-start.16 = (f32[2,2,128,128]{3,2,1,0:T(8,128)S(1)}, f32[2,2,128,128]{3,2,1,0:T(8,128)S(1)}, u32[]{:S(2)}, u32[]{:S(2)}) collective-permute-start(f32[2,2,128,128]{3,2,1,0:T(8,128)S(1)} %get-tuple-element.36.refs_4_), channel_id=1, source_target_pairs={{0,2},{1,3},{2,0},{3,1},{4,6},{5,7},{6,4},{7,5},{8,10},{9,11},{10,... | collective-permute-start | bytes 786440 | tf_op jit(solution)/shard_map/ppermute | solution.py:351
  115.2 18.8 %collective-permute-start.17 = (f32[2,2,128,128]{3,2,1,0:T(8,128)S(1)}, f32[2,2,128,128]{3,2,1,0:T(8,128)S(1)}, u32[]{:S(2)}, u32[]{:S(2)}) collective-permute-start(f32[2,2,128,128]{3,2,1,0:T(8,128)S(1)} %get-tuple-element.36.refs_4_), channel_id=1, source_target_pairs={{0,3},{1,2},{2,1},{3,0},{4,7},{5,6},{6,5},{7,4},{8,11},{9,10},{10,... | collective-permute-start | bytes 786440 | tf_op jit(solution)/shard_map/ppermute | solution.py:351
  133.9 41.3 %collective-permute-start.14 = (bf16[1024,256]{1,0:T(8,128)(2,1)S(1)}, bf16[1024,256]{1,0:T(8,128)(2,1)S(1)}, u32[]{:S(2)}, u32[]{:S(2)}) collective-permute-start(bf16[1024,256]{1,0:T(8,128)(2,1)S(1)} %get-tuple-element.35), channel_id=1, source_target_pairs={{0,8},{4,12},{8,0},{12,4},{1,9},{5,13},{9,1},{13,5},{2,10},{6,14},... | collective-permute-start | bytes 1572872 | tf_op jit(solution)/shard_map/ppermute | solution.py:354
  156.3 24.5 %collective-permute-start.19 = (bf16[1024,128]{1,0:T(8,128)(2,1)S(1)}, bf16[1024,128]{1,0:T(8,128)(2,1)S(1)}, u32[]{:S(2)}, u32[]{:S(2)}) collective-permute-start(bf16[1024,128]{1,0:T(8,128)(2,1)S(1)} %get-tuple-element.40), channel_id=1, source_target_pairs={{0,8},{4,12},{8,0},{12,4},{1,9},{5,13},{9,1},{13,5},{2,10},{6,14},... | collective-permute-start | bytes 786440 | tf_op jit(solution)/shard_map/ppermute | solution.py:354
  156.4 27.2 %collective-permute-start.20 = (bf16[512,128]{1,0:T(8,128)(2,1)S(1)}, bf16[512,128]{1,0:T(8,128)(2,1)S(1)}, u32[]{:S(2)}, u32[]{:S(2)}) collective-permute-start(bf16[512,128]{1,0:T(8,128)(2,1)S(1)} %get-tuple-element.41), channel_id=1, source_target_pairs={{0,8},{4,12},{8,0},{12,4},{1,9},{5,13},{9,1},{13,5},{2,10},{6,14},... | collective-permute-start | bytes 393224 | tf_op jit(solution)/shard_map/ppermute | solution.py:354
  161.3 24.3 %collective-permute-start.21 = (bf16[512,128]{1,0:T(8,128)(2,1)S(1)}, bf16[512,128]{1,0:T(8,128)(2,1)S(1)}, u32[]{:S(2)}, u32[]{:S(2)}) collective-permute-start(bf16[512,128]{1,0:T(8,128)(2,1)S(1)} %get-tuple-element.42), channel_id=1, source_target_pairs={{0,8},{4,12},{8,0},{12,4},{1,9},{5,13},{9,1},{13,5},{2,10},{6,14},... | collective-permute-start | bytes 393224 | tf_op jit(solution)/shard_map/ppermute | solution.py:354
